TPU v7x, 32 devices: a whole 2x2x4 slice. The times are simulated.
32 devices in a mesh: slab: 2 (over y), dom: 4 (over z), coil: 4 (over x, core).
Axes of the slice: x: 2, y: 2, z: 4, core: 2. Of those that a mesh axis runs over, the one named last changes fastest.
Arguments:
- basis_image: bfloat16 [2, 5, 16, 128, 128], P(None, None, 'slab', 'dom'), parts along dimension 2, may hold values from -6 to 6
- coil_maps: bfloat16 [2, 48, 16, 128, 128], P(None, 'coil', 'slab', 'dom'), parts along dimension 2, may hold values from -1.5 to 1.5
- point_spread: float32 [32, 2, 256, 256], P(None, None, 'dom'), may hold values from -6 to 6
- basis_products: float32 [32, 2, 5, 5], replicated, may hold values from -0.625 to 0.625
- sampled: int32 [32, 8], replicated, may hold values 0 or 1
- adjoint_data: float32 [2, 5, 16, 128, 128], P(None, None, ('slab', 'coil'), 'dom'), parts along dimension 2, may hold values from -2 to 2
Outputs:
- gradient: float32 [2, 5, 16, 128, 128], P(None, None, ('slab', 'coil'), 'dom'), parts along dimension 2
There are 2 independent parts, one for each index of `slab`. A program takes and returns all parts, laid end to end along the dimension named above; an argument that names none is the same for every part. Nothing has to cross between parts.
All inputs are finite; a program needn't handle non-finite values.
Results may differ from a plain program's by a relative error of at most 0.01.
Values may be sent and summed in bfloat16 or wider, within the bound.
No kernel may reach another device: no remote copies, remote signals or barrier semaphores. Data moves between devices by JAX's collectives and lax.ppermute only.
A program may use at most 128 MiB of HBM per device.

v0:
```python
import math

import jax
import jax.numpy as jnp
from jax import lax
from jax.sharding import PartitionSpec as P

K = 5
NZ = 8
NX = 128
NY = 128


def dft_table(count_in, count_out, length, sign):
    first = jnp.arange(count_in, dtype=jnp.int32)
    second = jnp.arange(count_out, dtype=jnp.int32)
    phase = (first[:, None] * second[None, :] % length).astype(jnp.float32) * (
        2.0 * math.pi / length
    )
    scale = 1.0 / math.sqrt(length)
    cosine = jnp.cos(phase) * scale
    sine = jnp.sin(phase) * (sign * scale)
    table = jnp.stack([jnp.stack([cosine, -sine]), jnp.stack([sine, cosine])])
    return table.astype(jnp.bfloat16)


def build_kernel(sampled, basis_products, point_spread):
    weights = basis_products[:, :, :, :, None] * sampled.astype(jnp.float32)[:, None, None, None, :]
    high = lax.Precision.HIGHEST
    kernel_real = jnp.einsum(
        "gkjq,gvu->kjqvu", weights[:, 0], point_spread[:, 0], precision=high
    ) - jnp.einsum("gkjq,gvu->kjqvu", weights[:, 1], point_spread[:, 1], precision=high)
    kernel_imag = jnp.einsum(
        "gkjq,gvu->kjqvu", weights[:, 0], point_spread[:, 1], precision=high
    ) + jnp.einsum("gkjq,gvu->kjqvu", weights[:, 1], point_spread[:, 0], precision=high)
    return (kernel_real, kernel_imag)


def apply_kernel(kernel_real, kernel_imag, spectrum):
    real_acc = jnp.zeros(spectrum.shape[1:], jnp.float32)
    imag_acc = jnp.zeros(spectrum.shape[1:], jnp.float32)
    for column in range(spectrum.shape[2]):
        real_in = spectrum[0][:, column][:, None]
        imag_in = spectrum[1][:, column][:, None]
        real_acc = (
            real_acc
            + kernel_real[:, column][None] * real_in
            - kernel_imag[:, column][None] * imag_in
        )
        imag_acc = (
            imag_acc
            + kernel_real[:, column][None] * imag_in
            + kernel_imag[:, column][None] * real_in
        )
    return jnp.stack([real_acc, imag_acc])


def transform(table, data, form):
    return jnp.einsum(form, table, data, preferred_element_type=jnp.float32)


def route_grid(rows, spectral):
    return lax.all_to_all(
        spectral(lax.all_to_all(rows, "dom", split_axis=5, concat_axis=4, tiled=True)),
        "dom",
        split_axis=5,
        concat_axis=4,
        tiled=True,
    )


def accumulate(maps_part, image_part, spread_part, basis_products, sampled, per_turn, route):
    forward_z = dft_table(NZ, NZ, NZ, -1)
    forward_y = dft_table(NY, 2 * NY, 2 * NY, -1)
    forward_x = dft_table(NX, 2 * NX, 2 * NX, -1)
    inverse_x = dft_table(2 * NX, NX, 2 * NX, 1)
    inverse_y = dft_table(2 * NY, NY, 2 * NY, 1)
    inverse_z = dft_table(NZ, NZ, NZ, 1)
    kernel_real, kernel_imag = build_kernel(sampled, basis_products, spread_part)
    image_f = image_part.astype(jnp.float32)

    def spectral(rows):
        spectrum = transform(forward_x, rows, "oixu,ibkqxw->obkqwu")
        weighted = apply_kernel(kernel_real, kernel_imag, spectrum).astype(jnp.bfloat16)
        return transform(inverse_x, weighted, "oiux,ibkqwu->obkqwx").astype(jnp.bfloat16)

    def one_turn(index, total):
        maps_now = lax.dynamic_slice_in_dim(maps_part, index * per_turn, per_turn, 1).astype(
            jnp.float32
        )
        coil_real = (
            maps_now[0][:, None] * image_f[0][None] - maps_now[1][:, None] * image_f[1][None]
        )
        coil_imag = (
            maps_now[0][:, None] * image_f[1][None] + maps_now[1][:, None] * image_f[0][None]
        )
        coil_image = jnp.stack([coil_real, coil_imag]).astype(jnp.bfloat16)
        partition = transform(forward_z, coil_image, "oizq,ibkzry->obkqry").astype(jnp.bfloat16)
        rows = transform(forward_y, partition, "oiyw,ibkqry->obkqrw").astype(jnp.bfloat16)
        columns = route(rows, spectral)
        back_rows = transform(inverse_y, columns, "oiwy,ibkqwr->obkqry").astype(jnp.bfloat16)
        coil_back = transform(inverse_z, back_rows, "oiqz,ibkqry->obkzry")
        grad_real = jnp.sum(
            maps_now[0][:, None] * coil_back[0] + maps_now[1][:, None] * coil_back[1], axis=0
        )
        grad_imag = jnp.sum(
            maps_now[0][:, None] * coil_back[1] - maps_now[1][:, None] * coil_back[0], axis=0
        )
        return total + jnp.stack([grad_real, grad_imag])

    turns = maps_part.shape[1] // per_turn
    zeros = jnp.zeros((2, K, NZ, image_part.shape[3], NY), jnp.float32)
    return lax.fori_loop(0, turns, one_turn, zeros)


def body(basis_image, coil_maps, point_spread, basis_products, sampled, adjoint_data):
    partial_sum = accumulate(
        coil_maps, basis_image, point_spread, basis_products, sampled, 1, route_grid
    )
    combined = lax.psum_scatter(
        partial_sum.astype(jnp.bfloat16), "coil", scatter_dimension=2, tiled=True
    ).astype(jnp.float32)
    return combined - adjoint_data


def solution(mesh):
    placed = (
        P(None, None, "slab", "dom", None),
        P(None, "coil", "slab", "dom", None),
        P(None, None, "dom", None),
        P(),
        P(),
        P(None, None, ("slab", "coil"), "dom", None),
    )
    return jax.shard_map(
        body,
        mesh=mesh,
        in_specs=placed,
        out_specs=P(None, None, ("slab", "coil"), "dom", None),
        check_vma=False,
    )
```

profile of v0, /device:TPU:0, one launch (start us, length us, event | category | flops | bytes accessed | tf_op | source)
XLA Modules:
  0.0 1890.2 jit_solution(7298154365591024769)
XLA Ops:
  13.3 10.8 fusion.51
  24.0 13.3 fusion.50
  37.4 23.3 %convolution_add_fusion = f32[5,5,8,64,256]{4,2,3,1,0:T(8,128)} fusion(f32[5,5,8,64,256]{4,2,3,1,0:T(8,128)S(1)} %fusion.51, f32[32,1,64,256]{3,2,1,0:T(8,128)S(1)} %get-tuple-element.315, f32[32,2,5,5,8]{0,4,3,2,1:T(8,128)S(1)} %broadcast_multiply_fusion), kind=kOutput, calls=%fused_computation.100 | convolution fusion | flops 1261568000 | bytes 28413952 | tf_op jit(solution)/shard_map/gkjq,gvu->kjqvu/dot_general | solution.py:35
  60.7 14.4 copy.73
  75.2 15.9 convolution_subtract_fusion
  91.1 14.5 copy.71
  106.0 1739.5 %while.15 = (s32[]{:T(128)}, f32[2,5,8,32,128]{4,2,0,3,1:T(8,128)}, bf16[2,12,8,32,128]{4,3,2,1,0:T(8,128)(2,1)}, f32[5,5,8,64,256]{4,3,2,0,1:T(8,128)}, f32[2,5...) while((s32[]{:T(128)}, f32[2,5,8,32,128]{4,2,0,3,1:T(8,128)}, ...), condition=%wide.region_1.2_spmd.clone, body=%wide.region_0.1_spmd.clone.sunk | while | flops 2072313856 | bytes 208536944 | solution.py:113
  123.3 37.5 %all_to_all.66 = bf16[4,2,81920]{2,1,0:T(2,128)(2,1)S(1)} all-to-all(bf16[4,2,81920]{2,1,0:T(2,128)(2,1)S(1)} %reshape.983), channel_id=1, replica_groups=mesh['slab'=2,'dom'=4,'coil'=4] {'dom'}, dimensions={0} | all-to-all | bytes 2621440 | tf_op jit(solution)/shard_map/while/body/eval_jaxpr/all_to_all | solution.py:64
  211.9 30.5 %all-to-all-done.1 = bf16[4,2,81920]{2,1,0:T(2,128)(2,1)} async-done(((bf16[4,2,81920]{2,1,0:T(2,128)(2,1)}), bf16[4,2,81920]{2,1,0:T(2,128)(2,1)}, u32[]{:S(2)}, u32[]{:S(2)}) %all-to-all-start.1) | async-done | bytes 1310752 | tf_op jit(solution)/shard_map/while/body/eval_jaxpr/all_to_all | solution.py:63
  272.1 33.3 %all_to_all.66 = bf16[4,2,81920]{2,1,0:T(2,128)(2,1)S(1)} all-to-all(bf16[4,2,81920]{2,1,0:T(2,128)(2,1)S(1)} %reshape.983), channel_id=1, replica_groups=mesh['slab'=2,'dom'=4,'coil'=4] {'dom'}, dimensions={0} | all-to-all | bytes 2621440 | tf_op jit(solution)/shard_map/while/body/eval_jaxpr/all_to_all | solution.py:64
  356.5 30.5 %all-to-all-done.1 = bf16[4,2,81920]{2,1,0:T(2,128)(2,1)} async-done(((bf16[4,2,81920]{2,1,0:T(2,128)(2,1)}), bf16[4,2,81920]{2,1,0:T(2,128)(2,1)}, u32[]{:S(2)}, u32[]{:S(2)}) %all-to-all-start.1) | async-done | bytes 1310752 | tf_op jit(solution)/shard_map/while/body/eval_jaxpr/all_to_all | solution.py:63
  416.6 33.3 %all_to_all.66 = bf16[4,2,81920]{2,1,0:T(2,128)(2,1)S(1)} all-to-all(bf16[4,2,81920]{2,1,0:T(2,128)(2,1)S(1)} %reshape.983), channel_id=1, replica_groups=mesh['slab'=2,'dom'=4,'coil'=4] {'dom'}, dimensions={0} | all-to-all | bytes 2621440 | tf_op jit(solution)/shard_map/while/body/eval_jaxpr/all_to_all | solution.py:64
  501.1 30.5 %all-to-all-done.1 = bf16[4,2,81920]{2,1,0:T(2,128)(2,1)} async-done(((bf16[4,2,81920]{2,1,0:T(2,128)(2,1)}), bf16[4,2,81920]{2,1,0:T(2,128)(2,1)}, u32[]{:S(2)}, u32[]{:S(2)}) %all-to-all-start.1) | async-done | bytes 1310752 | tf_op jit(solution)/shard_map/while/body/eval_jaxpr/all_to_all | solution.py:63
  561.2 33.3 %all_to_all.66 = bf16[4,2,81920]{2,1,0:T(2,128)(2,1)S(1)} all-to-all(bf16[4,2,81920]{2,1,0:T(2,128)(2,1)S(1)} %reshape.983), channel_id=1, replica_groups=mesh['slab'=2,'dom'=4,'coil'=4] {'dom'}, dimensions={0} | all-to-all | bytes 2621440 | tf_op jit(solution)/shard_map/while/body/eval_jaxpr/all_to_all | solution.py:64
  645.7 30.5 %all-to-all-done.1 = bf16[4,2,81920]{2,1,0:T(2,128)(2,1)} async-done(((bf16[4,2,81920]{2,1,0:T(2,128)(2,1)}), bf16[4,2,81920]{2,1,0:T(2,128)(2,1)}, u32[]{:S(2)}, u32[]{:S(2)}) %all-to-all-start.1) | async-done | bytes 1310752 | tf_op jit(solution)/shard_map/while/body/eval_jaxpr/all_to_all | solution.py:63
  705.8 33.3 %all_to_all.66 = bf16[4,2,81920]{2,1,0:T(2,128)(2,1)S(1)} all-to-all(bf16[4,2,81920]{2,1,0:T(2,128)(2,1)S(1)} %reshape.983), channel_id=1, replica_groups=mesh['slab'=2,'dom'=4,'coil'=4] {'dom'}, dimensions={0} | all-to-all | bytes 2621440 | tf_op jit(solution)/shard_map/while/body/eval_jaxpr/all_to_all | solution.py:64
  790.3 30.5 %all-to-all-done.1 = bf16[4,2,81920]{2,1,0:T(2,128)(2,1)} async-done(((bf16[4,2,81920]{2,1,0:T(2,128)(2,1)}), bf16[4,2,81920]{2,1,0:T(2,128)(2,1)}, u32[]{:S(2)}, u32[]{:S(2)}) %all-to-all-start.1) | async-done | bytes 1310752 | tf_op jit(solution)/shard_map/while/body/eval_jaxpr/all_to_all | solution.py:63
  850.4 33.3 %all_to_all.66 = bf16[4,2,81920]{2,1,0:T(2,128)(2,1)S(1)} all-to-all(bf16[4,2,81920]{2,1,0:T(2,128)(2,1)S(1)} %reshape.983), channel_id=1, replica_groups=mesh['slab'=2,'dom'=4,'coil'=4] {'dom'}, dimensions={0} | all-to-all | bytes 2621440 | tf_op jit(solution)/shard_map/while/body/eval_jaxpr/all_to_all | solution.py:64
  934.9 30.5 %all-to-all-done.1 = bf16[4,2,81920]{2,1,0:T(2,128)(2,1)} async-done(((bf16[4,2,81920]{2,1,0:T(2,128)(2,1)}), bf16[4,2,81920]{2,1,0:T(2,128)(2,1)}, u32[]{:S(2)}, u32[]{:S(2)}) %all-to-all-start.1) | async-done | bytes 1310752 | tf_op jit(solution)/shard_map/while/body/eval_jaxpr/all_to_all | solution.py:63
  995.0 33.3 %all_to_all.66 = bf16[4,2,81920]{2,1,0:T(2,128)(2,1)S(1)} all-to-all(bf16[4,2,81920]{2,1,0:T(2,128)(2,1)S(1)} %reshape.983), channel_id=1, replica_groups=mesh['slab'=2,'dom'=4,'coil'=4] {'dom'}, dimensions={0} | all-to-all | bytes 2621440 | tf_op jit(solution)/shard_map/while/body/eval_jaxpr/all_to_all | solution.py:64
  1079.5 30.5 %all-to-all-done.1 = bf16[4,2,81920]{2,1,0:T(2,128)(2,1)} async-done(((bf16[4,2,81920]{2,1,0:T(2,128)(2,1)}), bf16[4,2,81920]{2,1,0:T(2,128)(2,1)}, u32[]{:S(2)}, u32[]{:S(2)}) %all-to-all-start.1) | async-done | bytes 1310752 | tf_op jit(solution)/shard_map/while/body/eval_jaxpr/all_to_all | solution.py:63
  1139.6 33.3 %all_to_all.66 = bf16[4,2,81920]{2,1,0:T(2,128)(2,1)S(1)} all-to-all(bf16[4,2,81920]{2,1,0:T(2,128)(2,1)S(1)} %reshape.983), channel_id=1, replica_groups=mesh['slab'=2,'dom'=4,'coil'=4] {'dom'}, dimensions={0} | all-to-all | bytes 2621440 | tf_op jit(solution)/shard_map/while/body/eval_jaxpr/all_to_all | solution.py:64
  1224.1 30.5 %all-to-all-done.1 = bf16[4,2,81920]{2,1,0:T(2,128)(2,1)} async-done(((bf16[4,2,81920]{2,1,0:T(2,128)(2,1)}), bf16[4,2,81920]{2,1,0:T(2,128)(2,1)}, u32[]{:S(2)}, u32[]{:S(2)}) %all-to-all-start.1) | async-done | bytes 1310752 | tf_op jit(solution)/shard_map/while/body/eval_jaxpr/all_to_all | solution.py:63
  1284.2 33.3 %all_to_all.66 = bf16[4,2,81920]{2,1,0:T(2,128)(2,1)S(1)} all-to-all(bf16[4,2,81920]{2,1,0:T(2,128)(2,1)S(1)} %reshape.983), channel_id=1, replica_groups=mesh['slab'=2,'dom'=4,'coil'=4] {'dom'}, dimensions={0} | all-to-all | bytes 2621440 | tf_op jit(solution)/shard_map/while/body/eval_jaxpr/all_to_all | solution.py:64
  1368.7 30.5 %all-to-all-done.1 = bf16[4,2,81920]{2,1,0:T(2,128)(2,1)} async-done(((bf16[4,2,81920]{2,1,0:T(2,128)(2,1)}), bf16[4,2,81920]{2,1,0:T(2,128)(2,1)}, u32[]{:S(2)}, u32[]{:S(2)}) %all-to-all-start.1) | async-done | bytes 1310752 | tf_op jit(solution)/shard_map/while/body/eval_jaxpr/all_to_all | solution.py:63
  1428.8 33.3 %all_to_all.66 = bf16[4,2,81920]{2,1,0:T(2,128)(2,1)S(1)} all-to-all(bf16[4,2,81920]{2,1,0:T(2,128)(2,1)S(1)} %reshape.983), channel_id=1, replica_groups=mesh['slab'=2,'dom'=4,'coil'=4] {'dom'}, dimensions={0} | all-to-all | bytes 2621440 | tf_op jit(solution)/shard_map/while/body/eval_jaxpr/all_to_all | solution.py:64
  1513.3 30.5 %all-to-all-done.1 = bf16[4,2,81920]{2,1,0:T(2,128)(2,1)} async-done(((bf16[4,2,81920]{2,1,0:T(2,128)(2,1)}), bf16[4,2,81920]{2,1,0:T(2,128)(2,1)}, u32[]{:S(2)}, u32[]{:S(2)}) %all-to-all-start.1) | async-done | bytes 1310752 | tf_op jit(solution)/shard_map/while/body/eval_jaxpr/all_to_all | solution.py:63
  1573.4 33.3 %all_to_all.66 = bf16[4,2,81920]{2,1,0:T(2,128)(2,1)S(1)} all-to-all(bf16[4,2,81920]{2,1,0:T(2,128)(2,1)S(1)} %reshape.983), channel_id=1, replica_groups=mesh['slab'=2,'dom'=4,'coil'=4] {'dom'}, dimensions={0} | all-to-all | bytes 2621440 | tf_op jit(solution)/shard_map/while/body/eval_jaxpr/all_to_all | solution.py:64
  1657.8 30.5 %all-to-all-done.1 = bf16[4,2,81920]{2,1,0:T(2,128)(2,1)} async-done(((bf16[4,2,81920]{2,1,0:T(2,128)(2,1)}), bf16[4,2,81920]{2,1,0:T(2,128)(2,1)}, u32[]{:S(2)}, u32[]{:S(2)}) %all-to-all-start.1) | async-done | bytes 1310752 | tf_op jit(solution)/shard_map/while/body/eval_jaxpr/all_to_all | solution.py:63
  1718.0 33.3 %all_to_all.66 = bf16[4,2,81920]{2,1,0:T(2,128)(2,1)S(1)} all-to-all(bf16[4,2,81920]{2,1,0:T(2,128)(2,1)S(1)} %reshape.983), channel_id=1, replica_groups=mesh['slab'=2,'dom'=4,'coil'=4] {'dom'}, dimensions={0} | all-to-all | bytes 2621440 | tf_op jit(solution)/shard_map/while/body/eval_jaxpr/all_to_all | solution.py:64
  1802.4 30.5 %all-to-all-done.1 = bf16[4,2,81920]{2,1,0:T(2,128)(2,1)} async-done(((bf16[4,2,81920]{2,1,0:T(2,128)(2,1)}), bf16[4,2,81920]{2,1,0:T(2,128)(2,1)}, u32[]{:S(2)}, u32[]{:S(2)}) %all-to-all-start.1) | async-done | bytes 1310752 | tf_op jit(solution)/shard_map/while/body/eval_jaxpr/all_to_all | solution.py:63
  1849.5 31.8 %all-reduce.3.cloned.1.call-done = bf16[2,5,8,32,128]{4,3,2,1,0:T(8,128)(2,1)} async-done(((bf16[2,5,8,32,128]{4,3,2,1,0:T(8,128)(2,1)}), bf16[2,5,8,32,128]{4,3,2,1,0:T(8,128)(2,1)}) %all-reduce.3.cloned.1.call-update) | async-done | bytes 655376
  (562 shorter events, 978.7 us)
Async XLA Ops:
  6.5 1874.7 %all-reduce.3.cloned.1.call-start = ((), (), s32[]{:S(2)}) async-start(), calls=%async_computation.2 | async-start | bytes 1310720
  91.1 14.5 copy-start.4
  175.5 4.0 slice-start.2
  207.6 34.9 %all-to-all-start.1 = ((bf16[4,2,81920]{2,1,0:T(2,128)(2,1)}), bf16[4,2,81920]{2,1,0:T(2,128)(2,1)}, u32[]{:S(2)}, u32[]{:S(2)}) async-start(bf16[4,2,81920]{2,1,0:T(2,128)(2,1)} %reshape.985), calls=%async_computation.1 | async-start | bytes 2621440 | tf_op jit(solution)/shard_map/while/body/eval_jaxpr/all_to_all | solution.py:63
  320.2 4.0 slice-start.2
  352.2 34.8 %all-to-all-start.1 = ((bf16[4,2,81920]{2,1,0:T(2,128)(2,1)}), bf16[4,2,81920]{2,1,0:T(2,128)(2,1)}, u32[]{:S(2)}, u32[]{:S(2)}) async-start(bf16[4,2,81920]{2,1,0:T(2,128)(2,1)} %reshape.985), calls=%async_computation.1 | async-start | bytes 2621440 | tf_op jit(solution)/shard_map/while/body/eval_jaxpr/all_to_all | solution.py:63
  463.9 3.5 slice-start.1
  464.8 4.0 slice-start.2
  496.8 34.8 %all-to-all-start.1 = ((bf16[4,2,81920]{2,1,0:T(2,128)(2,1)}), bf16[4,2,81920]{2,1,0:T(2,128)(2,1)}, u32[]{:S(2)}, u32[]{:S(2)}) async-start(bf16[4,2,81920]{2,1,0:T(2,128)(2,1)} %reshape.985), calls=%async_computation.1 | async-start | bytes 2621440 | tf_op jit(solution)/shard_map/while/body/eval_jaxpr/all_to_all | solution.py:63
  608.5 3.5 slice-start.1
  609.4 4.0 slice-start.2
  641.4 34.8 %all-to-all-start.1 = ((bf16[4,2,81920]{2,1,0:T(2,128)(2,1)}), bf16[4,2,81920]{2,1,0:T(2,128)(2,1)}, u32[]{:S(2)}, u32[]{:S(2)}) async-start(bf16[4,2,81920]{2,1,0:T(2,128)(2,1)} %reshape.985), calls=%async_computation.1 | async-start | bytes 2621440 | tf_op jit(solution)/shard_map/while/body/eval_jaxpr/all_to_all | solution.py:63
  753.9 4.0 slice-start.2
  786.0 34.8 %all-to-all-start.1 = ((bf16[4,2,81920]{2,1,0:T(2,128)(2,1)}), bf16[4,2,81920]{2,1,0:T(2,128)(2,1)}, u32[]{:S(2)}, u32[]{:S(2)}) async-start(bf16[4,2,81920]{2,1,0:T(2,128)(2,1)} %reshape.985), calls=%async_computation.1 | async-start | bytes 2621440 | tf_op jit(solution)/shard_map/while/body/eval_jaxpr/all_to_all | solution.py:63
  897.6 3.5 slice-start.1
  898.5 4.0 slice-start.2
  930.6 34.8 %all-to-all-start.1 = ((bf16[4,2,81920]{2,1,0:T(2,128)(2,1)}), bf16[4,2,81920]{2,1,0:T(2,128)(2,1)}, u32[]{:S(2)}, u32[]{:S(2)}) async-start(bf16[4,2,81920]{2,1,0:T(2,128)(2,1)} %reshape.985), calls=%async_computation.1 | async-start | bytes 2621440 | tf_op jit(solution)/shard_map/while/body/eval_jaxpr/all_to_all | solution.py:63
  1042.2 3.5 slice-start.1
  1043.1 4.0 slice-start.2
  1075.2 34.8 %all-to-all-start.1 = ((bf16[4,2,81920]{2,1,0:T(2,128)(2,1)}), bf16[4,2,81920]{2,1,0:T(2,128)(2,1)}, u32[]{:S(2)}, u32[]{:S(2)}) async-start(bf16[4,2,81920]{2,1,0:T(2,128)(2,1)} %reshape.985), calls=%async_computation.1 | async-start | bytes 2621440 | tf_op jit(solution)/shard_map/while/body/eval_jaxpr/all_to_all | solution.py:63
  1186.8 3.5 slice-start.1
  1187.7 4.0 slice-start.2
  1219.8 34.8 %all-to-all-start.1 = ((bf16[4,2,81920]{2,1,0:T(2,128)(2,1)}), bf16[4,2,81920]{2,1,0:T(2,128)(2,1)}, u32[]{:S(2)}, u32[]{:S(2)}) async-start(bf16[4,2,81920]{2,1,0:T(2,128)(2,1)} %reshape.985), calls=%async_computation.1 | async-start | bytes 2621440 | tf_op jit(solution)/shard_map/while/body/eval_jaxpr/all_to_all | solution.py:63
  1332.3 4.0 slice-start.2
  1364.3 34.8 %all-to-all-start.1 = ((bf16[4,2,81920]{2,1,0:T(2,128)(2,1)}), bf16[4,2,81920]{2,1,0:T(2,128)(2,1)}, u32[]{:S(2)}, u32[]{:S(2)}) async-start(bf16[4,2,81920]{2,1,0:T(2,128)(2,1)} %reshape.985), calls=%async_computation.1 | async-start | bytes 2621440 | tf_op jit(solution)/shard_map/while/body/eval_jaxpr/all_to_all | solution.py:63
  1476.9 4.0 slice-start.2
  1508.9 34.8 %all-to-all-start.1 = ((bf16[4,2,81920]{2,1,0:T(2,128)(2,1)}), bf16[4,2,81920]{2,1,0:T(2,128)(2,1)}, u32[]{:S(2)}, u32[]{:S(2)}) async-start(bf16[4,2,81920]{2,1,0:T(2,128)(2,1)} %reshape.985), calls=%async_computation.1 | async-start | bytes 2621440 | tf_op jit(solution)/shard_map/while/body/eval_jaxpr/all_to_all | solution.py:63
  1621.5 4.0 slice-start.2
  1653.5 34.8 %all-to-all-start.1 = ((bf16[4,2,81920]{2,1,0:T(2,128)(2,1)}), bf16[4,2,81920]{2,1,0:T(2,128)(2,1)}, u32[]{:S(2)}, u32[]{:S(2)}) async-start(bf16[4,2,81920]{2,1,0:T(2,128)(2,1)} %reshape.985), calls=%async_computation.1 | async-start | bytes 2621440 | tf_op jit(solution)/shard_map/while/body/eval_jaxpr/all_to_all | solution.py:63
  1766.1 4.0 slice-start.2
  1798.1 34.8 %all-to-all-start.1 = ((bf16[4,2,81920]{2,1,0:T(2,128)(2,1)}), bf16[4,2,81920]{2,1,0:T(2,128)(2,1)}, u32[]{:S(2)}, u32[]{:S(2)}) async-start(bf16[4,2,81920]{2,1,0:T(2,128)(2,1)} %reshape.985), calls=%async_computation.1 | async-start | bytes 2621440 | tf_op jit(solution)/shard_map/while/body/eval_jaxpr/all_to_all | solution.py:63
  1845.5 35.7 %copy-start.5 = (f32[2,5,2,32,128]{4,3,2,1,0:T(8,128)S(1)}, f32[2,5,2,32,128]{4,3,2,1,0:T(8,128)}, u32[]{:S(2)}) copy-start(f32[2,5,2,32,128]{4,3,2,1,0:T(8,128)} %param.13) | copy-start | bytes 983044
  (80 other events, 167.6 us)
Sparse Core Ops, SparseCore 0:
  1848.3 32.8 all-reduce.2
where the time goes:
time: 1910 us; the launch traced here: 1890 us
  local copies, waits for them, and re-layouts  662 us (35%)
  blocking collectives  404 us (21%)
  waiting for transfers between devices  397 us (21%)
  other arithmetic  200 us (10%)
  matrix products  157 us (8%)
  starting transfers between devices  51.8 us (3%)
    all_to_all x12, blocking collectives, route_grid(): lax.all_to_all(rows, 'dom', split_axis=5, concat_axis=4, tiled=True)  404 us
    all_to_all x12, waiting for transfers between devices, route_grid(): lax.all_to_all(spectral(lax.all_to_all(rows, 'dom', split_axis=5, concat_...  366 us
    while x240, local copies, waits for them, and re-layouts  260 us
    another operation x45, other arithmetic  190 us
    another operation x24, local copies, waits for them, and re-layouts  148 us
    convert_element_type x12, local copies, waits for them, and re-layouts, one_turn(): transform(forward_y, partition, 'oiyw,ibkqry->obkqrw').astype(jnp.bfloat16)  99.3 us
    dot_general x72, matrix products, transform(): return jnp.einsum(form, table, data, preferred_element_type=jnp.float32)  93.5 us
    convert_element_type x12, local copies, waits for them, and re-layouts, spectral(): transform(inverse_x, weighted, 'oiux,ibkqwu->obkqwx').astype(jnp.bfloat16)  70 us
  transfers between devices with their start and end apart: 13, of which 13 were waited for; matrix products, arithmetic and copies ran while one was open for 0% of the time, Pallas kernels for 0%

commit v1 on v0

v1 whole, which is shorter than its diff:
```python
import functools
import math

import jax
import jax.numpy as jnp
import numpy as np
from jax import lax
from jax.experimental import pallas as pl
from jax.experimental.pallas import tpu as pltpu
from jax.sharding import PartitionSpec as P

K = 5
NZ = 8
BF = jnp.bfloat16
F32 = jnp.float32
HALF = math.sqrt(0.5)


def table(count_in, count_out, length, sign):
    phase = (np.arange(count_in)[:, None] * np.arange(count_out)[None, :] % length).astype(
        np.float32
    ) * np.float32(2.0 * math.pi / length)
    scale = 1.0 / math.sqrt(length)
    cosine = np.cos(phase) * np.float32(scale)
    sine = np.sin(phase) * np.float32(sign * scale)
    return np.stack([np.stack([cosine, -sine]), np.stack([sine, cosine])]).astype(BF)


def add(a, b):
    return (a[0] + b[0], a[1] + b[1])


def sub(a, b):
    return (a[0] - b[0], a[1] - b[1])


def add_turned(a, b, sign):
    return (a[0] - b[1], a[1] + b[0]) if sign > 0 else (a[0] + b[1], a[1] - b[0])


def four(v, sign):
    a, b = add(v[0], v[2]), sub(v[0], v[2])
    c, d = add(v[1], v[3]), sub(v[1], v[3])
    return [add(a, c), add_turned(b, d, sign), sub(a, c), add_turned(b, d, -sign)]


def eight(re, im, sign):
    v = list(zip(re, im))
    e, o = four(v[0::2], sign), four(v[1::2], sign)
    h = jnp.asarray(HALF, re[0].dtype)
    once = add_turned(o[1], o[1], sign)
    once = (once[0] * h, once[1] * h)
    thrice = add_turned((-o[3][0], -o[3][1]), o[3], sign)
    thrice = (thrice[0] * h, thrice[1] * h)
    out = [None] * 8
    for q, t in ((0, o[0]), (1, once), (3, thrice)):
        out[q], out[q + 4] = add(e[q], t), sub(e[q], t)
    out[2], out[6] = add_turned(e[2], o[2], sign), add_turned(e[2], o[2], -sign)
    return [x[0] for x in out], [x[1] for x in out]


def tree(terms):
    while len(terms) > 1:
        terms = [
            terms[i] + terms[i + 1] if i + 1 < len(terms) else terms[i]
            for i in range(0, len(terms), 2)
        ]
    return terms[0]


def coils_kernel(width, pieces, first, last, *refs):
    maps = refs[:pieces]
    image, weights_hbm, ty, tx, tix, tiy = refs[pieces : pieces + 6]
    rest = list(refs[pieces + 6 :])
    acc_in = None if first else rest.pop(0)
    out = rest.pop(0)
    rows, spec, mid, weights, sem = rest[:5]
    acc = rest[5] if last else out
    tiles = width // 16
    step = pl.program_id(0)
    fetch = pltpu.make_async_copy(weights_hbm, weights, sem)

    @pl.when(step == 0)
    def _():
        fetch.start()
        acc[...] = jnp.zeros_like(acc) if first else acc_in[...]

    def maps_of(part, z):
        return jnp.concatenate([m[part, 0, z] for m in maps], axis=0)

    def forward(j, _):
        for z in range(NZ):
            mr, mi = maps_of(0, z), maps_of(1, z)
            ir = jnp.concatenate([image[r, 0, j, z] for r in range(pieces)], axis=0)
            ii = jnp.concatenate([image[r, 1, j, z] for r in range(pieces)], axis=0)
            product = jnp.concatenate([mr * ir - mi * ii, mr * ii + mi * ir], axis=1)
            rows[z] = jnp.dot(product, ty[...], preferred_element_type=F32).astype(BF).T
        for t in range(tiles):
            a, b = pl.ds(t * 16, 16), pl.ds(width + t * 16, 16)
            re, im = eight(
                [rows[z, a].astype(F32) for z in range(NZ)],
                [rows[z, b].astype(F32) for z in range(NZ)],
                -1,
            )
            for q in range(NZ):
                mid[q, a] = jnp.concatenate([re[q], im[q]], axis=1).astype(BF)
        for q in range(NZ):
            spec[j, q] = jnp.dot(mid[q], tx[...], preferred_element_type=F32).astype(BF)
        return 0

    lax.fori_loop(0, K, forward, 0)

    @pl.when(step == 0)
    def _():
        fetch.wait()

    half = tx.shape[1] // 2

    def apply(i, _):
        q = i // tiles
        a = pl.ds(pl.multiple_of(i % tiles * 16, 16), 16)
        sr = [spec[j, q, a, :half] for j in range(K)]
        si = [spec[j, q, a, half:] for j in range(K)]
        for k in range(K):
            re, im = [], []
            for j in range(K):
                kr, ki = weights[q, k, j, 0, a], weights[q, k, j, 1, a]
                re.append(kr * sr[j] - ki * si[j])
                im.append(kr * si[j] + ki * sr[j])
            spec[k, q, a, :half] = tree(re)
            spec[k, q, a, half:] = tree(im)
        return 0

    lax.fori_loop(0, NZ * tiles, apply, 0)
    ny = tiy.shape[1] // 2
    nx = tix.shape[1] // 2

    def inverse(k, _):
        for q in range(NZ):
            mid[q] = jnp.dot(spec[k, q], tix[...], preferred_element_type=F32).astype(BF)
        for t in range(tiles):
            a, b = pl.ds(t * 16, 16), pl.ds(width + t * 16, 16)
            re, im = eight(
                [mid[q, a, :nx].astype(F32) for q in range(NZ)],
                [mid[q, a, nx:].astype(F32) for q in range(NZ)],
                1,
            )
            for z in range(NZ):
                rows[z, a] = re[z].astype(BF)
                rows[z, b] = im[z].astype(BF)
        for z in range(NZ):
            back = jnp.dot(rows[z].T, tiy[...], preferred_element_type=F32)
            br, bi = back[:, :ny], back[:, ny:]
            mr, mi = maps_of(0, z).astype(F32), maps_of(1, z).astype(F32)
            acc[z, 0, k] += mr * br + mi * bi
            acc[z, 1, k] += mr * bi - mi * br
        return 0

    lax.fori_loop(0, K, inverse, 0)
    if last:

        @pl.when(step == pl.num_programs(0) - 1)
        def _():
            out[...] = acc[...].astype(BF)


def coils(maps, image, weights, tables, acc, last):
    count = maps[0].shape[1]
    width = tables[0].shape[1] // 2
    nx, ny = tables[2].shape[1] // 2, tables[3].shape[1] // 2
    pieces = len(maps)
    whole = lambda a: pl.BlockSpec(
        a.shape, lambda c: (0,) * a.ndim, pipeline_mode=pl.Buffered(buffer_count=1)
    )
    shape = (NZ, 2, K, nx, ny)
    out = jax.ShapeDtypeStruct(shape, BF if last else F32)
    args = [*maps, image, weights, *tables]
    specs = [pl.BlockSpec((2, 1) + m.shape[2:], lambda c: (0, c, 0, 0, 0)) for m in maps]
    specs += [whole(image), pl.BlockSpec(memory_space=pl.ANY)] + [whole(t) for t in tables]
    if acc is not None:
        args.append(acc)
        specs.append(whole(acc))
    scratch = [
        pltpu.VMEM((NZ, 2 * width, nx), BF),
        pltpu.VMEM((K, NZ, width, tables[1].shape[1]), BF),
        pltpu.VMEM((NZ, width, 2 * nx), BF),
        pltpu.VMEM(weights.shape, BF),
        pltpu.SemaphoreType.DMA,
    ]
    if last:
        scratch.append(pltpu.VMEM(shape, F32))
    planes = count * K * NZ
    return pl.pallas_call(
        functools.partial(coils_kernel, width, pieces, acc is None, last),
        grid=(count,),
        in_specs=specs,
        out_specs=whole(out),
        out_shape=out,
        scratch_shapes=scratch,
        compiler_params=pltpu.CompilerParams(vmem_limit_bytes=60 * 2**20),
        cost_estimate=pl.CostEstimate(
            flops=planes * width * 4 * 2 * 200_000, bytes_accessed=30_000_000, transcendentals=0
        ),
    )(*args)


def kernel_weights(sampled, basis_products, point_spread, pad):
    scale = float(table(1, 1, NZ, 1)[0, 0, 0, 0].astype(np.float32)) ** 2
    picked = basis_products[:, :, :, :, None] * (
        sampled.astype(F32)[:, None, None, None, :] * scale
    )
    real, imag = picked[:, 0], picked[:, 1]
    pairs = jnp.stack([jnp.stack([real, -imag], 1), jnp.stack([imag, real], 1)], 1)
    spread = point_spread.astype(BF)
    if pad:
        spread = jnp.pad(spread, ((0, 0), (0, 0), (0, pad), (0, 0)))
    return jnp.einsum(
        "gpikjq,givu->qkjpvu", pairs.astype(BF), spread, preferred_element_type=F32
    ).astype(BF)


def swap(value, axis, bit):
    size = lax.axis_size(axis)
    return lax.ppermute(value, axis, [(i, i ^ bit) for i in range(size)])


def gather_rows(value, axis):
    one, two = swap(value, axis, 1), swap(value, axis, 2)
    return [value, one, two, swap(two, axis, 1)]


def body(basis_image, coil_maps, point_spread, basis_products, sampled, adjoint_data):
    dom, here = lax.axis_size("dom"), lax.axis_index("dom")
    coil, me = lax.axis_size("coil"), lax.axis_index("coil")
    rows, ny = basis_image.shape[3], basis_image.shape[4]
    nx = rows * dom
    own = point_spread.shape[2]
    width = max(64, own)
    butterfly = dom == 4 and coil == 4 and rows % 16 == 0

    forward, inverse = table(nx, 2 * nx, 2 * nx, -1), table(2 * nx, nx, 2 * nx, 1)
    tx = forward.transpose(1, 2, 0, 3)
    tix = inverse.transpose(1, 2, 0, 3)
    forward, inverse = table(ny, 2 * ny, 2 * ny, -1), table(2 * ny, ny, 2 * ny, 1)
    extra = ((0, 0), (0, 0), (0, 0), (0, width - own))
    ty = np.pad(forward.transpose(1, 2, 0, 3), extra)
    tiy = np.pad(inverse.transpose(1, 3, 0, 2), extra).transpose(0, 3, 2, 1)
    ty = lax.dynamic_slice_in_dim(jnp.asarray(ty), here * own, width, 3).reshape(2 * ny, 2 * width)
    tiy = lax.dynamic_slice_in_dim(jnp.asarray(tiy), here * own, width, 1).reshape(
        2 * width, 2 * ny
    )
    weights = kernel_weights(sampled, basis_products, point_spread, width - own)

    if butterfly:
        order = here ^ jnp.arange(dom)
        tx = jnp.take(jnp.asarray(tx.reshape(2, dom, rows, -1)), order, axis=1)
        tix = jnp.take(jnp.asarray(tix.reshape(2 * 2 * nx * 2, dom, rows)), order, axis=1)
        core = me % 2
        mine = lax.dynamic_slice_in_dim(basis_image, core * (NZ // 2), NZ // 2, 2)
        mine = jnp.stack(gather_rows(mine, "dom"))
        other = swap(mine, "coil", 1)
        image = jnp.concatenate(
            [jnp.where(core == 0, mine, other), jnp.where(core == 0, other, mine)], axis=3
        )
        chunks = CHUNKS
    else:
        image = lax.all_gather(basis_image, "dom", axis=3, tiled=True)[None]
        chunks = (coil_maps.shape[1],)
    tx, tix = jnp.asarray(tx).reshape(2 * nx, 4 * nx), jnp.asarray(tix).reshape(4 * nx, 2 * nx)
    tables = (ty, tx, tix, tiy)

    total, start = None, 0
    for count in chunks:
        part = lax.slice_in_dim(coil_maps, start, start + count, axis=1)
        start += count
        if butterfly:
            maps = gather_rows(part, "dom")
        else:
            maps = [lax.all_gather(part, "dom", axis=3, tiled=True)]
        total = coils(maps, image, weights, tables, total, start == coil_maps.shape[1])

    if not butterfly:
        total = lax.psum_scatter(total.transpose(1, 2, 0, 3, 4), "coil", scatter_dimension=2, tiled=True)
        total = lax.psum_scatter(total, "dom", scatter_dimension=3, tiled=True)
        return total.astype(F32) - adjoint_data

    def exchange(value, dim, bit, axis, index):
        send = lax.dynamic_index_in_dim(value, 1 - index, dim, keepdims=False)
        keep = lax.dynamic_index_in_dim(value, index, dim, keepdims=False)
        return keep.astype(F32) + swap(send.astype(BF), axis, bit).astype(F32)

    total = total.reshape(coil // 2, 2, NZ // coil, 2, K, dom // 2, 2, rows, ny)
    total = exchange(total, 1, 1, "coil", me % 2)
    total = exchange(total.astype(BF), 0, 2, "coil", me // 2)
    total = total.astype(BF)
    keep, send = total[:, :, :, :, 0], total[:, :, :, :, 1]
    total = (keep.astype(F32) + swap(send, "dom", 1).astype(F32)).astype(BF)
    keep, send = total[:, :, :, 0], total[:, :, :, 1]
    total = keep.astype(F32) + swap(send, "dom", 2).astype(F32)
    return total.transpose(1, 2, 0, 3, 4) - adjoint_data


CHUNKS = (3, 3, 3, 3)


def solution(mesh):
    placed = (
        P(None, None, "slab", "dom", None),
        P(None, "coil", "slab", "dom", None),
        P(None, None, "dom", None),
        P(),
        P(),
        P(None, None, ("slab", "coil"), "dom", None),
    )
    return jax.shard_map(
        body,
        mesh=mesh,
        in_specs=placed,
        out_specs=P(None, None, ("slab", "coil"), "dom", None),
        check_vma=False,
    )
```

time: 1910 us -> 317 us (0.17); the launches traced: 1890 us -> 317 us
  local copies, waits for them, and re-layouts: 662 us -> 27.7 us
  blocking collectives: 404 us -> 0 us
  waiting for transfers between devices: 397 us -> 78.1 us
  other arithmetic: 200 us -> 12.9 us
  Pallas kernels: 0 us -> 156 us
  matrix products: 157 us -> 6.69 us
    all_to_all x12 -> x0, blocking collectives: 404 us -> none  [route_grid(): lax.all_to_all(rows, 'dom', split_axis=5, concat_axis=4, tiled=True)]
    all_to_all x12 -> x0, waiting for transfers between devices: 366 us -> none  [route_grid(): lax.all_to_all(spectral(lax.all_to_all(rows, 'dom', split_axis=5, concat_...]
    while x241 -> x0, local copies, waits for them, and re-layouts: 262 us -> none
    another operation x51 -> x3, other arithmetic: 190 us -> 3.08 us  [the longest x1 2.34 us: body(): mine = jnp.stack(gather_rows(mine, 'dom'))]
    convert_element_type x24 -> x0, local copies, waits for them, and re-layouts: 169 us -> none  [the longest x12 99.3 us: one_turn(): transform(forward_y, partition, 'oiyw,ibkqry->obkqrw').astype(jnp.bfloat16)]
    pallas_call x0 -> x4, Pallas kernels: none -> 156 us  [coils(): pl.pallas_call(functools.partial(coils_kernel, width, pieces, acc is None...]
    dot_general x76 -> x1, matrix products: 157 us -> 6.69 us  [kernel_weights(): jnp.einsum('gpikjq,givu->qkjpvu', pairs.astype(BF), spread, preferred_ele...]
    another operation x24 -> x1, local copies, waits for them, and re-layouts: 148 us -> 0.02 us  [body(): mine = jnp.stack(gather_rows(mine, 'dom'))]
  transfers between devices with their start and end apart: 13 -> 20, of which waited for: 13 -> 7; matrix products, arithmetic and copies ran while one was open for 0% -> 12% of each run, Pallas kernels for 0% -> 37%
where the time goes in v1:
time: 317 us
  Pallas kernels  156 us (49%)
  waiting for transfers between devices  78.1 us (25%)
  starting transfers between devices  34.9 us (11%)
  local copies, waits for them, and re-layouts  27.7 us (9%)
  other arithmetic  12.9 us (4%)
  matrix products  6.69 us (2%)
    pallas_call x4, Pallas kernels, coils(): pl.pallas_call(functools.partial(coils_kernel, width, pieces, acc is None...  156 us
    ppermute x20, waiting for transfers between devices, swap(): return lax.ppermute(value, axis, [(i, i ^ bit) for i in range(size)])  78.1 us
    ppermute x20, starting transfers between devices, swap(): return lax.ppermute(value, axis, [(i, i ^ bit) for i in range(size)])  34.9 us
    dot_general x1, local copies, waits for them, and re-layouts, kernel_weights(): jnp.einsum('gpikjq,givu->qkjpvu', pairs.astype(BF), spread, preferred_ele...  10.7 us
    dot_general x1, matrix products, kernel_weights(): jnp.einsum('gpikjq,givu->qkjpvu', pairs.astype(BF), spread, preferred_ele...  6.69 us
  transfers between devices with their start and end apart: 20, of which 7 were waited for; matrix products, arithmetic and copies ran while one was open for 12% of the time, Pallas kernels for 37%

profile of v1, /device:TPU:0, one launch (start us, length us, event | category | flops | bytes accessed | tf_op | source)
XLA Modules:
  0.0 316.7 jit_solution(12972806214795935003)
XLA Ops:
  1.8 4.0 %collective-permute-start.4 = (bf16[2,5,4,32,128]{4,3,2,1,0:T(8,128)(2,1)}, bf16[2,5,4,32,128]{4,3,2,1,0:T(8,128)(2,1)S(1)}, u32[]{:S(2)}, u32[]{:S(2)}) collective-permute-start(bf16[2,5,4,32,128]{4,3,2,1,0:T(8,128)(2,1)} %constant_dynamic-slice_fusion.4), channel_id=1, source_target_pairs={{0,8},{4,12},{8,0},{12,4},{1,9},{5,13},{9,1},{13,5},{2,10},{6,14},... | collective-permute-start | bytes 983048 | tf_op jit(solution)/shard_map/ppermute | solution.py:224
  5.9 1.6 collective-permute-start.3
  7.5 2.7 fusion.11
  10.6 2.9 collective-permute-start.11
  15.3 7.3 %collective-permute-done.4 = bf16[2,5,4,32,128]{4,3,2,1,0:T(8,128)(2,1)S(1)} collective-permute-done((bf16[2,5,4,32,128]{4,3,2,1,0:T(8,128)(2,1)}, bf16[2,5,4,32,128]{4,3,2,1,0:T(8,128)(2,1)S(1)}, u32[]{:S(2)}, u32[]{:S(2)}) %collective-permute-start.4) | collective-permute-done | bytes 327712 | tf_op jit(solution)/shard_map/ppermute | solution.py:224
  22.7 2.5 convert_bitcast_fusion
  25.2 2.0 collective-permute-start.10
  27.2 27.7 %collective-permute-done.5 = bf16[2,5,4,32,128]{4,3,2,1,0:T(8,128)(2,1)S(1)} collective-permute-done((bf16[2,5,4,32,128]{4,3,2,1,0:T(8,128)(2,1)S(1)}, bf16[2,5,4,32,128]{4,3,2,1,0:T(8,128)(2,1)S(1)}, u32[]{:S(2)}, u32[]{:S(2)}) %collective-permute-start.5) | collective-permute-done | bytes 327712 | tf_op jit(solution)/shard_map/ppermute | solution.py:224
  54.9 2.3 pad_maximum_fusion.1
  59.5 6.7 %convolution_bitcast_fusion = bf16[2,5,5,8,64,256]{5,3,4,2,1,0:T(8,128)(2,1)} fusion(bf16[32,2,64,256,1,1,1]{3,2,1,0,6,5,4:T(8,128)(2,1)S(1)} %convert_bitcast_fusion, bf16[32,1,2,5,5,8]{0,5,2,4,3,1:T(8,128)(2,1)S(1)} %copy-done.10, bf16[32,1,2,5,5,8]{0,5,2,4,3,1:T(8,128)(2,1)S(1)} %copy-done.9), kind=kOutput, calls=%fused_computation.3 | convolution fusion | flops 838963200 | bytes 15255552 | tf_op jit(solution)/shard_map/gpikjq,givu->qkjpvu/dot_general | solution.py:217
  66.2 10.7 %copy.44 = bf16[2,5,5,8,64,256]{5,4,0,2,1,3:T(8,128)(2,1)} copy(bf16[2,5,5,8,64,256]{5,3,4,2,1,0:T(8,128)(2,1)} %convolution_bitcast_fusion) | data formatting | bytes 26214400 | tf_op jit(solution)/shard_map/gpikjq,givu->qkjpvu/dot_general | solution.py:217
  78.4 1.4 select_n.87.refs_8_
  82.7 1.6 broadcast_select_fusion.1
  84.3 1.8 pad_maximum_fusion.refs_4_
  86.1 1.8 collective-permute-start.7
  87.9 1.8 collective-permute-start.1
  89.7 10.8 %collective-permute-done.15.refs_3_ = bf16[2,3,8,32,128]{4,3,2,1,0:T(8,128)(2,1)S(1)} collective-permute-done((bf16[2,3,8,32,128]{4,3,2,1,0:T(8,128)(2,1)}, bf16[2,3,8,32,128]{4,3,2,1,0:T(8,128)(2,1)S(1)}, u32[]{:S(2)}, u32[]{:S(2)}) %collective-permute-start.15) | collective-permute-done | bytes 393248 | tf_op jit(solution)/shard_map/ppermute | solution.py:224
  100.5 2.4 collective-permute-start.12
  102.9 38.0 %shard_map.100.refs_10_ = f32[8,2,5,128,128]{4,3,2,1,0:T(8,128)} custom-call(bf16[2,3,8,32,128]{4,3,2,1,0:T(8,128)(2,1)} %get-tuple-element.9.refs_0_, bf16[2,3,8,32,128]{4,3,2,1,0:T(8,128)(2,1)} %collective-permute-done.13.refs_1_, bf16[2,3,8,32,128]{4,3,2,1,0:T(8,128)(2,1)} %collective-permute-done.14.refs_2_, bf16[2,3,8,32,128]{4,3,2,1,0:T(8,128)(2,1)} %copy-done.17, ...), custom_call_target="tpu_custom_call" | custom-call | flops 12288000000 | bytes 30000000 | tf_op jit(solution)/shard_map/pallas_call | solution.py:193
  141.6 1.3 collective-permute-start.9
  144.4 39.6 %shard_map.101.refs_10_ = f32[8,2,5,128,128]{4,3,2,1,0:T(8,128)} custom-call(bf16[2,3,8,32,128]{4,3,2,1,0:T(8,128)(2,1)} %get-tuple-element.12.refs_0_, bf16[2,3,8,32,128]{4,3,2,1,0:T(8,128)(2,1)} %collective-permute-done.10.refs_1_, bf16[2,3,8,32,128]{4,3,2,1,0:T(8,128)(2,1)} %collective-permute-done.11.refs_2_, bf16[2,3,8,32,128]{4,3,2,1,0:T(8,128)(2,1)} %copy-done.19, ...), custom_call_target="tpu_custom_call" | custom-call | flops 12288000000 | bytes 30000000 | tf_op jit(solution)/shard_map/pallas_call | solution.py:193
  184.8 39.5 %shard_map.102.refs_10_ = f32[8,2,5,128,128]{4,3,2,1,0:T(8,128)} custom-call(bf16[2,3,8,32,128]{4,3,2,1,0:T(8,128)(2,1)} %get-tuple-element.10.refs_0_, bf16[2,3,8,32,128]{4,3,2,1,0:T(8,128)(2,1)} %copy-done.15, bf16[2,3,8,32,128]{4,3,2,1,0:T(8,128)(2,1)} %copy-done.13, bf16[2,3,8,32,128]{4,3,2,1,0:T(8,128)(2,1)} %collective-permute-done.9.refs_3_, ...), custom_call_target="tpu_custom_call" | custom-call | flops 12288000000 | bytes 30000000 | tf_op jit(solution)/shard_map/pallas_call | solution.py:193
  225.8 39.0 %shard_map.103 = bf16[8,2,5,128,128]{4,3,2,1,0:T(8,128)(2,1)} custom-call(bf16[2,3,8,32,128]{4,3,2,1,0:T(8,128)(2,1)} %get-tuple-element.11.refs_0_, bf16[2,3,8,32,128]{4,3,2,1,0:T(8,128)(2,1)} %copy-done.16, bf16[2,3,8,32,128]{4,3,2,1,0:T(8,128)(2,1)} %copy-done.14, bf16[2,3,8,32,128]{4,3,2,1,0:T(8,128)(2,1)} %copy-done.18, ...), custom_call_target="tpu_custom_call" | custom-call | flops 12288000000 | bytes 30000000 | tf_op jit(solution)/shard_map/pallas_call | solution.py:193
  264.9 2.3 constant_dynamic-slice_fusion.1
  267.6 3.1 collective-permute-done.16
  270.8 1.9 fusion.1
  272.7 1.6 collective-permute-start.17
  274.3 15.3 %collective-permute-done.17 = bf16[2,2,5,2,2,32,128]{6,5,0,2,1,3,4:T(8,128)(2,1)S(1)} collective-permute-done((bf16[2,2,5,2,2,32,128]{6,5,0,2,1,3,4:T(8,128)(2,1)S(1)}, bf16[2,2,5,2,2,32,128]{6,5,0,2,1,3,4:T(8,128)(2,1)S(1)}, u32[]{:S(2)}, u32[]{:S(2)}) %collective-permute-start.17) | collective-permute-done | bytes 655392 | tf_op jit(solution)/shard_map/ppermute | solution.py:224
  289.8 1.4 collective-permute-start.18
  291.2 7.6 %collective-permute-done.18 = bf16[2,2,5,2,32,128]{5,4,0,2,1,3:T(8,128)(2,1)S(1)} collective-permute-done((bf16[2,2,5,2,32,128]{5,4,0,2,1,3:T(8,128)(2,1)S(1)}, bf16[2,2,5,2,32,128]{5,4,0,2,1,3:T(8,128)(2,1)S(1)}, u32[]{:S(2)}, u32[]{:S(2)}) %collective-permute-start.18) | collective-permute-done | bytes 327712 | tf_op jit(solution)/shard_map/ppermute | solution.py:224
  298.9 10.7 %collective-permute-start.19 = (bf16[2,2,5,32,128]{4,3,0,2,1:T(8,128)(2,1)S(1)}, bf16[2,2,5,32,128]{4,3,0,2,1:T(8,128)(2,1)S(1)}, u32[]{:S(2)}, u32[]{:S(2)}) collective-permute-start(bf16[2,2,5,32,128]{4,3,0,2,1:T(8,128)(2,1)S(1)} %slice_bitcast_fusion.2), channel_id=1, source_target_pairs={{0,8},{4,12},{8,0},{12,4},{1,9},{5,13},{9,1},{13,5},{2,10},{6,14},... | collective-permute-start | bytes 491528 | tf_op jit(solution)/shard_map/ppermute | solution.py:224
  309.6 6.3 %collective-permute-done.19 = bf16[2,2,5,32,128]{4,3,0,2,1:T(8,128)(2,1)S(1)} collective-permute-done((bf16[2,2,5,32,128]{4,3,0,2,1:T(8,128)(2,1)S(1)}, bf16[2,2,5,32,128]{4,3,0,2,1:T(8,128)(2,1)S(1)}, u32[]{:S(2)}, u32[]{:S(2)}) %collective-permute-start.19) | collective-permute-done | bytes 163872 | tf_op jit(solution)/shard_map/ppermute | solution.py:224
  (92 shorter events, 16.9 us)
Async XLA Ops:
  1.8 11.7 %copy-start.12 = (s32[32,8]{0,1:T(8,128)S(1)}, s32[32,8]{0,1:T(8,128)}, u32[]{:S(2)}) copy-start(s32[32,8]{0,1:T(8,128)} %param.14) | copy-start | bytes 3076
  1.8 11.7 %copy-start.11 = (f32[32,2,5,5]{0,1,3,2:T(2,128)S(1)}, f32[32,2,5,5]{0,1,3,2:T(2,128)}, u32[]{:S(2)}) copy-start(f32[32,2,5,5]{0,1,3,2:T(2,128)} %param.13) | copy-start | bytes 19204
  1.8 20.7 %collective-permute-start.4 = (bf16[2,5,4,32,128]{4,3,2,1,0:T(8,128)(2,1)}, bf16[2,5,4,32,128]{4,3,2,1,0:T(8,128)(2,1)S(1)}, u32[]{:S(2)}, u32[]{:S(2)}) collective-permute-start(bf16[2,5,4,32,128]{4,3,2,1,0:T(8,128)(2,1)} %constant_dynamic-slice_fusion.4), channel_id=1, source_target_pairs={{0,8},{4,12},{8,0},{12,4},{1,9},{5,13},{9,1},{13,5},{2,10},{6,14},... | collective-permute-start | bytes 983048 | tf_op jit(solution)/shard_map/ppermute | solution.py:224
  5.9 19.3 %collective-permute-start.3 = (bf16[2,5,4,32,128]{4,3,2,1,0:T(8,128)(2,1)}, bf16[2,5,4,32,128]{4,3,2,1,0:T(8,128)(2,1)}, u32[]{:S(2)}, u32[]{:S(2)}) collective-permute-start(bf16[2,5,4,32,128]{4,3,2,1,0:T(8,128)(2,1)} %constant_dynamic-slice_fusion.4), channel_id=1, source_target_pairs={{0,4},{4,0},{8,12},{12,8},{1,5},{5,1},{9,13},{13,9},{2,6},{6,2},{1... | collective-permute-start | bytes 983048 | tf_op jit(solution)/shard_map/ppermute | solution.py:224
  10.2 71.2 %collective-permute-start.14 = (bf16[2,3,8,32,128]{4,3,2,1,0:T(8,128)(2,1)}, bf16[2,3,8,32,128]{4,3,2,1,0:T(8,128)(2,1)}, u32[]{:S(2)}, u32[]{:S(2)}) collective-permute-start(bf16[2,3,8,32,128]{4,3,2,1,0:T(8,128)(2,1)} %get-tuple-element.9.refs_0_), channel_id=1, source_target_pairs={{0,8},{4,12},{8,0},{12,4},{1,9},{5,13},{9,1},{13,5},{2,10},{6,14},... | collective-permute-start | bytes 1179656 | tf_op jit(solution)/shard_map/ppermute | solution.py:224
  10.5 75.6 %collective-permute-start.13 = (bf16[2,3,8,32,128]{4,3,2,1,0:T(8,128)(2,1)}, bf16[2,3,8,32,128]{4,3,2,1,0:T(8,128)(2,1)}, u32[]{:S(2)}, u32[]{:S(2)}) collective-permute-start(bf16[2,3,8,32,128]{4,3,2,1,0:T(8,128)(2,1)} %get-tuple-element.9.refs_0_), channel_id=1, source_target_pairs={{0,4},{4,0},{8,12},{12,8},{1,5},{5,1},{9,13},{13,9},{2,6},{6,2},{1... | collective-permute-start | bytes 1179656 | tf_op jit(solution)/shard_map/ppermute | solution.py:224
  10.6 77.3 %collective-permute-start.11 = (bf16[2,3,8,32,128]{4,3,2,1,0:T(8,128)(2,1)}, bf16[2,3,8,32,128]{4,3,2,1,0:T(8,128)(2,1)}, u32[]{:S(2)}, u32[]{:S(2)}) collective-permute-start(bf16[2,3,8,32,128]{4,3,2,1,0:T(8,128)(2,1)} %get-tuple-element.12.refs_0_), channel_id=1, source_target_pairs={{0,8},{4,12},{8,0},{12,4},{1,9},{5,13},{9,1},{13,5},{2,10},{6,14},... | collective-permute-start | bytes 1179656 | tf_op jit(solution)/shard_map/ppermute | solution.py:224
  22.6 32.3 %collective-permute-start.5 = (bf16[2,5,4,32,128]{4,3,2,1,0:T(8,128)(2,1)S(1)}, bf16[2,5,4,32,128]{4,3,2,1,0:T(8,128)(2,1)S(1)}, u32[]{:S(2)}, u32[]{:S(2)}) collective-permute-start(bf16[2,5,4,32,128]{4,3,2,1,0:T(8,128)(2,1)S(1)} %collective-permute-done.4), channel_id=1, source_target_pairs={{0,4},{4,0},{8,12},{12,8},{1,5},{5,1},{9,13},{13,9},{2,6},{6,2},{1... | collective-permute-start | bytes 983048 | tf_op jit(solution)/shard_map/ppermute | solution.py:224
  25.2 115.6 %collective-permute-start.10 = (bf16[2,3,8,32,128]{4,3,2,1,0:T(8,128)(2,1)}, bf16[2,3,8,32,128]{4,3,2,1,0:T(8,128)(2,1)}, u32[]{:S(2)}, u32[]{:S(2)}) collective-permute-start(bf16[2,3,8,32,128]{4,3,2,1,0:T(8,128)(2,1)} %get-tuple-element.12.refs_0_), channel_id=1, source_target_pairs={{0,4},{4,0},{8,12},{12,8},{1,5},{5,1},{9,13},{13,9},{2,6},{6,2},{1... | collective-permute-start | bytes 1179656 | tf_op jit(solution)/shard_map/ppermute | solution.py:224
  54.9 4.6 %copy-start.9 = (bf16[32,1,2,5,5,8]{0,5,2,4,3,1:T(8,128)(2,1)S(1)}, bf16[32,1,2,5,5,8]{0,5,2,4,3,1:T(8,128)(2,1)}, u32[]{:S(2)}) copy-start(bf16[32,1,2,5,5,8]{0,5,2,4,3,1:T(8,128)(2,1)} %get-tuple-element.15) | copy-start | bytes 76804
  54.9 4.6 %copy-start.10 = (bf16[32,1,2,5,5,8]{0,5,2,4,3,1:T(8,128)(2,1)S(1)}, bf16[32,1,2,5,5,8]{0,5,2,4,3,1:T(8,128)(2,1)}, u32[]{:S(2)}) copy-start(bf16[32,1,2,5,5,8]{0,5,2,4,3,1:T(8,128)(2,1)} %get-tuple-element.16) | copy-start | bytes 76804
  57.2 25.3 %collective-permute-start.6 = (bf16[4,2,5,4,32,128]{5,4,3,2,1,0:T(8,128)(2,1)}, bf16[4,2,5,4,32,128]{5,4,3,2,1,0:T(8,128)(2,1)}, u32[]{:S(2)}, u32[]{:S(2)}) collective-permute-start(bf16[4,2,5,4,32,128]{5,4,3,2,1,0:T(8,128)(2,1)} %pad_maximum_fusion.1), channel_id=1, source_target_pairs={{0,1},{1,0},{2,3},{3,2},{4,5},{5,4},{6,7},{7,6},{8,9},{9,8},{10,11... | collective-permute-start | bytes 3932168 | tf_op jit(solution)/shard_map/ppermute | solution.py:224
  66.2 10.7 %copy-start.2 = (bf16[1024,4,32]{0,2,1:T(8,128)(2,1)S(1)}, bf16[1024,4,32]{0,2,1:T(8,128)(2,1)}, u32[]{:S(2)}) copy-start(bf16[1024,4,32]{0,2,1:T(8,128)(2,1)} %constant.96.clone) | copy-start | bytes 786436
  78.3 3.0 copy-start.6
  78.4 4.4 %copy-start.4 = (bf16[2,5,4,32,128]{4,3,2,1,0:T(8,128)(2,1)S(1)}, bf16[2,5,4,32,128]{4,3,2,1,0:T(8,128)(2,1)}, u32[]{:S(2)}) copy-start(bf16[2,5,4,32,128]{4,3,2,1,0:T(8,128)(2,1)} %copy-done.3) | copy-start | bytes 983044
  81.4 60.2 %collective-permute-start.8 = (bf16[2,3,8,32,128]{4,3,2,1,0:T(8,128)(2,1)S(1)}, bf16[2,3,8,32,128]{4,3,2,1,0:T(8,128)(2,1)S(1)}, u32[]{:S(2)}, u32[]{:S(2)}) collective-permute-start(bf16[2,3,8,32,128]{4,3,2,1,0:T(8,128)(2,1)S(1)} %copy-done.6), channel_id=1, source_target_pairs={{0,8},{4,12},{8,0},{12,4},{1,9},{5,13},{9,1},{13,5},{2,10},{6,14},... | collective-permute-start | bytes 1179656 | tf_op jit(solution)/shard_map/ppermute | solution.py:224
  82.5 18.0 %collective-permute-start.15 = (bf16[2,3,8,32,128]{4,3,2,1,0:T(8,128)(2,1)}, bf16[2,3,8,32,128]{4,3,2,1,0:T(8,128)(2,1)S(1)}, u32[]{:S(2)}, u32[]{:S(2)}) collective-permute-start(bf16[2,3,8,32,128]{4,3,2,1,0:T(8,128)(2,1)} %collective-permute-done.14.refs_2_), channel_id=1, source_target_pairs={{0,4},{4,0},{8,12},{12,8},{1,5},{5,1},{9,13},{13,9},{2,6},{6,2},{1... | collective-permute-start | bytes 1179656 | tf_op jit(solution)/shard_map/ppermute | solution.py:224
  84.3 3.6 %copy-start.5 = (bf16[2,3,8,32,128]{4,3,2,1,0:T(8,128)(2,1)S(1)}, bf16[2,3,8,32,128]{4,3,2,1,0:T(8,128)(2,1)}, u32[]{:S(2)}) copy-start(bf16[2,3,8,32,128]{4,3,2,1,0:T(8,128)(2,1)} %get-tuple-element.11.refs_0_) | copy-start | bytes 1179652
  86.1 97.9 %collective-permute-start.7 = (bf16[2,3,8,32,128]{4,3,2,1,0:T(8,128)(2,1)S(1)}, bf16[2,3,8,32,128]{4,3,2,1,0:T(8,128)(2,1)S(1)}, u32[]{:S(2)}, u32[]{:S(2)}) collective-permute-start(bf16[2,3,8,32,128]{4,3,2,1,0:T(8,128)(2,1)S(1)} %copy-done.6), channel_id=1, source_target_pairs={{0,4},{4,0},{8,12},{12,8},{1,5},{5,1},{9,13},{13,9},{2,6},{6,2},{1... | collective-permute-start | bytes 1179656 | tf_op jit(solution)/shard_map/ppermute | solution.py:224
  87.9 55.1 %collective-permute-start.1 = (bf16[2,3,8,32,128]{4,3,2,1,0:T(8,128)(2,1)S(1)}, bf16[2,3,8,32,128]{4,3,2,1,0:T(8,128)(2,1)S(1)}, u32[]{:S(2)}, u32[]{:S(2)}) collective-permute-start(bf16[2,3,8,32,128]{4,3,2,1,0:T(8,128)(2,1)S(1)} %copy-done.5), channel_id=1, source_target_pairs={{0,8},{4,12},{8,0},{12,4},{1,9},{5,13},{9,1},{13,5},{2,10},{6,14},... | collective-permute-start | bytes 1179656 | tf_op jit(solution)/shard_map/ppermute | solution.py:224
  100.5 43.2 %collective-permute-start.12 = (bf16[2,3,8,32,128]{4,3,2,1,0:T(8,128)(2,1)}, bf16[2,3,8,32,128]{4,3,2,1,0:T(8,128)(2,1)S(1)}, u32[]{:S(2)}, u32[]{:S(2)}) collective-permute-start(bf16[2,3,8,32,128]{4,3,2,1,0:T(8,128)(2,1)} %collective-permute-done.11.refs_2_), channel_id=1, source_target_pairs={{0,4},{4,0},{8,12},{12,8},{1,5},{5,1},{9,13},{13,9},{2,6},{6,2},{1... | collective-permute-start | bytes 1179656 | tf_op jit(solution)/shard_map/ppermute | solution.py:224
  140.9 83.5 %collective-permute-start = (bf16[2,3,8,32,128]{4,3,2,1,0:T(8,128)(2,1)S(1)}, bf16[2,3,8,32,128]{4,3,2,1,0:T(8,128)(2,1)S(1)}, u32[]{:S(2)}, u32[]{:S(2)}) collective-permute-start(bf16[2,3,8,32,128]{4,3,2,1,0:T(8,128)(2,1)S(1)} %copy-done.5), channel_id=1, source_target_pairs={{0,4},{4,0},{8,12},{12,8},{1,5},{5,1},{9,13},{13,9},{2,6},{6,2},{1... | collective-permute-start | bytes 1179656 | tf_op jit(solution)/shard_map/ppermute | solution.py:224
  141.6 42.4 %copy-start.13 = (bf16[2,3,8,32,128]{4,3,2,1,0:T(8,128)(2,1)}, bf16[2,3,8,32,128]{4,3,2,1,0:T(8,128)(2,1)S(1)}, u32[]{:S(2)}) copy-start(bf16[2,3,8,32,128]{4,3,2,1,0:T(8,128)(2,1)S(1)} %collective-permute-done.8.refs_2_) | copy-start | bytes 1179652
  141.6 42.4 %collective-permute-start.9 = (bf16[2,3,8,32,128]{4,3,2,1,0:T(8,128)(2,1)S(1)}, bf16[2,3,8,32,128]{4,3,2,1,0:T(8,128)(2,1)}, u32[]{:S(2)}, u32[]{:S(2)}) collective-permute-start(bf16[2,3,8,32,128]{4,3,2,1,0:T(8,128)(2,1)S(1)} %collective-permute-done.8.refs_2_), channel_id=1, source_target_pairs={{0,4},{4,0},{8,12},{12,8},{1,5},{5,1},{9,13},{13,9},{2,6},{6,2},{1... | collective-permute-start | bytes 1179656 | tf_op jit(solution)/shard_map/ppermute | solution.py:224
  143.0 41.0 %copy-start.14 = (bf16[2,3,8,32,128]{4,3,2,1,0:T(8,128)(2,1)}, bf16[2,3,8,32,128]{4,3,2,1,0:T(8,128)(2,1)S(1)}, u32[]{:S(2)}) copy-start(bf16[2,3,8,32,128]{4,3,2,1,0:T(8,128)(2,1)S(1)} %collective-permute-done.1.refs_2_) | copy-start | bytes 1179652
  143.0 81.4 %collective-permute-start.2 = (bf16[2,3,8,32,128]{4,3,2,1,0:T(8,128)(2,1)S(1)}, bf16[2,3,8,32,128]{4,3,2,1,0:T(8,128)(2,1)S(1)}, u32[]{:S(2)}, u32[]{:S(2)}) collective-permute-start(bf16[2,3,8,32,128]{4,3,2,1,0:T(8,128)(2,1)S(1)} %collective-permute-done.1.refs_2_), channel_id=1, source_target_pairs={{0,4},{4,0},{8,12},{12,8},{1,5},{5,1},{9,13},{13,9},{2,6},{6,2},{1... | collective-permute-start | bytes 1179656 | tf_op jit(solution)/shard_map/ppermute | solution.py:224
  267.5 3.2 %collective-permute-start.16 = (bf16[2,2,2,5,2,2,32,128]{7,6,1,3,2,4,5,0:T(8,128)(2,1)S(1)}, bf16[2,2,2,5,2,2,32,128]{7,6,1,3,2,4,5,0:T(8,128)(2,1)}, u32[]{:S(2)}, u32[]{:S(2)}) collective-permute-start(bf16[2,2,2,5,2,2,32,128]{7,6,1,3,2,4,5,0:T(8,128)(2,1)S(1)} %bitcast.78), channel_id=1, source_target_pairs={{0,1},{1,0},{2,3},{3,2},{4,5},{5,4},{6,7},{7,6},{8,9},{9,8},{10,11... | collective-permute-start | bytes 3932168 | tf_op jit(solution)/shard_map/ppermute | solution.py:224
  272.7 16.8 %collective-permute-start.17 = (bf16[2,2,5,2,2,32,128]{6,5,0,2,1,3,4:T(8,128)(2,1)S(1)}, bf16[2,2,5,2,2,32,128]{6,5,0,2,1,3,4:T(8,128)(2,1)S(1)}, u32[]{:S(2)}, u32[]{:S(2)}) collective-permute-start(bf16[2,2,5,2,2,32,128]{6,5,0,2,1,3,4:T(8,128)(2,1)S(1)} %dynamic-slice_bitcast_fusion), channel_id=1, source_target_pairs={{0,2},{1,3},{2,0},{3,1},{4,6},{5,7},{6,4},{7,5},{8,10},{9,11},{10,... | collective-permute-start | bytes 1966088 | tf_op jit(solution)/shard_map/ppermute | solution.py:224
  289.5 27.1 %copy-start.1 = (bf16[2,5,8,32,128]{4,3,2,1,0:T(8,128)(2,1)S(1)}, bf16[2,5,8,32,128]{4,3,2,1,0:T(8,128)(2,1)}, u32[]{:S(2)}) copy-start(bf16[2,5,8,32,128]{4,3,2,1,0:T(8,128)(2,1)} %param.10) | copy-start | bytes 1966084
  289.8 26.1 %copy-start.7 = (f32[2,5,2,32,128]{4,3,2,1,0:T(8,128)S(1)}, f32[2,5,2,32,128]{4,3,2,1,0:T(8,128)}, u32[]{:S(2)}) copy-start(f32[2,5,2,32,128]{4,3,2,1,0:T(8,128)} %param.15) | copy-start | bytes 983044
  289.8 9.0 %collective-permute-start.18 = (bf16[2,2,5,2,32,128]{5,4,0,2,1,3:T(8,128)(2,1)S(1)}, bf16[2,2,5,2,32,128]{5,4,0,2,1,3:T(8,128)(2,1)S(1)}, u32[]{:S(2)}, u32[]{:S(2)}) collective-permute-start(bf16[2,2,5,2,32,128]{5,4,0,2,1,3:T(8,128)(2,1)S(1)} %slice_bitcast_fusion), channel_id=1, source_target_pairs={{0,4},{4,0},{8,12},{12,8},{1,5},{5,1},{9,13},{13,9},{2,6},{6,2},{1... | collective-permute-start | bytes 983048 | tf_op jit(solution)/shard_map/ppermute | solution.py:224
  298.9 16.9 %collective-permute-start.19 = (bf16[2,2,5,32,128]{4,3,0,2,1:T(8,128)(2,1)S(1)}, bf16[2,2,5,32,128]{4,3,0,2,1:T(8,128)(2,1)S(1)}, u32[]{:S(2)}, u32[]{:S(2)}) collective-permute-start(bf16[2,2,5,32,128]{4,3,0,2,1:T(8,128)(2,1)S(1)} %slice_bitcast_fusion.2), channel_id=1, source_target_pairs={{0,8},{4,12},{8,0},{12,4},{1,9},{5,13},{9,1},{13,5},{2,10},{6,14},... | collective-permute-start | bytes 491528 | tf_op jit(solution)/shard_map/ppermute | solution.py:224
  (8 other events, 11.0 us)

commit v2 on v1

v2 whole, which is shorter than its diff:
```python
import functools
import math

import jax
import jax.numpy as jnp
import numpy as np
from jax import lax
from jax.experimental import pallas as pl
from jax.experimental.pallas import tpu as pltpu
from jax.sharding import PartitionSpec as P

K = 5
NZ = 8
BF = jnp.bfloat16
F32 = jnp.float32
HALF = math.sqrt(0.5)


def table(count_in, count_out, length, sign):
    phase = (np.arange(count_in)[:, None] * np.arange(count_out)[None, :] % length).astype(
        np.float32
    ) * np.float32(2.0 * math.pi / length)
    scale = 1.0 / math.sqrt(length)
    cosine = np.cos(phase) * np.float32(scale)
    sine = np.sin(phase) * np.float32(sign * scale)
    return np.stack([np.stack([cosine, -sine]), np.stack([sine, cosine])]).astype(BF)


def add(a, b):
    return (a[0] + b[0], a[1] + b[1])


def sub(a, b):
    return (a[0] - b[0], a[1] - b[1])


def add_turned(a, b, sign):
    return (a[0] - b[1], a[1] + b[0]) if sign > 0 else (a[0] + b[1], a[1] - b[0])


def four(v, sign):
    a, b = add(v[0], v[2]), sub(v[0], v[2])
    c, d = add(v[1], v[3]), sub(v[1], v[3])
    return [add(a, c), add_turned(b, d, sign), sub(a, c), add_turned(b, d, -sign)]


def eight(re, im, sign):
    v = list(zip(re, im))
    e, o = four(v[0::2], sign), four(v[1::2], sign)
    h = jnp.asarray(HALF, re[0].dtype)
    once = add_turned(o[1], o[1], sign)
    once = (once[0] * h, once[1] * h)
    thrice = add_turned((-o[3][0], -o[3][1]), o[3], sign)
    thrice = (thrice[0] * h, thrice[1] * h)
    out = [None] * 8
    for q, t in ((0, o[0]), (1, once), (3, thrice)):
        out[q], out[q + 4] = add(e[q], t), sub(e[q], t)
    out[2], out[6] = add_turned(e[2], o[2], sign), add_turned(e[2], o[2], -sign)
    return [x[0] for x in out], [x[1] for x in out]


def tree(terms):
    while len(terms) > 1:
        terms = [
            terms[i] + terms[i + 1] if i + 1 < len(terms) else terms[i]
            for i in range(0, len(terms), 2)
        ]
    return terms[0]


def coils_kernel(width, pieces, images, first, last, where, *refs):
    maps, refs = refs[:pieces], refs[pieces:]
    shared, refs = refs[:images], refs[images:]
    weights_hbm, ty, tx, tix, tiy = refs[:5]
    rest = list(refs[5:])
    acc_in = None if first else rest.pop(0)
    outs, rest = (rest[:2], rest[2:]) if last else (rest[:1], rest[1:])
    image, rows, spec, mid, product, weights, sems, image_sems = rest[:8]
    acc = rest[8] if last else outs[0]
    nx, ny = tix.shape[1] // 2, tiy.shape[1] // 2
    tiles = width // 16
    step = pl.program_id(0)
    me = where[1]
    fetch = [
        pltpu.make_async_copy(weights_hbm.at[q], weights.at[q], sems.at[q]) for q in range(NZ)
    ]
    resume = None if first else pltpu.make_async_copy(acc_in, acc, sems.at[NZ])
    groups = image.shape[0]
    arrive = []
    for b, ref in enumerate(shared):
        for x in range(ref.shape[0]):
            slot = ((x ^ (me // 2)) * 2 + (b ^ (me % 2))) if groups > 1 else 0
            arrive.append(
                pltpu.make_async_copy(ref.at[x], image.at[slot], image_sems.at[len(arrive)])
            )

    @pl.when(step == 0)
    def _():
        for copy in arrive:
            copy.start()
        for copy in fetch:
            copy.start()
        if first:
            acc[...] = jnp.zeros_like(acc)
        else:
            resume.start()
        for copy in arrive:
            copy.wait()

    def image_of(part, j, z):
        group, plane = z // (NZ // groups), z % (NZ // groups)
        return jnp.concatenate(
            [image[group, r, part, j, plane] for r in range(image.shape[1])], axis=0
        )

    def maps_of(part, z):
        return jnp.concatenate([m[part, 0, z] for m in maps], axis=0)

    def forward(j, _):
        for z in range(NZ):
            mr, mi = maps_of(0, z), maps_of(1, z)
            ir, ii = image_of(0, j, z), image_of(1, j, z)
            product[j, z * nx : (z + 1) * nx] = jnp.concatenate(
                [mr * ir - mi * ii, mr * ii + mi * ir], axis=1
            )
        turned = jnp.dot(product[j], ty[...], preferred_element_type=F32).astype(BF)
        for z in range(NZ):
            rows[j, z] = turned[z * nx : (z + 1) * nx].T
        for t in range(tiles):
            a, b = pl.ds(t * 16, 16), pl.ds(width + t * 16, 16)
            re, im = eight(
                [rows[j, z, a].astype(F32) for z in range(NZ)],
                [rows[j, z, b].astype(F32) for z in range(NZ)],
                -1,
            )
            for q in range(NZ):
                mid[j, pl.ds(q * width + t * 16, 16)] = jnp.concatenate(
                    [re[q], im[q]], axis=1
                ).astype(BF)
        spec[j] = jnp.dot(mid[j], tx[...], preferred_element_type=F32).astype(BF)
        return 0

    for j in range(K):
        forward(j, 0)

    half = tx.shape[1] // 2

    def apply(q, t):
        a = pl.ds(t * 16, 16)
        at = pl.ds(pl.multiple_of(q * width + t * 16, 16), 16)
        sr = [spec[j, at, :half] for j in range(K)]
        si = [spec[j, at, half:] for j in range(K)]
        for k in range(K):
            re, im = [], []
            for j in range(K):
                kr, ki = weights[q, k, j, 0, a], weights[q, k, j, 1, a]
                re.append(kr * sr[j] - ki * si[j])
                im.append(kr * si[j] + ki * sr[j])
            spec[k, at, :half] = tree(re)
            spec[k, at, half:] = tree(im)

    def apply_all(q, _):
        @pl.when(step == 0)
        def _():
            pltpu.make_async_copy(weights_hbm.at[q], weights.at[q], sems.at[q]).wait()

        for t in range(tiles):
            apply(q, t)
        return 0

    lax.fori_loop(0, NZ, apply_all, 0)
    if not first:

        @pl.when(step == 0)
        def _():
            resume.wait()


    def inverse(k, _):
        mid[k] = jnp.dot(spec[k], tix[...], preferred_element_type=F32).astype(BF)
        for t in range(tiles):
            a, b = pl.ds(t * 16, 16), pl.ds(width + t * 16, 16)
            re, im = eight(
                [mid[k, pl.ds(q * width + t * 16, 16), :nx].astype(F32) for q in range(NZ)],
                [mid[k, pl.ds(q * width + t * 16, 16), nx:].astype(F32) for q in range(NZ)],
                1,
            )
            for z in range(NZ):
                rows[k, z, a] = re[z].astype(BF)
                rows[k, z, b] = im[z].astype(BF)
        turned = jnp.concatenate([rows[k, z].T for z in range(NZ)], axis=0)
        backs = jnp.dot(turned, tiy[...], preferred_element_type=F32)
        for z in range(NZ):
            back = backs[z * nx : (z + 1) * nx]
            br, bi = back[:, :ny], back[:, ny:]
            mr, mi = maps_of(0, z).astype(F32), maps_of(1, z).astype(F32)
            acc[z, 0, k] += mr * br + mi * bi
            acc[z, 1, k] += mr * bi - mi * br
        return 0

    for k in range(K):
        inverse(k, 0)
    if last:

        @pl.when(step == pl.num_programs(0) - 1)
        def _():
            for x in range(2):
                for z in range(NZ // 4):
                    base = (x ^ (me // 2)) * (NZ // 2) + z
                    for c in range(2):
                        outs[c][x, z] = acc[base + (c ^ (me % 2)) * (NZ // 4)].astype(BF)


def coils(maps, images, weights, tables, acc, last, where):
    count = maps[0].shape[1]
    spec_width = tables[1].shape[2]
    width = tables[0].shape[2] // 2
    nx, ny = tables[2].shape[2] // 2, tables[3].shape[2] // 2
    anywhere = pl.BlockSpec(memory_space=pl.ANY)
    shape = (NZ, 2, K, nx, ny)
    half = (2, NZ // 4, 2, K, nx, ny)
    out = [jax.ShapeDtypeStruct(half, BF)] * 2 if last else jax.ShapeDtypeStruct(shape, F32)
    block = lambda dims: pl.BlockSpec(
        dims, lambda c, w: (0,) * len(dims), pipeline_mode=pl.Buffered(buffer_count=1)
    )
    args = [*maps, *images, weights, *tables]
    specs = [pl.BlockSpec((2, 1) + m.shape[2:], lambda c, w: (0, c, 0, 0, 0)) for m in maps]
    specs += [anywhere] * (len(images) + 1)
    specs += [
        pl.BlockSpec(
            (None,) + t.shape[1:],
            lambda c, w: (w[0], 0, 0),
            pipeline_mode=pl.Buffered(buffer_count=1),
        )
        for t in tables
    ]
    if acc is not None:
        args.append(acc)
        specs.append(anywhere)
    groups = sum(i.shape[0] for i in images)
    scratch = [
        pltpu.VMEM((groups,) + images[0].shape[1:], BF),
        pltpu.VMEM((K, NZ, 2 * width, nx), BF),
        pltpu.VMEM((K, NZ * width, spec_width), BF),
        pltpu.VMEM((K, NZ * width, 2 * nx), BF),
        pltpu.VMEM((K, NZ * nx, 2 * ny), BF),
        pltpu.VMEM(weights.shape, BF),
        pltpu.SemaphoreType.DMA((NZ + 1,)),
        pltpu.SemaphoreType.DMA((groups,)),
    ]
    if last:
        scratch.append(pltpu.VMEM(shape, F32))
    planes = count * K * NZ
    return pl.pallas_call(
        functools.partial(coils_kernel, width, len(maps), len(images), acc is None, last),
        grid_spec=pltpu.PrefetchScalarGridSpec(
            num_scalar_prefetch=1,
            grid=(count,),
            in_specs=specs,
            out_specs=[block(half)] * 2 if last else block(shape),
            scratch_shapes=scratch,
        ),
        out_shape=out,
        compiler_params=pltpu.CompilerParams(vmem_limit_bytes=60 * 2**20),
        cost_estimate=pl.CostEstimate(
            flops=planes * width * 4 * 2 * 200_000, bytes_accessed=30_000_000, transcendentals=0
        ),
    )(where, *args)


def kernel_weights(sampled, basis_products, point_spread, pad):
    scale = float(table(1, 1, NZ, 1)[0, 0, 0, 0].astype(np.float32)) ** 2
    picked = basis_products[:, :, :, :, None] * (
        sampled.astype(F32)[:, None, None, None, :] * scale
    )
    real, imag = picked[:, 0], picked[:, 1]
    pairs = jnp.stack([jnp.stack([real, -imag], 1), jnp.stack([imag, real], 1)], 1)
    spread = point_spread.astype(BF)
    if pad:
        spread = jnp.pad(spread, ((0, 0), (0, 0), (0, pad), (0, 0)))
    return jnp.einsum(
        "gpikjq,givu->qkjpvu", pairs.astype(BF), spread, preferred_element_type=F32
    ).astype(BF)


def swap(value, axis, bit):
    size = lax.axis_size(axis)
    return lax.ppermute(value, axis, [(i, i ^ bit) for i in range(size)])


def body(basis_image, coil_maps, point_spread, basis_products, sampled, adjoint_data):
    dom, here = lax.axis_size("dom"), lax.axis_index("dom")
    coil, me = lax.axis_size("coil"), lax.axis_index("coil")
    rows, ny = basis_image.shape[3], basis_image.shape[4]
    nx = rows * dom
    own = point_spread.shape[2]
    width = max(64, own)
    butterfly = dom == 4 and rows % 16 == 0

    forward, inverse = table(ny, 2 * ny, 2 * ny, -1), table(2 * ny, ny, 2 * ny, 1)
    extra = ((0, 0), (0, 0), (0, 0), (0, width - own))
    forward = np.pad(forward.transpose(1, 2, 0, 3), extra)
    inverse = np.pad(inverse.transpose(1, 0, 3, 2), extra).transpose(0, 3, 1, 2)
    ty = np.stack([forward[..., d * own : d * own + width] for d in range(dom)])
    tiy = np.stack([inverse[:, d * own : d * own + width] for d in range(dom)])
    forward, inverse = table(nx, 2 * nx, 2 * nx, -1), table(2 * nx, nx, 2 * nx, 1)
    tx = forward.transpose(1, 2, 0, 3).reshape(2, dom, rows, 4 * nx)
    tix = inverse.transpose(1, 2, 0, 3).reshape(4 * nx, 2, dom, rows)
    orders = [[d ^ r for r in range(dom)] if butterfly else range(dom) for d in range(dom)]
    if not butterfly:
        orders = orders[:1]
    tx = np.stack([tx[:, list(o)] for o in orders])
    tix = np.stack([tix[:, :, list(o)] for o in orders])
    if not butterfly:
        ty = lax.dynamic_slice_in_dim(jnp.asarray(ty), here, 1, 0)
        tiy = lax.dynamic_slice_in_dim(jnp.asarray(tiy), here, 1, 0)
    tables = [
        jnp.asarray(ty).reshape(-1, 2 * ny, 2 * width),
        jnp.asarray(tx).reshape(-1, 2 * nx, 4 * nx),
        jnp.asarray(tix).reshape(-1, 4 * nx, 2 * nx),
        jnp.asarray(tiy).reshape(-1, 2 * width, 2 * ny),
    ]
    where = jnp.stack([here if butterfly else 0 * here, me]).astype(jnp.int32)
    weights = kernel_weights(sampled, basis_products, point_spread, width - own)
    count = coil_maps.shape[1]

    if butterfly:
        sizes = CHUNKS if sum(CHUNKS) == count else (count,)
        starts = [sum(sizes[:m]) for m in range(len(sizes))]
        parts = [
            lax.slice_in_dim(coil_maps, a, a + n, axis=1) for a, n in zip(starts, sizes)
        ] + [None, None]

        def begin(part):
            return None if part is None else (swap(part, "dom", 1), swap(part, "dom", 2))

        mine = lax.dynamic_slice_in_dim(basis_image, me * (NZ // coil), NZ // coil, 2)
        mine = [mine] + [swap(mine, "dom", r) for r in (1, 2, 3)]
        first = begin(parts[0])
        mine, parts[1] = lax.optimization_barrier((mine, parts[1]))
        mine = jnp.stack(mine)
        second = begin(parts[1])
        there = swap(mine, "coil", 2)
        third = swap(first[1], "dom", 1)
        there, weights, third, first, second = lax.optimization_barrier(
            (there, weights, third, first, second)
        )
        both = jnp.stack([mine, there])
        images = [both, swap(both, "coil", 1)]
        total = None
        for m in range(len(sizes)):
            maps = [parts[m], *first, third]
            images, maps, second, parts[m + 2], total = lax.optimization_barrier(
                (images, maps, second, parts[m + 2], total)
            )
            if second is not None:
                third = swap(second[1], "dom", 1)
            first, second = second, begin(parts[m + 2])
            total = coils(maps, images, weights, tables, total, m == len(sizes) - 1, where)
    else:
        images = [lax.all_gather(basis_image, "dom", axis=3, tiled=True)[None, None]]
        maps = [lax.all_gather(coil_maps, "dom", axis=3, tiled=True)]
        total = coils(maps, images, weights, tables, None, True, where)

    def plus(a, b):
        return a.astype(F32) + b.astype(F32)

    keep, send = total
    total = plus(keep, swap(send, "coil", 1)).astype(BF)
    total = plus(total[0], swap(total[1], "coil", 2)).astype(BF)
    if not butterfly:
        total = lax.psum_scatter(total, "dom", scatter_dimension=3, tiled=True)
        return total.astype(F32).transpose(1, 2, 0, 3, 4) - adjoint_data
    total = total.reshape(NZ // coil, 2, K, 2, 2, rows, ny)
    total = plus(total[:, :, :, :, 0], swap(total[:, :, :, :, 1], "dom", 1)).astype(BF)
    total = plus(total[:, :, :, 0], swap(total[:, :, :, 1], "dom", 2))
    return total.transpose(1, 2, 0, 3, 4) - adjoint_data


CHUNKS = (2, 3, 3, 4)


def solution(mesh):
    placed = (
        P(None, None, "slab", "dom", None),
        P(None, "coil", "slab", "dom", None),
        P(None, None, "dom", None),
        P(),
        P(),
        P(None, None, ("slab", "coil"), "dom", None),
    )
    return jax.shard_map(
        body,
        mesh=mesh,
        in_specs=placed,
        out_specs=P(None, None, ("slab", "coil"), "dom", None),
        check_vma=False,
    )
```

time: 317 us -> 229 us (0.72)
  Pallas kernels: 156 us -> 116 us
  waiting for transfers between devices: 78.1 us -> 52.5 us
  local copies, waits for them, and re-layouts: 27.7 us -> 17.9 us
  other arithmetic: 12.9 us -> 6.58 us
  starting transfers between devices: 34.9 us -> 28.6 us
    pallas_call x4, Pallas kernels: 156 us -> 116 us  [coils(): pl.pallas_call(functools.partial(coils_kernel, width, len(maps), len(imag...]
    ppermute x20 -> x21, waiting for transfers between devices: 78.1 us -> 52.5 us  [swap(): return lax.ppermute(value, axis, [(i, i ^ bit) for i in range(size)])]
    ppermute x20 -> x21, starting transfers between devices: 34.9 us -> 28.6 us  [swap(): return lax.ppermute(value, axis, [(i, i ^ bit) for i in range(size)])]
    dynamic_slice x5 -> x1, local copies, waits for them, and re-layouts: 5.18 us -> 0.01 us  [body(): lax.dynamic_slice_in_dim(basis_image, me * (NZ // coil), NZ // coil, 2)]
  transfers between devices with their start and end apart: 20 -> 21, of which waited for: 7 -> 10; matrix products, arithmetic and copies ran while one was open for 12% -> 11% of each run, Pallas kernels for 37% -> 35%
where the time goes in v2:
time: 229 us
  Pallas kernels  116 us (51%)
  waiting for transfers between devices  52.5 us (23%)
  starting transfers between devices  28.6 us (12%)
  local copies, waits for them, and re-layouts  17.9 us (8%)
  matrix products  6.7 us (3%)
  other arithmetic  6.58 us (3%)
    pallas_call x4, Pallas kernels, coils(): pl.pallas_call(functools.partial(coils_kernel, width, len(maps), len(imag...  116 us
    ppermute x21, waiting for transfers between devices, swap(): return lax.ppermute(value, axis, [(i, i ^ bit) for i in range(size)])  52.5 us
    ppermute x21, starting transfers between devices, swap(): return lax.ppermute(value, axis, [(i, i ^ bit) for i in range(size)])  28.6 us
    dot_general x1, local copies, waits for them, and re-layouts, kernel_weights(): jnp.einsum('gpikjq,givu->qkjpvu', pairs.astype(BF), spread, preferred_ele...  10.7 us
    dot_general x1, matrix products, kernel_weights(): jnp.einsum('gpikjq,givu->qkjpvu', pairs.astype(BF), spread, preferred_ele...  6.7 us
  transfers between devices with their start and end apart: 21, of which 10 were waited for; matrix products, arithmetic and copies ran while one was open for 11% of the time, Pallas kernels for 35%

profile of v2, /device:TPU:0, one launch (start us, length us, event | category | flops | bytes accessed | tf_op | source)
XLA Modules:
  0.0 228.7 jit_solution(3391751690175336749)
XLA Ops:
  0.0 1.1 copy-done
  1.1 3.1 %collective-permute-start = (bf16[2,5,2,32,128]{4,3,2,1,0:T(8,128)(2,1)S(1)}, bf16[2,5,2,32,128]{4,3,2,1,0:T(8,128)(2,1)S(1)}, u32[]{:S(2)}, u32[]{:S(2)}) collective-permute-start(bf16[2,5,2,32,128]{4,3,2,1,0:T(8,128)(2,1)S(1)} %constant_dynamic-slice_fusion), channel_id=1, source_target_pairs={{0,4},{4,0},{8,12},{12,8},{1,5},{5,1},{9,13},{13,9},{2,6},{6,2},{1... | collective-permute-start | bytes 491528 | tf_op jit(solution)/shard_map/ppermute | solution.py:288
  4.2 2.6 %collective-permute-start.1 = (bf16[2,5,2,32,128]{4,3,2,1,0:T(8,128)(2,1)S(1)}, bf16[2,5,2,32,128]{4,3,2,1,0:T(8,128)(2,1)S(1)}, u32[]{:S(2)}, u32[]{:S(2)}) collective-permute-start(bf16[2,5,2,32,128]{4,3,2,1,0:T(8,128)(2,1)S(1)} %constant_dynamic-slice_fusion), channel_id=1, source_target_pairs={{0,8},{4,12},{8,0},{12,4},{1,9},{5,13},{9,1},{13,5},{2,10},{6,14},... | collective-permute-start | bytes 491528 | tf_op jit(solution)/shard_map/ppermute | solution.py:288
  6.8 1.0 slice.39.refs_0_
  7.8 2.0 collective-permute-start.4
  9.7 2.5 %collective-permute-start.6 = (bf16[2,2,8,32,128]{4,3,2,1,0:T(8,128)(2,1)S(1)}, bf16[2,2,8,32,128]{4,3,2,1,0:T(8,128)(2,1)S(1)}, u32[]{:S(2)}, u32[]{:S(2)}) collective-permute-start(bf16[2,2,8,32,128]{4,3,2,1,0:T(8,128)(2,1)S(1)} %slice.39.refs_0_), channel_id=1, source_target_pairs={{0,4},{4,0},{8,12},{12,8},{1,5},{5,1},{9,13},{13,9},{2,6},{6,2},{1... | collective-permute-start | bytes 786440 | tf_op jit(solution)/shard_map/ppermute | solution.py:288
  12.2 1.2 fusion.10
  13.4 2.8 %convert_bitcast_fusion = bf16[32,2,64,256,1,1,1]{3,2,1,0,6,5,4:T(8,128)(2,1)S(1)} fusion(f32[32,2,64,256]{3,2,1,0:T(8,128)} %param.12), kind=kLoop, calls=%fused_computation.5 | loop fusion | flops 1048576 | bytes 6291456 | tf_op jit(solution)/shard_map/convert_element_type | solution.py:278
  16.3 8.6 %collective-permute-done.1 = bf16[2,5,2,32,128]{4,3,2,1,0:T(8,128)(2,1)S(1)} collective-permute-done((bf16[2,5,2,32,128]{4,3,2,1,0:T(8,128)(2,1)S(1)}, bf16[2,5,2,32,128]{4,3,2,1,0:T(8,128)(2,1)S(1)}, u32[]{:S(2)}, u32[]{:S(2)}) %collective-permute-start.1) | collective-permute-done | bytes 163872 | tf_op jit(solution)/shard_map/ppermute | solution.py:288
  25.0 1.6 collective-permute-start.3
  26.6 4.1 %collective-permute-start.7 = (bf16[2,3,8,32,128]{4,3,2,1,0:T(8,128)(2,1)S(1)}, bf16[2,3,8,32,128]{4,3,2,1,0:T(8,128)(2,1)S(1)}, u32[]{:S(2)}, u32[]{:S(2)}) collective-permute-start(bf16[2,3,8,32,128]{4,3,2,1,0:T(8,128)(2,1)S(1)} %get-tuple-element.80.refs_0_), channel_id=1, source_target_pairs={{0,4},{4,0},{8,12},{12,8},{1,5},{5,1},{9,13},{13,9},{2,6},{6,2},{1... | collective-permute-start | bytes 1179656 | tf_op jit(solution)/shard_map/ppermute | solution.py:288
  31.7 2.4 %collective-permute-done.4.refs_2_ = bf16[2,2,8,32,128]{4,3,2,1,0:T(8,128)(2,1)S(1)} collective-permute-done((bf16[2,2,8,32,128]{4,3,2,1,0:T(8,128)(2,1)S(1)}, bf16[2,2,8,32,128]{4,3,2,1,0:T(8,128)(2,1)S(1)}, u32[]{:S(2)}, u32[]{:S(2)}) %collective-permute-start.4) | collective-permute-done | bytes 262176 | tf_op jit(solution)/shard_map/ppermute | solution.py:288
  34.1 6.7 %convolution_bitcast_fusion = bf16[2,5,5,8,64,256]{5,3,4,2,1,0:T(8,128)(2,1)} fusion(bf16[32,2,64,256,1,1,1]{3,2,1,0,6,5,4:T(8,128)(2,1)S(1)} %convert_bitcast_fusion, bf16[32,1,2,5,5,8]{0,5,2,4,3,1:T(8,128)(2,1)S(1)} %get-tuple-element.112, bf16[32,1,2,5,5,8]{0,5,2,4,3,1:T(8,128)(2,1)S(1)} %get-tuple-element.111), kind=kOutput, calls=%fused_computation.1 | convolution fusion | flops 838963200 | bytes 15255552 | tf_op jit(solution)/shard_map/gpikjq,givu->qkjpvu/dot_general | solution.py:281
  40.8 10.7 %copy.31 = bf16[2,5,5,8,64,256]{5,4,0,2,1,3:T(8,128)(2,1)} copy(bf16[2,5,5,8,64,256]{5,3,4,2,1,0:T(8,128)(2,1)} %convolution_bitcast_fusion) | data formatting | bytes 26214400 | tf_op jit(solution)/shard_map/gpikjq,givu->qkjpvu/dot_general | solution.py:281
  51.5 3.6 %collective-permute-done.5.refs_3_ = bf16[2,2,8,32,128]{4,3,2,1,0:T(8,128)(2,1)S(1)} collective-permute-done((bf16[2,2,8,32,128]{4,3,2,1,0:T(8,128)(2,1)S(1)}, bf16[2,2,8,32,128]{4,3,2,1,0:T(8,128)(2,1)S(1)}, u32[]{:S(2)}, u32[]{:S(2)}) %collective-permute-start.5) | collective-permute-done | bytes 262176 | tf_op jit(solution)/shard_map/ppermute | solution.py:288
  56.0 1.5 slice.41.refs_0_
  58.2 1.0 collective-permute-done.9.refs_5_
  59.2 3.0 %collective-permute-start.12 = (bf16[2,3,8,32,128]{4,3,2,1,0:T(8,128)(2,1)S(1)}, bf16[2,3,8,32,128]{4,3,2,1,0:T(8,128)(2,1)}, u32[]{:S(2)}, u32[]{:S(2)}) collective-permute-start(bf16[2,3,8,32,128]{4,3,2,1,0:T(8,128)(2,1)S(1)} %get-tuple-element.89.refs_0_), channel_id=1, source_target_pairs={{0,8},{4,12},{8,0},{12,4},{1,9},{5,13},{9,1},{13,5},{2,10},{6,14},... | collective-permute-start | bytes 1179656 | tf_op jit(solution)/shard_map/ppermute | solution.py:288
  62.2 22.6 %shard_map.100.refs_11_ = f32[8,2,5,128,128]{4,3,2,1,0:T(8,128)} custom-call(s32[2]{0:T(128)} %pad_add_fusion.where, bf16[2,2,8,32,128]{4,3,2,1,0:T(8,128)(2,1)} %copy-done.7, bf16[2,2,8,32,128]{4,3,2,1,0:T(8,128)(2,1)} %copy-done.19, bf16[2,2,8,32,128]{4,3,2,1,0:T(8,128)(2,1)} %copy-done.18, bf16[2,2,8,32,128]{4,3,2,1,0:T(8,128)(2,1)} %copy-done.20, ...), custom_call_target="tpu_custom_call" | custom-call | flops 8192000000 | bytes 30000000 | tf_op jit(solution)/shard_map/pallas_call | solution.py:254
  84.9 2.3 %collective-permute-done.10.refs_3_ = bf16[2,3,8,32,128]{4,3,2,1,0:T(8,128)(2,1)S(1)} collective-permute-done((bf16[2,3,8,32,128]{4,3,2,1,0:T(8,128)(2,1)S(1)}, bf16[2,3,8,32,128]{4,3,2,1,0:T(8,128)(2,1)S(1)}, u32[]{:S(2)}, u32[]{:S(2)}) %collective-permute-start.10) | collective-permute-done | bytes 393248 | tf_op jit(solution)/shard_map/ppermute | solution.py:288
  88.3 2.7 %collective-permute-start.15 = (bf16[2,4,8,32,128]{4,3,2,1,0:T(8,128)(2,1)S(1)}, bf16[2,4,8,32,128]{4,3,2,1,0:T(8,128)(2,1)S(1)}, u32[]{:S(2)}, u32[]{:S(2)}) collective-permute-start(bf16[2,4,8,32,128]{4,3,2,1,0:T(8,128)(2,1)S(1)} %slice.41.refs_0_), channel_id=1, source_target_pairs={{0,8},{4,12},{8,0},{12,4},{1,9},{5,13},{9,1},{13,5},{2,10},{6,14},... | collective-permute-start | bytes 1572872 | tf_op jit(solution)/shard_map/ppermute | solution.py:288
  91.3 29.3 %shard_map.101.refs_11_ = f32[8,2,5,128,128]{4,3,2,1,0:T(8,128)} custom-call(s32[2]{0:T(128)} %pad_add_fusion.where, bf16[2,3,8,32,128]{4,3,2,1,0:T(8,128)(2,1)} %copy-done.5, bf16[2,3,8,32,128]{4,3,2,1,0:T(8,128)(2,1)} %copy-done.13, bf16[2,3,8,32,128]{4,3,2,1,0:T(8,128)(2,1)} %copy-done.14, bf16[2,3,8,32,128]{4,3,2,1,0:T(8,128)(2,1)} %copy-done.16, ...), custom_call_target="tpu_custom_call" | custom-call | flops 12288000000 | bytes 30000000 | tf_op jit(solution)/shard_map/pallas_call | solution.py:254
  120.8 1.6 collective-permute-start.16
  122.4 29.0 %shard_map.102.refs_11_ = f32[8,2,5,128,128]{4,3,2,1,0:T(8,128)} custom-call(s32[2]{0:T(128)} %pad_add_fusion.where, bf16[2,3,8,32,128]{4,3,2,1,0:T(8,128)(2,1)} %copy-done.4, bf16[2,3,8,32,128]{4,3,2,1,0:T(8,128)(2,1)} %copy-done.15, bf16[2,3,8,32,128]{4,3,2,1,0:T(8,128)(2,1)} %collective-permute-done.12.refs_2_, bf16[2,3,8,32,128]{4,3,2,1,0:T(8,128)(2,1)} %copy-done.17, ...), custom_call_target="tpu_custom_call" | custom-call | flops 12288000000 | bytes 30000000 | tf_op jit(solution)/shard_map/pallas_call | solution.py:254
  152.3 35.2 %shard_map.103 = (bf16[2,2,2,5,128,128]{5,4,3,2,1,0:T(8,128)(2,1)}, bf16[2,2,2,5,128,128]{5,4,3,2,1,0:T(8,128)(2,1)}) custom-call(s32[2]{0:T(128)} %pad_add_fusion.where, bf16[2,4,8,32,128]{4,3,2,1,0:T(8,128)(2,1)} %copy-done.3, bf16[2,4,8,32,128]{4,3,2,1,0:T(8,128)(2,1)} %copy-done.10, bf16[2,4,8,32,128]{4,3,2,1,0:T(8,128)(2,1)} %copy-done.11, ...), custom_call_target="tpu_custom_call" | custom-call | flops 16384000000 | bytes 30000000 | tf_op jit(solution)/shard_map/pallas_call | solution.py:254
  187.6 3.2 %collective-permute-done.17 = bf16[2,2,2,5,128,128]{5,4,3,2,1,0:T(8,128)(2,1)S(1)} collective-permute-done((bf16[2,2,2,5,128,128]{5,4,3,2,1,0:T(8,128)(2,1)}, bf16[2,2,2,5,128,128]{5,4,3,2,1,0:T(8,128)(2,1)S(1)}, u32[]{:S(2)}, u32[]{:S(2)}) %collective-permute-start.17) | collective-permute-done | bytes 1310752 | tf_op jit(solution)/shard_map/ppermute | solution.py:288
  190.8 1.8 add_convert_fusion
  192.7 1.4 collective-permute-start.18
  194.0 15.5 %collective-permute-done.18 = bf16[2,2,5,128,128]{4,3,2,1,0:T(8,128)(2,1)S(1)} collective-permute-done((bf16[2,2,5,128,128]{4,3,2,1,0:T(8,128)(2,1)S(1)}, bf16[2,2,5,128,128]{4,3,2,1,0:T(8,128)(2,1)S(1)}, u32[]{:S(2)}, u32[]{:S(2)}) %collective-permute-start.18) | collective-permute-done | bytes 655392 | tf_op jit(solution)/shard_map/ppermute | solution.py:288
  210.6 8.3 %collective-permute-done.19 = bf16[2,2,5,2,32,128]{5,4,0,2,1,3:T(8,128)(2,1)S(1)} collective-permute-done((bf16[2,2,5,2,32,128]{5,4,0,2,1,3:T(8,128)(2,1)S(1)}, bf16[2,2,5,2,32,128]{5,4,0,2,1,3:T(8,128)(2,1)S(1)}, u32[]{:S(2)}, u32[]{:S(2)}) %collective-permute-start.19) | collective-permute-done | bytes 327712 | tf_op jit(solution)/shard_map/ppermute | solution.py:288
  219.0 1.5 collective-permute-start.20
  220.5 7.4 %collective-permute-done.20 = bf16[2,2,5,32,128]{4,3,0,2,1:T(8,128)(2,1)S(1)} collective-permute-done((bf16[2,2,5,32,128]{4,3,0,2,1:T(8,128)(2,1)S(1)}, bf16[2,2,5,32,128]{4,3,0,2,1:T(8,128)(2,1)S(1)}, u32[]{:S(2)}, u32[]{:S(2)}) %collective-permute-start.20) | collective-permute-done | bytes 163872 | tf_op jit(solution)/shard_map/ppermute | solution.py:288
  (79 shorter events, 7.2 us)
Async XLA Ops:
  0.0 13.4 %copy-start.9 = (s32[32,8]{0,1:T(8,128)S(1)}, s32[32,8]{0,1:T(8,128)}, u32[]{:S(2)}) copy-start(s32[32,8]{0,1:T(8,128)} %param.14) | copy-start | bytes 3076
  1.1 15.2 %collective-permute-start = (bf16[2,5,2,32,128]{4,3,2,1,0:T(8,128)(2,1)S(1)}, bf16[2,5,2,32,128]{4,3,2,1,0:T(8,128)(2,1)S(1)}, u32[]{:S(2)}, u32[]{:S(2)}) collective-permute-start(bf16[2,5,2,32,128]{4,3,2,1,0:T(8,128)(2,1)S(1)} %constant_dynamic-slice_fusion), channel_id=1, source_target_pairs={{0,4},{4,0},{8,12},{12,8},{1,5},{5,1},{9,13},{13,9},{2,6},{6,2},{1... | collective-permute-start | bytes 491528 | tf_op jit(solution)/shard_map/ppermute | solution.py:288
  4.2 20.7 %collective-permute-start.1 = (bf16[2,5,2,32,128]{4,3,2,1,0:T(8,128)(2,1)S(1)}, bf16[2,5,2,32,128]{4,3,2,1,0:T(8,128)(2,1)S(1)}, u32[]{:S(2)}, u32[]{:S(2)}) collective-permute-start(bf16[2,5,2,32,128]{4,3,2,1,0:T(8,128)(2,1)S(1)} %constant_dynamic-slice_fusion), channel_id=1, source_target_pairs={{0,8},{4,12},{8,0},{12,4},{1,9},{5,13},{9,1},{13,5},{2,10},{6,14},... | collective-permute-start | bytes 491528 | tf_op jit(solution)/shard_map/ppermute | solution.py:288
  6.8 18.1 %collective-permute-start.2 = (bf16[2,5,2,32,128]{4,3,2,1,0:T(8,128)(2,1)S(1)}, bf16[2,5,2,32,128]{4,3,2,1,0:T(8,128)(2,1)S(1)}, u32[]{:S(2)}, u32[]{:S(2)}) collective-permute-start(bf16[2,5,2,32,128]{4,3,2,1,0:T(8,128)(2,1)S(1)} %constant_dynamic-slice_fusion), channel_id=1, source_target_pairs={{0,12},{4,8},{8,4},{12,0},{1,13},{5,9},{9,5},{13,1},{2,14},{6,10},... | collective-permute-start | bytes 491528 | tf_op jit(solution)/shard_map/ppermute | solution.py:288
  7.8 8.5 %copy-start.7 = (bf16[2,2,8,32,128]{4,3,2,1,0:T(8,128)(2,1)}, bf16[2,2,8,32,128]{4,3,2,1,0:T(8,128)(2,1)S(1)}, u32[]{:S(2)}) copy-start(bf16[2,2,8,32,128]{4,3,2,1,0:T(8,128)(2,1)S(1)} %slice.39.refs_0_) | copy-start | bytes 786436
  7.8 26.4 %collective-permute-start.4 = (bf16[2,2,8,32,128]{4,3,2,1,0:T(8,128)(2,1)S(1)}, bf16[2,2,8,32,128]{4,3,2,1,0:T(8,128)(2,1)S(1)}, u32[]{:S(2)}, u32[]{:S(2)}) collective-permute-start(bf16[2,2,8,32,128]{4,3,2,1,0:T(8,128)(2,1)S(1)} %slice.39.refs_0_), channel_id=1, source_target_pairs={{0,8},{4,12},{8,0},{12,4},{1,9},{5,13},{9,1},{13,5},{2,10},{6,14},... | collective-permute-start | bytes 786440 | tf_op jit(solution)/shard_map/ppermute | solution.py:288
  9.7 41.7 %collective-permute-start.6 = (bf16[2,2,8,32,128]{4,3,2,1,0:T(8,128)(2,1)S(1)}, bf16[2,2,8,32,128]{4,3,2,1,0:T(8,128)(2,1)S(1)}, u32[]{:S(2)}, u32[]{:S(2)}) collective-permute-start(bf16[2,2,8,32,128]{4,3,2,1,0:T(8,128)(2,1)S(1)} %slice.39.refs_0_), channel_id=1, source_target_pairs={{0,4},{4,0},{8,12},{12,8},{1,5},{5,1},{9,13},{13,9},{2,6},{6,2},{1... | collective-permute-start | bytes 786440 | tf_op jit(solution)/shard_map/ppermute | solution.py:288
  13.4 17.4 %copy-start.5 = (bf16[2,3,8,32,128]{4,3,2,1,0:T(8,128)(2,1)}, bf16[2,3,8,32,128]{4,3,2,1,0:T(8,128)(2,1)S(1)}, u32[]{:S(2)}) copy-start(bf16[2,3,8,32,128]{4,3,2,1,0:T(8,128)(2,1)S(1)} %get-tuple-element.80.refs_0_) | copy-start | bytes 1179652
  13.4 45.8 %copy-start.4 = (bf16[2,3,8,32,128]{4,3,2,1,0:T(8,128)(2,1)}, bf16[2,3,8,32,128]{4,3,2,1,0:T(8,128)(2,1)S(1)}, u32[]{:S(2)}) copy-start(bf16[2,3,8,32,128]{4,3,2,1,0:T(8,128)(2,1)S(1)} %get-tuple-element.89.refs_0_) | copy-start | bytes 1179652
  25.0 30.1 %collective-permute-start.3 = (bf16[4,2,5,2,32,128]{5,4,3,2,1,0:T(8,128)(2,1)S(1)}, bf16[4,2,5,2,32,128]{5,4,3,2,1,0:T(8,128)(2,1)S(1)}, u32[]{:S(2)}, u32[]{:S(2)}) collective-permute-start(bf16[4,2,5,2,32,128]{5,4,3,2,1,0:T(8,128)(2,1)S(1)} %get-tuple-element.108), channel_id=1, source_target_pairs={{0,2},{1,3},{2,0},{3,1},{4,6},{5,7},{6,4},{7,5},{8,10},{9,11},{10,... | collective-permute-start | bytes 1966088 | tf_op jit(solution)/shard_map/ppermute | solution.py:288
  26.6 28.4 %collective-permute-start.7 = (bf16[2,3,8,32,128]{4,3,2,1,0:T(8,128)(2,1)S(1)}, bf16[2,3,8,32,128]{4,3,2,1,0:T(8,128)(2,1)S(1)}, u32[]{:S(2)}, u32[]{:S(2)}) collective-permute-start(bf16[2,3,8,32,128]{4,3,2,1,0:T(8,128)(2,1)S(1)} %get-tuple-element.80.refs_0_), channel_id=1, source_target_pairs={{0,4},{4,0},{8,12},{12,8},{1,5},{5,1},{9,13},{13,9},{2,6},{6,2},{1... | collective-permute-start | bytes 1179656 | tf_op jit(solution)/shard_map/ppermute | solution.py:288
  30.8 24.3 %collective-permute-start.8 = (bf16[2,3,8,32,128]{4,3,2,1,0:T(8,128)(2,1)S(1)}, bf16[2,3,8,32,128]{4,3,2,1,0:T(8,128)(2,1)S(1)}, u32[]{:S(2)}, u32[]{:S(2)}) collective-permute-start(bf16[2,3,8,32,128]{4,3,2,1,0:T(8,128)(2,1)S(1)} %get-tuple-element.80.refs_0_), channel_id=1, source_target_pairs={{0,8},{4,12},{8,0},{12,4},{1,9},{5,13},{9,1},{13,5},{2,10},{6,14},... | collective-permute-start | bytes 1179656 | tf_op jit(solution)/shard_map/ppermute | solution.py:288
  34.1 20.9 %collective-permute-start.5 = (bf16[2,2,8,32,128]{4,3,2,1,0:T(8,128)(2,1)S(1)}, bf16[2,2,8,32,128]{4,3,2,1,0:T(8,128)(2,1)S(1)}, u32[]{:S(2)}, u32[]{:S(2)}) collective-permute-start(bf16[2,2,8,32,128]{4,3,2,1,0:T(8,128)(2,1)S(1)} %collective-permute-done.4.refs_2_), channel_id=1, source_target_pairs={{0,4},{4,0},{8,12},{12,8},{1,5},{5,1},{9,13},{13,9},{2,6},{6,2},{1... | collective-permute-start | bytes 786440 | tf_op jit(solution)/shard_map/ppermute | solution.py:288
  55.1 7.1 %copy-start.14 = (bf16[2,3,8,32,128]{4,3,2,1,0:T(8,128)(2,1)}, bf16[2,3,8,32,128]{4,3,2,1,0:T(8,128)(2,1)S(1)}, u32[]{:S(2)}) copy-start(bf16[2,3,8,32,128]{4,3,2,1,0:T(8,128)(2,1)S(1)} %collective-permute-done.8.refs_2_) | copy-start | bytes 1179652
  55.9 3.2 %collective-permute-start.9 = (bf16[2,4,2,5,2,32,128]{6,5,4,3,2,1,0:T(8,128)(2,1)S(1)}, bf16[2,4,2,5,2,32,128]{6,5,4,3,2,1,0:T(8,128)(2,1)}, u32[]{:S(2)}, u32[]{:S(2)}) collective-permute-start(bf16[2,4,2,5,2,32,128]{6,5,4,3,2,1,0:T(8,128)(2,1)S(1)} %pad_maximum_fusion.refs_4_), channel_id=1, source_target_pairs={{0,1},{1,0},{2,3},{3,2},{4,5},{5,4},{6,7},{7,6},{8,9},{9,8},{10,11... | collective-permute-start | bytes 3932168 | tf_op jit(solution)/shard_map/ppermute | solution.py:288
  57.5 30.8 %copy-start.3 = (bf16[2,4,8,32,128]{4,3,2,1,0:T(8,128)(2,1)}, bf16[2,4,8,32,128]{4,3,2,1,0:T(8,128)(2,1)S(1)}, u32[]{:S(2)}) copy-start(bf16[2,4,8,32,128]{4,3,2,1,0:T(8,128)(2,1)S(1)} %slice.41.refs_0_) | copy-start | bytes 1572868
  59.2 28.0 %collective-permute-start.11 = (bf16[2,3,8,32,128]{4,3,2,1,0:T(8,128)(2,1)S(1)}, bf16[2,3,8,32,128]{4,3,2,1,0:T(8,128)(2,1)S(1)}, u32[]{:S(2)}, u32[]{:S(2)}) collective-permute-start(bf16[2,3,8,32,128]{4,3,2,1,0:T(8,128)(2,1)S(1)} %get-tuple-element.89.refs_0_), channel_id=1, source_target_pairs={{0,4},{4,0},{8,12},{12,8},{1,5},{5,1},{9,13},{13,9},{2,6},{6,2},{1... | collective-permute-start | bytes 1179656 | tf_op jit(solution)/shard_map/ppermute | solution.py:288
  59.2 28.8 %collective-permute-start.12 = (bf16[2,3,8,32,128]{4,3,2,1,0:T(8,128)(2,1)S(1)}, bf16[2,3,8,32,128]{4,3,2,1,0:T(8,128)(2,1)}, u32[]{:S(2)}, u32[]{:S(2)}) collective-permute-start(bf16[2,3,8,32,128]{4,3,2,1,0:T(8,128)(2,1)S(1)} %get-tuple-element.89.refs_0_), channel_id=1, source_target_pairs={{0,8},{4,12},{8,0},{12,4},{1,9},{5,13},{9,1},{13,5},{2,10},{6,14},... | collective-permute-start | bytes 1179656 | tf_op jit(solution)/shard_map/ppermute | solution.py:288
  62.2 25.0 %collective-permute-start.10 = (bf16[2,3,8,32,128]{4,3,2,1,0:T(8,128)(2,1)S(1)}, bf16[2,3,8,32,128]{4,3,2,1,0:T(8,128)(2,1)S(1)}, u32[]{:S(2)}, u32[]{:S(2)}) collective-permute-start(bf16[2,3,8,32,128]{4,3,2,1,0:T(8,128)(2,1)S(1)} %collective-permute-done.8.refs_2_), channel_id=1, source_target_pairs={{0,4},{4,0},{8,12},{12,8},{1,5},{5,1},{9,13},{13,9},{2,6},{6,2},{1... | collective-permute-start | bytes 1179656 | tf_op jit(solution)/shard_map/ppermute | solution.py:288
  87.9 32.6 %copy-start.15 = (bf16[2,3,8,32,128]{4,3,2,1,0:T(8,128)(2,1)}, bf16[2,3,8,32,128]{4,3,2,1,0:T(8,128)(2,1)S(1)}, u32[]{:S(2)}) copy-start(bf16[2,3,8,32,128]{4,3,2,1,0:T(8,128)(2,1)S(1)} %collective-permute-done.11.refs_1_) | copy-start | bytes 1179652
  87.9 32.8 %collective-permute-start.14 = (bf16[2,4,8,32,128]{4,3,2,1,0:T(8,128)(2,1)S(1)}, bf16[2,4,8,32,128]{4,3,2,1,0:T(8,128)(2,1)S(1)}, u32[]{:S(2)}, u32[]{:S(2)}) collective-permute-start(bf16[2,4,8,32,128]{4,3,2,1,0:T(8,128)(2,1)S(1)} %slice.41.refs_0_), channel_id=1, source_target_pairs={{0,4},{4,0},{8,12},{12,8},{1,5},{5,1},{9,13},{13,9},{2,6},{6,2},{1... | collective-permute-start | bytes 1572872 | tf_op jit(solution)/shard_map/ppermute | solution.py:288
  88.3 32.5 %collective-permute-start.15 = (bf16[2,4,8,32,128]{4,3,2,1,0:T(8,128)(2,1)S(1)}, bf16[2,4,8,32,128]{4,3,2,1,0:T(8,128)(2,1)S(1)}, u32[]{:S(2)}, u32[]{:S(2)}) collective-permute-start(bf16[2,4,8,32,128]{4,3,2,1,0:T(8,128)(2,1)S(1)} %slice.41.refs_0_), channel_id=1, source_target_pairs={{0,8},{4,12},{8,0},{12,4},{1,9},{5,13},{9,1},{13,5},{2,10},{6,14},... | collective-permute-start | bytes 1572872 | tf_op jit(solution)/shard_map/ppermute | solution.py:288
  91.0 29.8 %collective-permute-start.13 = (bf16[2,3,8,32,128]{4,3,2,1,0:T(8,128)(2,1)}, bf16[2,3,8,32,128]{4,3,2,1,0:T(8,128)(2,1)S(1)}, u32[]{:S(2)}, u32[]{:S(2)}) collective-permute-start(bf16[2,3,8,32,128]{4,3,2,1,0:T(8,128)(2,1)} %collective-permute-done.12.refs_2_), channel_id=1, source_target_pairs={{0,4},{4,0},{8,12},{12,8},{1,5},{5,1},{9,13},{13,9},{2,6},{6,2},{1... | collective-permute-start | bytes 1179656 | tf_op jit(solution)/shard_map/ppermute | solution.py:288
  120.8 30.7 %copy-start.10 = (bf16[2,4,8,32,128]{4,3,2,1,0:T(8,128)(2,1)}, bf16[2,4,8,32,128]{4,3,2,1,0:T(8,128)(2,1)S(1)}, u32[]{:S(2)}) copy-start(bf16[2,4,8,32,128]{4,3,2,1,0:T(8,128)(2,1)S(1)} %collective-permute-done.14.refs_1_) | copy-start | bytes 1572868
  120.8 30.7 %copy-start.11 = (bf16[2,4,8,32,128]{4,3,2,1,0:T(8,128)(2,1)}, bf16[2,4,8,32,128]{4,3,2,1,0:T(8,128)(2,1)S(1)}, u32[]{:S(2)}) copy-start(bf16[2,4,8,32,128]{4,3,2,1,0:T(8,128)(2,1)S(1)} %collective-permute-done.15.refs_2_) | copy-start | bytes 1572868
  120.8 30.7 %collective-permute-start.16 = (bf16[2,4,8,32,128]{4,3,2,1,0:T(8,128)(2,1)S(1)}, bf16[2,4,8,32,128]{4,3,2,1,0:T(8,128)(2,1)S(1)}, u32[]{:S(2)}, u32[]{:S(2)}) collective-permute-start(bf16[2,4,8,32,128]{4,3,2,1,0:T(8,128)(2,1)S(1)} %collective-permute-done.15.refs_2_), channel_id=1, source_target_pairs={{0,4},{4,0},{8,12},{12,8},{1,5},{5,1},{9,13},{13,9},{2,6},{6,2},{1... | collective-permute-start | bytes 1572872 | tf_op jit(solution)/shard_map/ppermute | solution.py:288
  187.5 3.3 %collective-permute-start.17 = (bf16[2,2,2,5,128,128]{5,4,3,2,1,0:T(8,128)(2,1)}, bf16[2,2,2,5,128,128]{5,4,3,2,1,0:T(8,128)(2,1)S(1)}, u32[]{:S(2)}, u32[]{:S(2)}) collective-permute-start(bf16[2,2,2,5,128,128]{5,4,3,2,1,0:T(8,128)(2,1)} %get-tuple-element.102), channel_id=1, source_target_pairs={{0,1},{1,0},{2,3},{3,2},{4,5},{5,4},{6,7},{7,6},{8,9},{9,8},{10,11... | collective-permute-start | bytes 3932168 | tf_op jit(solution)/shard_map/ppermute | solution.py:288
  192.7 16.8 %collective-permute-start.18 = (bf16[2,2,5,128,128]{4,3,2,1,0:T(8,128)(2,1)S(1)}, bf16[2,2,5,128,128]{4,3,2,1,0:T(8,128)(2,1)S(1)}, u32[]{:S(2)}, u32[]{:S(2)}) collective-permute-start(bf16[2,2,5,128,128]{4,3,2,1,0:T(8,128)(2,1)S(1)} %slice_bitcast_fusion), channel_id=1, source_target_pairs={{0,2},{1,3},{2,0},{3,1},{4,6},{5,7},{6,4},{7,5},{8,10},{9,11},{10,... | collective-permute-start | bytes 1966088 | tf_op jit(solution)/shard_map/ppermute | solution.py:288
  209.7 18.2 %copy-start.6 = (f32[2,5,2,32,128]{4,3,2,1,0:T(8,128)S(1)}, f32[2,5,2,32,128]{4,3,2,1,0:T(8,128)}, u32[]{:S(2)}) copy-start(f32[2,5,2,32,128]{4,3,2,1,0:T(8,128)} %param.15) | copy-start | bytes 983044
  209.7 19.0 %copy-start.1 = (bf16[2,5,8,32,128]{4,3,2,1,0:T(8,128)(2,1)S(1)}, bf16[2,5,8,32,128]{4,3,2,1,0:T(8,128)(2,1)}, u32[]{:S(2)}) copy-start(bf16[2,5,8,32,128]{4,3,2,1,0:T(8,128)(2,1)} %param.10) | copy-start | bytes 1966084
  209.8 9.0 %collective-permute-start.19 = (bf16[2,2,5,2,32,128]{5,4,0,2,1,3:T(8,128)(2,1)S(1)}, bf16[2,2,5,2,32,128]{5,4,0,2,1,3:T(8,128)(2,1)S(1)}, u32[]{:S(2)}, u32[]{:S(2)}) collective-permute-start(bf16[2,2,5,2,32,128]{5,4,0,2,1,3:T(8,128)(2,1)S(1)} %bitcast.60), channel_id=1, source_target_pairs={{0,4},{4,0},{8,12},{12,8},{1,5},{5,1},{9,13},{13,9},{2,6},{6,2},{1... | collective-permute-start | bytes 983048 | tf_op jit(solution)/shard_map/ppermute | solution.py:288
  219.0 9.0 %collective-permute-start.20 = (bf16[2,2,5,32,128]{4,3,0,2,1:T(8,128)(2,1)S(1)}, bf16[2,2,5,32,128]{4,3,0,2,1:T(8,128)(2,1)S(1)}, u32[]{:S(2)}, u32[]{:S(2)}) collective-permute-start(bf16[2,2,5,32,128]{4,3,0,2,1:T(8,128)(2,1)S(1)} %slice_bitcast_fusion.2), channel_id=1, source_target_pairs={{0,8},{4,12},{8,0},{12,4},{1,9},{5,13},{9,1},{13,5},{2,10},{6,14},... | collective-permute-start | bytes 491528 | tf_op jit(solution)/shard_map/ppermute | solution.py:288
  (10 other events, 27.7 us)

commit v3 on v2

--- a/solution.py
+++ b/solution.py
@@ -1,4 +1,5 @@
 import functools
+import itertools
 import math
 
 import jax
@@ -71,8 +72,8 @@
 def coils_kernel(width, pieces, images, first, last, where, *refs):
     maps, refs = refs[:pieces], refs[pieces:]
     shared, refs = refs[:images], refs[images:]
-    weights_hbm, ty, tx, tix, tiy = refs[:5]
-    rest = list(refs[5:])
+    *weights_hbm, ty, tx, tix, tiy = refs[:6]
+    rest = list(refs[6:])
     acc_in = None if first else rest.pop(0)
     outs, rest = (rest[:2], rest[2:]) if last else (rest[:1], rest[1:])
     image, rows, spec, mid, product, weights, sems, image_sems = rest[:8]
@@ -81,10 +82,13 @@
     tiles = width // 16
     step = pl.program_id(0)
     me = where[1]
-    fetch = [
-        pltpu.make_async_copy(weights_hbm.at[q], weights.at[q], sems.at[q]) for q in range(NZ)
-    ]
-    resume = None if first else pltpu.make_async_copy(acc_in, acc, sems.at[NZ])
+
+    def fetch(part, q):
+        return pltpu.make_async_copy(
+            weights_hbm[part].at[q], weights.at[part, q], sems.at[2 * q + part]
+        )
+
+    resume = None if first else pltpu.make_async_copy(acc_in, acc, sems.at[2 * NZ])
     groups = image.shape[0]
     arrive = []
     for b, ref in enumerate(shared):
@@ -98,8 +102,9 @@
     def _():
         for copy in arrive:
             copy.start()
-        for copy in fetch:
-            copy.start()
+        for q in range(NZ):
+            fetch(0, q).start()
+            fetch(1, q).start()
         if first:
             acc[...] = jnp.zeros_like(acc)
         else:
@@ -153,7 +158,7 @@
         for k in range(K):
             re, im = [], []
             for j in range(K):
-                kr, ki = weights[q, k, j, 0, a], weights[q, k, j, 1, a]
+                kr, ki = weights[0, q, k, j, a], weights[1, q, k, j, a]
                 re.append(kr * sr[j] - ki * si[j])
                 im.append(kr * si[j] + ki * sr[j])
             spec[k, at, :half] = tree(re)
@@ -162,7 +167,8 @@
     def apply_all(q, _):
         @pl.when(step == 0)
         def _():
-            pltpu.make_async_copy(weights_hbm.at[q], weights.at[q], sems.at[q]).wait()
+            fetch(0, q).wait()
+            fetch(1, q).wait()
 
         for t in range(tiles):
             apply(q, t)
@@ -204,11 +210,13 @@
 
         @pl.when(step == pl.num_programs(0) - 1)
         def _():
-            for x in range(2):
-                for z in range(NZ // 4):
-                    base = (x ^ (me // 2)) * (NZ // 2) + z
-                    for c in range(2):
-                        outs[c][x, z] = acc[base + (c ^ (me % 2)) * (NZ // 4)].astype(BF)
+            low, high, block = outs[0].shape[2], outs[0].shape[3], outs[0].shape[6]
+            for c, x, z, part in itertools.product(range(2), range(2), range(NZ // 4), range(2)):
+                plane = (x ^ (me // 2)) * (NZ // 2) + (c ^ (me % 2)) * (NZ // 4) + z
+                for lo, hi in itertools.product(range(low), range(high)):
+                    a, b = (lo, x) if part == 1 and low == 2 else (x, lo)
+                    at = (hi * low + lo) * block
+                    outs[c][part, a, b, hi, :, z] = acc[plane, part, :, at : at + block].astype(BF)
 
 
 def coils(maps, images, weights, tables, acc, last, where):
@@ -218,14 +226,15 @@
     nx, ny = tables[2].shape[2] // 2, tables[3].shape[2] // 2
     anywhere = pl.BlockSpec(memory_space=pl.ANY)
     shape = (NZ, 2, K, nx, ny)
-    half = (2, NZ // 4, 2, K, nx, ny)
+    split = 2 if len(maps) == 4 else 1
+    half = (2, 2, split, split, K, NZ // 4, nx // split**2, ny)
     out = [jax.ShapeDtypeStruct(half, BF)] * 2 if last else jax.ShapeDtypeStruct(shape, F32)
     block = lambda dims: pl.BlockSpec(
         dims, lambda c, w: (0,) * len(dims), pipeline_mode=pl.Buffered(buffer_count=1)
     )
-    args = [*maps, *images, weights, *tables]
+    args = [*maps, *images, *weights, *tables]
     specs = [pl.BlockSpec((2, 1) + m.shape[2:], lambda c, w: (0, c, 0, 0, 0)) for m in maps]
-    specs += [anywhere] * (len(images) + 1)
+    specs += [anywhere] * (len(images) + 2)
     specs += [
         pl.BlockSpec(
             (None,) + t.shape[1:],
@@ -244,8 +253,8 @@
         pltpu.VMEM((K, NZ * width, spec_width), BF),
         pltpu.VMEM((K, NZ * width, 2 * nx), BF),
         pltpu.VMEM((K, NZ * nx, 2 * ny), BF),
-        pltpu.VMEM(weights.shape, BF),
-        pltpu.SemaphoreType.DMA((NZ + 1,)),
+        pltpu.VMEM((2,) + weights[0].shape, BF),
+        pltpu.SemaphoreType.DMA((2 * NZ + 1,)),
         pltpu.SemaphoreType.DMA((groups,)),
     ]
     if last:
@@ -261,7 +270,7 @@
             scratch_shapes=scratch,
         ),
         out_shape=out,
-        compiler_params=pltpu.CompilerParams(vmem_limit_bytes=60 * 2**20),
+        compiler_params=pltpu.CompilerParams(vmem_limit_bytes=34 * 2**20),
         cost_estimate=pl.CostEstimate(
             flops=planes * width * 4 * 2 * 200_000, bytes_accessed=30_000_000, transcendentals=0
         ),
@@ -274,13 +283,18 @@
         sampled.astype(F32)[:, None, None, None, :] * scale
     )
     real, imag = picked[:, 0], picked[:, 1]
-    pairs = jnp.stack([jnp.stack([real, -imag], 1), jnp.stack([imag, real], 1)], 1)
     spread = point_spread.astype(BF)
     if pad:
         spread = jnp.pad(spread, ((0, 0), (0, 0), (0, pad), (0, 0)))
-    return jnp.einsum(
-        "gpikjq,givu->qkjpvu", pairs.astype(BF), spread, preferred_element_type=F32
-    ).astype(BF)
+    return [
+        jnp.einsum(
+            "gikjq,givu->qkjvu",
+            jnp.stack(pair, 1).astype(BF),
+            spread,
+            preferred_element_type=F32,
+        ).astype(BF)
+        for pair in ((real, -imag), (imag, real))
+    ]
 
 
 def swap(value, axis, bit):
@@ -329,33 +343,29 @@
         starts = [sum(sizes[:m]) for m in range(len(sizes))]
         parts = [
             lax.slice_in_dim(coil_maps, a, a + n, axis=1) for a, n in zip(starts, sizes)
-        ] + [None, None]
-
-        def begin(part):
-            return None if part is None else (swap(part, "dom", 1), swap(part, "dom", 2))
+        ]
+        fence = lax.optimization_barrier
 
         mine = lax.dynamic_slice_in_dim(basis_image, me * (NZ // coil), NZ // coil, 2)
         mine = [mine] + [swap(mine, "dom", r) for r in (1, 2, 3)]
-        first = begin(parts[0])
-        mine, parts[1] = lax.optimization_barrier((mine, parts[1]))
+        mine, weights[0], parts = fence((mine, weights[0], parts))
         mine = jnp.stack(mine)
-        second = begin(parts[1])
         there = swap(mine, "coil", 2)
-        third = swap(first[1], "dom", 1)
-        there, weights, third, first, second = lax.optimization_barrier(
-            (there, weights, third, first, second)
+        one, two = swap(parts[0], "dom", 1), swap(parts[0], "dom", 2)
+        ahead = [swap(p, "dom", 2) for p in parts[1:2]]
+        there, weights[1], one, two, ahead, parts = fence(
+            (there, weights[1], one, two, ahead, parts)
         )
         both = jnp.stack([mine, there])
         images = [both, swap(both, "coil", 1)]
+        held = [one, two, swap(two, "dom", 1)]
         total = None
         for m in range(len(sizes)):
-            maps = [parts[m], *first, third]
-            images, maps, second, parts[m + 2], total = lax.optimization_barrier(
-                (images, maps, second, parts[m + 2], total)
-            )
-            if second is not None:
-                third = swap(second[1], "dom", 1)
-            first, second = second, begin(parts[m + 2])
+            images, held, ahead, parts, total = fence((images, held, ahead, parts, total))
+            maps, held = [parts[m], *held], []
+            if ahead:
+                held = [swap(parts[m + 1], "dom", 1), ahead[0], swap(ahead[0], "dom", 1)]
+                ahead = [swap(p, "dom", 2) for p in parts[m + 2 : m + 3]]
             total = coils(maps, images, weights, tables, total, m == len(sizes) - 1, where)
     else:
         images = [lax.all_gather(basis_image, "dom", axis=3, tiled=True)[None, None]]
@@ -365,16 +375,19 @@
     def plus(a, b):
         return a.astype(F32) + b.astype(F32)
 
+    def half(value, axis, bit):
+        return plus(value[0], swap(value[1], axis, bit)).astype(BF)
+
     keep, send = total
     total = plus(keep, swap(send, "coil", 1)).astype(BF)
-    total = plus(total[0], swap(total[1], "coil", 2)).astype(BF)
     if not butterfly:
-        total = lax.psum_scatter(total, "dom", scatter_dimension=3, tiled=True)
-        return total.astype(F32).transpose(1, 2, 0, 3, 4) - adjoint_data
-    total = total.reshape(NZ // coil, 2, K, 2, 2, rows, ny)
-    total = plus(total[:, :, :, :, 0], swap(total[:, :, :, :, 1], "dom", 1)).astype(BF)
-    total = plus(total[:, :, :, 0], swap(total[:, :, :, 1], "dom", 2))
-    return total.transpose(1, 2, 0, 3, 4) - adjoint_data
+        total = plus(total[:, 0], swap(total[:, 1], "coil", 2)).astype(BF)
+        total = lax.psum_scatter(total[:, 0, 0], "dom", scatter_dimension=3, tiled=True)
+        return total.astype(F32) - adjoint_data
+    real, imag = half(total[0], "coil", 2), half(total[1], "dom", 1)
+    real, imag = half(real, "dom", 1), half(imag, "coil", 2)
+    there = swap(jnp.stack([real[1], imag[1]]), "dom", 2)
+    return jnp.stack([plus(real[0], there[0]), plus(imag[0], there[1])]) - adjoint_data
 
 
 CHUNKS = (2, 3, 3, 4)

time: 229 us -> 212 us (0.926)
  Pallas kernels: 116 us -> 101 us
  local copies, waits for them, and re-layouts: 17.9 us -> 20.7 us
  matrix products: 6.7 us -> 3.91 us
    pallas_call x4, Pallas kernels: 116 us -> 101 us  [coils(): pl.pallas_call(functools.partial(coils_kernel, width, len(maps), len(imag...]
    unnamed x43 -> x30, local copies, waits for them, and re-layouts: 3.43 us -> 9.83 us
    dot_general x1 -> x2, matrix products: 6.7 us -> 3.91 us  [kernel_weights(): jnp.einsum('gikjq,givu->qkjvu', jnp.stack(pair, 1).astype(BF), spread, pr...]
    dot_general x1 -> x2, local copies, waits for them, and re-layouts: 10.7 us -> 8.59 us  [kernel_weights(): jnp.einsum('gikjq,givu->qkjvu', jnp.stack(pair, 1).astype(BF), spread, pr...]
    ppermute x21 -> x23, waiting for transfers between devices: 52.5 us -> 51.2 us  [swap(): return lax.ppermute(value, axis, [(i, i ^ bit) for i in range(size)])]
    ppermute x21 -> x23, starting transfers between devices: 28.6 us -> 27.5 us  [swap(): return lax.ppermute(value, axis, [(i, i ^ bit) for i in range(size)])]
  transfers between devices with their start and end apart: 21 -> 23, of which waited for: 10 -> 10; matrix products, arithmetic and copies ran while one was open for 11% -> 9% of each run, Pallas kernels for 35% -> 33%
where the time goes in v3:
time: 212 us; the launch traced here: 211 us
  Pallas kernels  101 us (48%)
  waiting for transfers between devices  51.2 us (24%)
  starting transfers between devices  27.5 us (13%)
  local copies, waits for them, and re-layouts  20.7 us (10%)
  other arithmetic  5.93 us (3%)
  matrix products  3.91 us (2%)
    pallas_call x4, Pallas kernels, coils(): pl.pallas_call(functools.partial(coils_kernel, width, len(maps), len(imag...  101 us
    ppermute x23, waiting for transfers between devices, swap(): return lax.ppermute(value, axis, [(i, i ^ bit) for i in range(size)])  51.2 us
    ppermute x23, starting transfers between devices, swap(): return lax.ppermute(value, axis, [(i, i ^ bit) for i in range(size)])  27.5 us
    unnamed x30, local copies, waits for them, and re-layouts  9.83 us
    dot_general x2, local copies, waits for them, and re-layouts, kernel_weights(): jnp.einsum('gikjq,givu->qkjvu', jnp.stack(pair, 1).astype(BF), spread, pr...  8.59 us
  transfers between devices with their start and end apart: 23, of which 10 were waited for; matrix products, arithmetic and copies ran while one was open for 9% of the time, Pallas kernels for 33%

profile of v3, /device:TPU:0, one launch (start us, length us, event | category | flops | bytes accessed | tf_op | source)
XLA Modules:
  0.0 211.0 jit_solution(6296633541026043966)
XLA Ops:
  1.1 5.1 %collective-permute-start.2 = (bf16[2,5,2,32,128]{4,3,2,1,0:T(8,128)(2,1)S(1)}, bf16[2,5,2,32,128]{4,3,2,1,0:T(8,128)(2,1)S(1)}, u32[]{:S(2)}, u32[]{:S(2)}) collective-permute-start(bf16[2,5,2,32,128]{4,3,2,1,0:T(8,128)(2,1)S(1)} %constant_dynamic-slice_fusion), channel_id=1, source_target_pairs={{0,12},{4,8},{8,4},{12,0},{1,13},{5,9},{9,5},{13,1},{2,14},{6,10},... | collective-permute-start | bytes 491528 | tf_op jit(solution)/shard_map/ppermute | solution.py:302
  10.4 2.5 %convert_bitcast_fusion = bf16[32,2,64,256,1,1]{3,2,1,0,5,4:T(8,128)(2,1)S(1)} fusion(f32[32,2,64,256]{3,2,1,0:T(8,128)} %param.12), kind=kLoop, calls=%fused_computation.7 | loop fusion | flops 1048576 | bytes 6291456 | tf_op jit(solution)/shard_map/convert_element_type | solution.py:286
  12.9 2.0 convolution_bitcast_fusion.1
  14.9 4.3 %copy.35 = bf16[5,5,8,64,256]{4,3,1,0,2:T(8,128)(2,1)} copy(bf16[5,5,8,64,256]{4,2,3,1,0:T(8,128)(2,1)S(1)} %convolution_bitcast_fusion.1) | data formatting | bytes 13107200 | tf_op jit(solution)/shard_map/gikjq,givu->qkjvu/dot_general | solution.py:290
  20.2 1.6 collective-permute-start.3
  21.8 1.5 collective-permute-start.6
  23.2 1.5 collective-permute-start.5
  25.3 2.0 convolution_bitcast_fusion
  27.2 4.3 %copy.36 = bf16[5,5,8,64,256]{4,3,1,0,2:T(8,128)(2,1)} copy(bf16[5,5,8,64,256]{4,2,3,1,0:T(8,128)(2,1)S(1)} %convolution_bitcast_fusion) | data formatting | bytes 13107200 | tf_op jit(solution)/shard_map/gikjq,givu->qkjvu/dot_general | solution.py:290
  31.6 20.7 %collective-permute-done.5.refs_2_ = bf16[2,2,8,32,128]{4,3,2,1,0:T(8,128)(2,1)S(1)} collective-permute-done((bf16[2,2,8,32,128]{4,3,2,1,0:T(8,128)(2,1)S(1)}, bf16[2,2,8,32,128]{4,3,2,1,0:T(8,128)(2,1)S(1)}, u32[]{:S(2)}, u32[]{:S(2)}) %collective-permute-start.5) | collective-permute-done | bytes 262176 | tf_op jit(solution)/shard_map/ppermute | solution.py:302
  53.0 8.7 %collective-permute-done.8.refs_3_ = bf16[2,2,8,32,128]{4,3,2,1,0:T(8,128)(2,1)} collective-permute-done((bf16[2,2,8,32,128]{4,3,2,1,0:T(8,128)(2,1)S(1)}, bf16[2,2,8,32,128]{4,3,2,1,0:T(8,128)(2,1)}, u32[]{:S(2)}, u32[]{:S(2)}) %collective-permute-start.8) | collective-permute-done | bytes 262176 | tf_op jit(solution)/shard_map/ppermute | solution.py:302
  62.0 1.7 collective-permute-start.10
  63.8 1.3 collective-permute-start.11
  65.1 2.9 %copy-done.2 = bf16[5,5,8,64,256]{4,3,1,0,2:T(8,128)(2,1)S(1)} copy-done((bf16[5,5,8,64,256]{4,3,1,0,2:T(8,128)(2,1)S(1)}, bf16[5,5,8,64,256]{4,3,1,0,2:T(8,128)(2,1)}, u32[]{:S(2)}) %copy-start.2) | copy-done | bytes 6553624
  68.9 1.2 copy-done.5
  70.1 1.2 copy-done.7
  73.3 16.7 %shard_map.100.refs_12_ = f32[8,2,5,128,128]{4,3,2,1,0:T(8,128)S(1)} custom-call(s32[2]{0:T(128)S(1)} %pad_add_fusion.where, bf16[2,2,8,32,128]{4,3,2,1,0:T(8,128)(2,1)S(1)} %slice.72.refs_0_, bf16[2,2,8,32,128]{4,3,2,1,0:T(8,128)(2,1)S(1)} %copy-done.4, bf16[2,2,8,32,128]{4,3,2,1,0:T(8,128)(2,1)S(1)} %collective-permute-done.5.refs_2_, ...), custom_call_target="tpu_custom_call" | custom-call | flops 8192000000 | bytes 30000000 | tf_op jit(solution)/shard_map/pallas_call | solution.py:263
  90.0 1.8 collective-permute-start.12
  92.1 1.6 collective-permute-start.14
  93.7 26.0 %shard_map.101.refs_12_ = f32[8,2,5,128,128]{4,3,2,1,0:T(8,128)S(1)} custom-call(s32[2]{0:T(128)S(1)} %pad_add_fusion.where, bf16[2,3,8,32,128]{4,3,2,1,0:T(8,128)(2,1)S(1)} %get-tuple-element.94.refs_0_, bf16[2,3,8,32,128]{4,3,2,1,0:T(8,128)(2,1)S(1)} %collective-permute-done.9.refs_1_, bf16[2,3,8,32,128]{4,3,2,1,0:T(8,128)(2,1)S(1)} %collective-permute-done.6.refs_2_, ...), custom_call_target="tpu_custom_call" | custom-call | flops 12288000000 | bytes 30000000 | tf_op jit(solution)/shard_map/pallas_call | solution.py:263
  119.8 1.4 collective-permute-start.15
  121.9 26.2 %shard_map.102.refs_12_ = f32[8,2,5,128,128]{4,3,2,1,0:T(8,128)S(1)} custom-call(s32[2]{0:T(128)S(1)} %pad_add_fusion.where, bf16[2,3,8,32,128]{4,3,2,1,0:T(8,128)(2,1)S(1)} %get-tuple-element.103.refs_0_, bf16[2,3,8,32,128]{4,3,2,1,0:T(8,128)(2,1)S(1)} %collective-permute-done.12.refs_1_, bf16[2,3,8,32,128]{4,3,2,1,0:T(8,128)(2,1)S(1)} %collective-permute-done.11.refs_2_, ...), custom_call_target="tpu_custom_call" | custom-call | flops 12288000000 | bytes 30000000 | tf_op jit(solution)/shard_map/pallas_call | solution.py:263
  148.1 32.5 %shard_map.103 = (bf16[2,2,2,2,5,2,32,128]{7,6,5,4,3,2,1,0:T(8,128)(2,1)S(1)}, bf16[2,2,2,2,5,2,32,128]{7,6,5,4,3,2,1,0:T(8,128)(2,1)S(1)}) custom-call(s32[2]{0:T(128)S(1)} %pad_add_fusion.where, bf16[2,4,8,32,128]{4,3,2,1,0:T(8,128)(2,1)S(1)} %slice.75.refs_0_, bf16[2,4,8,32,128]{4,3,2,1,0:T(8,128)(2,1)S(1)} %collective-permute-done.15.refs_1_, ...), custom_call_target="tpu_custom_call" | custom-call | flops 16384000000 | bytes 30000000 | tf_op jit(solution)/shard_map/pallas_call | solution.py:263
  180.7 3.0 %collective-permute-done.17 = bf16[2,2,2,2,5,2,32,128]{7,6,5,4,3,2,1,0:T(8,128)(2,1)S(1)} collective-permute-done((bf16[2,2,2,2,5,2,32,128]{7,6,5,4,3,2,1,0:T(8,128)(2,1)S(1)}, bf16[2,2,2,2,5,2,32,128]{7,6,5,4,3,2,1,0:T(8,128)(2,1)S(1)}, u32[]{:S(2)}, u32[]{:S(2)}) %collective-permute-start.17) | collective-permute-done | bytes 1310752 | tf_op jit(solution)/shard_map/ppermute | solution.py:302
  184.9 1.4 collective-permute-start.20
  186.3 7.8 %collective-permute-done.18 = bf16[2,2,5,2,32,128]{5,4,3,2,1,0:T(8,128)(2,1)S(1)} collective-permute-done((bf16[2,2,5,2,32,128]{5,4,3,2,1,0:T(8,128)(2,1)S(1)}, bf16[2,2,5,2,32,128]{5,4,3,2,1,0:T(8,128)(2,1)S(1)}, u32[]{:S(2)}, u32[]{:S(2)}) %collective-permute-start.18) | collective-permute-done | bytes 327712 | tf_op jit(solution)/shard_map/ppermute | solution.py:302
  194.6 1.6 collective-permute-start.21
  196.2 1.5 collective-permute-start.19
  197.7 2.3 %collective-permute-done.21 = bf16[2,5,2,32,128]{4,3,2,1,0:T(8,128)(2,1)S(1)} collective-permute-done((bf16[2,5,2,32,128]{4,3,2,1,0:T(8,128)(2,1)S(1)}, bf16[2,5,2,32,128]{4,3,2,1,0:T(8,128)(2,1)S(1)}, u32[]{:S(2)}, u32[]{:S(2)}) %collective-permute-start.21) | collective-permute-done | bytes 163872 | tf_op jit(solution)/shard_map/ppermute | solution.py:302
  200.1 1.5 collective-permute-done.19
  201.7 2.5 %collective-permute-start.22 = (bf16[2,5,2,32,128]{4,3,2,1,0:T(8,128)(2,1)S(1)}, bf16[2,5,2,32,128]{4,3,2,1,0:T(8,128)(2,1)S(1)}, u32[]{:S(2)}, u32[]{:S(2)}) collective-permute-start(bf16[2,5,2,32,128]{4,3,2,1,0:T(8,128)(2,1)S(1)} %pad_maximum_fusion.2), channel_id=1, source_target_pairs={{0,8},{4,12},{8,0},{12,4},{1,9},{5,13},{9,1},{13,5},{2,10},{6,14},... | collective-permute-start | bytes 491528 | tf_op jit(solution)/shard_map/ppermute | solution.py:302
  204.2 5.9 %collective-permute-done.22 = bf16[2,5,2,32,128]{4,3,2,1,0:T(8,128)(2,1)S(1)} collective-permute-done((bf16[2,5,2,32,128]{4,3,2,1,0:T(8,128)(2,1)S(1)}, bf16[2,5,2,32,128]{4,3,2,1,0:T(8,128)(2,1)S(1)}, u32[]{:S(2)}, u32[]{:S(2)}) %collective-permute-start.22) | collective-permute-done | bytes 163872 | tf_op jit(solution)/shard_map/ppermute | solution.py:302
  (76 shorter events, 14.5 us)
Async XLA Ops:
  1.1 18.1 %collective-permute-start.2 = (bf16[2,5,2,32,128]{4,3,2,1,0:T(8,128)(2,1)S(1)}, bf16[2,5,2,32,128]{4,3,2,1,0:T(8,128)(2,1)S(1)}, u32[]{:S(2)}, u32[]{:S(2)}) collective-permute-start(bf16[2,5,2,32,128]{4,3,2,1,0:T(8,128)(2,1)S(1)} %constant_dynamic-slice_fusion), channel_id=1, source_target_pairs={{0,12},{4,8},{8,4},{12,0},{1,13},{5,9},{9,5},{13,1},{2,14},{6,10},... | collective-permute-start | bytes 491528 | tf_op jit(solution)/shard_map/ppermute | solution.py:302
  6.2 13.9 %collective-permute-start.1 = (bf16[2,5,2,32,128]{4,3,2,1,0:T(8,128)(2,1)S(1)}, bf16[2,5,2,32,128]{4,3,2,1,0:T(8,128)(2,1)S(1)}, u32[]{:S(2)}, u32[]{:S(2)}) collective-permute-start(bf16[2,5,2,32,128]{4,3,2,1,0:T(8,128)(2,1)S(1)} %constant_dynamic-slice_fusion), channel_id=1, source_target_pairs={{0,8},{4,12},{8,0},{12,4},{1,9},{5,13},{9,1},{13,5},{2,10},{6,14},... | collective-permute-start | bytes 491528 | tf_op jit(solution)/shard_map/ppermute | solution.py:302
  6.2 13.9 %collective-permute-start = (bf16[2,5,2,32,128]{4,3,2,1,0:T(8,128)(2,1)S(1)}, bf16[2,5,2,32,128]{4,3,2,1,0:T(8,128)(2,1)S(1)}, u32[]{:S(2)}, u32[]{:S(2)}) collective-permute-start(bf16[2,5,2,32,128]{4,3,2,1,0:T(8,128)(2,1)S(1)} %constant_dynamic-slice_fusion), channel_id=1, source_target_pairs={{0,4},{4,0},{8,12},{12,8},{1,5},{5,1},{9,13},{13,9},{2,6},{6,2},{1... | collective-permute-start | bytes 491528 | tf_op jit(solution)/shard_map/ppermute | solution.py:302
  14.9 4.3 %copy-start.13 = (bf16[2,12,8,32,128]{4,3,2,1,0:T(8,128)(2,1)S(1)}, bf16[2,12,8,32,128]{4,3,2,1,0:T(8,128)(2,1)}, u32[]{:S(2)}) copy-start(bf16[2,12,8,32,128]{4,3,2,1,0:T(8,128)(2,1)} %param.11) | copy-start | bytes 4718596
  20.2 32.0 %collective-permute-start.3 = (bf16[4,2,5,2,32,128]{5,4,3,2,1,0:T(8,128)(2,1)S(1)}, bf16[4,2,5,2,32,128]{5,4,3,2,1,0:T(8,128)(2,1)S(1)}, u32[]{:S(2)}, u32[]{:S(2)}) collective-permute-start(bf16[4,2,5,2,32,128]{5,4,3,2,1,0:T(8,128)(2,1)S(1)} %get-tuple-element.124), channel_id=1, source_target_pairs={{0,2},{1,3},{2,0},{3,1},{4,6},{5,7},{6,4},{7,5},{8,10},{9,11},{10,... | collective-permute-start | bytes 1966088 | tf_op jit(solution)/shard_map/ppermute | solution.py:302
  21.8 30.5 %collective-permute-start.6 = (bf16[2,3,8,32,128]{4,3,2,1,0:T(8,128)(2,1)S(1)}, bf16[2,3,8,32,128]{4,3,2,1,0:T(8,128)(2,1)S(1)}, u32[]{:S(2)}, u32[]{:S(2)}) collective-permute-start(bf16[2,3,8,32,128]{4,3,2,1,0:T(8,128)(2,1)S(1)} %get-tuple-element.94.refs_0_), channel_id=1, source_target_pairs={{0,8},{4,12},{8,0},{12,4},{1,9},{5,13},{9,1},{13,5},{2,10},{6,14},... | collective-permute-start | bytes 1179656 | tf_op jit(solution)/shard_map/ppermute | solution.py:302
  23.2 29.0 %collective-permute-start.5 = (bf16[2,2,8,32,128]{4,3,2,1,0:T(8,128)(2,1)S(1)}, bf16[2,2,8,32,128]{4,3,2,1,0:T(8,128)(2,1)S(1)}, u32[]{:S(2)}, u32[]{:S(2)}) collective-permute-start(bf16[2,2,8,32,128]{4,3,2,1,0:T(8,128)(2,1)S(1)} %slice.72.refs_0_), channel_id=1, source_target_pairs={{0,8},{4,12},{8,0},{12,4},{1,9},{5,13},{9,1},{13,5},{2,10},{6,14},... | collective-permute-start | bytes 786440 | tf_op jit(solution)/shard_map/ppermute | solution.py:302
  24.7 27.5 %collective-permute-start.4 = (bf16[2,2,8,32,128]{4,3,2,1,0:T(8,128)(2,1)S(1)}, bf16[2,2,8,32,128]{4,3,2,1,0:T(8,128)(2,1)S(1)}, u32[]{:S(2)}, u32[]{:S(2)}) collective-permute-start(bf16[2,2,8,32,128]{4,3,2,1,0:T(8,128)(2,1)S(1)} %slice.72.refs_0_), channel_id=1, source_target_pairs={{0,4},{4,0},{8,12},{12,8},{1,5},{5,1},{9,13},{13,9},{2,6},{6,2},{1... | collective-permute-start | bytes 786440 | tf_op jit(solution)/shard_map/ppermute | solution.py:302
  52.9 8.8 %collective-permute-start.7 = (bf16[2,4,2,5,2,32,128]{6,5,4,3,2,1,0:T(8,128)(2,1)S(1)}, bf16[2,4,2,5,2,32,128]{6,5,4,3,2,1,0:T(8,128)(2,1)}, u32[]{:S(2)}, u32[]{:S(2)}) collective-permute-start(bf16[2,4,2,5,2,32,128]{6,5,4,3,2,1,0:T(8,128)(2,1)S(1)} %pad_maximum_fusion.refs_4_), channel_id=1, source_target_pairs={{0,1},{1,0},{2,3},{3,2},{4,5},{5,4},{6,7},{7,6},{8,9},{9,8},{10,11... | collective-permute-start | bytes 3932168 | tf_op jit(solution)/shard_map/ppermute | solution.py:302
  52.9 8.8 %collective-permute-start.8 = (bf16[2,2,8,32,128]{4,3,2,1,0:T(8,128)(2,1)S(1)}, bf16[2,2,8,32,128]{4,3,2,1,0:T(8,128)(2,1)}, u32[]{:S(2)}, u32[]{:S(2)}) collective-permute-start(bf16[2,2,8,32,128]{4,3,2,1,0:T(8,128)(2,1)S(1)} %collective-permute-done.5.refs_2_), channel_id=1, source_target_pairs={{0,4},{4,0},{8,12},{12,8},{1,5},{5,1},{9,13},{13,9},{2,6},{6,2},{1... | collective-permute-start | bytes 786440 | tf_op jit(solution)/shard_map/ppermute | solution.py:302
  61.8 28.2 %collective-permute-start.9 = (bf16[2,3,8,32,128]{4,3,2,1,0:T(8,128)(2,1)S(1)}, bf16[2,3,8,32,128]{4,3,2,1,0:T(8,128)(2,1)S(1)}, u32[]{:S(2)}, u32[]{:S(2)}) collective-permute-start(bf16[2,3,8,32,128]{4,3,2,1,0:T(8,128)(2,1)S(1)} %get-tuple-element.94.refs_0_), channel_id=1, source_target_pairs={{0,4},{4,0},{8,12},{12,8},{1,5},{5,1},{9,13},{13,9},{2,6},{6,2},{1... | collective-permute-start | bytes 1179656 | tf_op jit(solution)/shard_map/ppermute | solution.py:302
  62.0 27.9 %collective-permute-start.10 = (bf16[2,3,8,32,128]{4,3,2,1,0:T(8,128)(2,1)S(1)}, bf16[2,3,8,32,128]{4,3,2,1,0:T(8,128)(2,1)S(1)}, u32[]{:S(2)}, u32[]{:S(2)}) collective-permute-start(bf16[2,3,8,32,128]{4,3,2,1,0:T(8,128)(2,1)S(1)} %collective-permute-done.6.refs_2_), channel_id=1, source_target_pairs={{0,4},{4,0},{8,12},{12,8},{1,5},{5,1},{9,13},{13,9},{2,6},{6,2},{1... | collective-permute-start | bytes 1179656 | tf_op jit(solution)/shard_map/ppermute | solution.py:302
  63.8 26.2 %collective-permute-start.11 = (bf16[2,3,8,32,128]{4,3,2,1,0:T(8,128)(2,1)S(1)}, bf16[2,3,8,32,128]{4,3,2,1,0:T(8,128)(2,1)S(1)}, u32[]{:S(2)}, u32[]{:S(2)}) collective-permute-start(bf16[2,3,8,32,128]{4,3,2,1,0:T(8,128)(2,1)S(1)} %get-tuple-element.103.refs_0_), channel_id=1, source_target_pairs={{0,8},{4,12},{8,0},{12,4},{1,9},{5,13},{9,1},{13,5},{2,10},{6,14},... | collective-permute-start | bytes 1179656 | tf_op jit(solution)/shard_map/ppermute | solution.py:302
  65.1 2.9 %copy-start.2 = (bf16[5,5,8,64,256]{4,3,1,0,2:T(8,128)(2,1)S(1)}, bf16[5,5,8,64,256]{4,3,1,0,2:T(8,128)(2,1)}, u32[]{:S(2)}) copy-start(bf16[5,5,8,64,256]{4,3,1,0,2:T(8,128)(2,1)} %copy.35) | copy-start | bytes 19660804
  68.9 1.2 copy-start.5
  73.3 20.5 %copy-start.6 = (bf16[4,512,256]{2,1,0:T(8,128)(2,1)S(1)}, bf16[4,512,256]{2,1,0:T(8,128)(2,1)}, u32[]{:S(2)}) copy-start(bf16[4,512,256]{2,1,0:T(8,128)(2,1)} %constant.30.refs_10_) | copy-start | bytes 3145732
  73.3 20.5 %copy-start.8 = (bf16[4,256,512]{2,1,0:T(8,128)(2,1)S(1)}, bf16[4,256,512]{2,1,0:T(8,128)(2,1)}, u32[]{:S(2)}) copy-start(bf16[4,256,512]{2,1,0:T(8,128)(2,1)} %constant.29.refs_9_) | copy-start | bytes 3145732
  73.3 20.5 %copy-start.10 = (bf16[4,128,256]{2,1,0:T(8,128)(2,1)S(1)}, bf16[4,128,256]{2,1,0:T(8,128)(2,1)}, u32[]{:S(2)}) copy-start(bf16[4,128,256]{2,1,0:T(8,128)(2,1)} %constant.31.refs_11_) | copy-start | bytes 786436
  73.3 20.5 %copy-start.12 = (bf16[4,256,128]{2,1,0:T(8,128)(2,1)S(1)}, bf16[4,256,128]{2,1,0:T(8,128)(2,1)}, u32[]{:S(2)}) copy-start(bf16[4,256,128]{2,1,0:T(8,128)(2,1)} %constant.28.refs_8_) | copy-start | bytes 786436
  90.0 29.7 %collective-permute-start.12 = (bf16[2,3,8,32,128]{4,3,2,1,0:T(8,128)(2,1)S(1)}, bf16[2,3,8,32,128]{4,3,2,1,0:T(8,128)(2,1)S(1)}, u32[]{:S(2)}, u32[]{:S(2)}) collective-permute-start(bf16[2,3,8,32,128]{4,3,2,1,0:T(8,128)(2,1)S(1)} %get-tuple-element.103.refs_0_), channel_id=1, source_target_pairs={{0,4},{4,0},{8,12},{12,8},{1,5},{5,1},{9,13},{13,9},{2,6},{6,2},{1... | collective-permute-start | bytes 1179656 | tf_op jit(solution)/shard_map/ppermute | solution.py:302
  91.8 28.0 %collective-permute-start.13 = (bf16[2,3,8,32,128]{4,3,2,1,0:T(8,128)(2,1)S(1)}, bf16[2,3,8,32,128]{4,3,2,1,0:T(8,128)(2,1)S(1)}, u32[]{:S(2)}, u32[]{:S(2)}) collective-permute-start(bf16[2,3,8,32,128]{4,3,2,1,0:T(8,128)(2,1)S(1)} %collective-permute-done.11.refs_2_), channel_id=1, source_target_pairs={{0,4},{4,0},{8,12},{12,8},{1,5},{5,1},{9,13},{13,9},{2,6},{6,2},{1... | collective-permute-start | bytes 1179656 | tf_op jit(solution)/shard_map/ppermute | solution.py:302
  92.1 27.7 %collective-permute-start.14 = (bf16[2,4,8,32,128]{4,3,2,1,0:T(8,128)(2,1)S(1)}, bf16[2,4,8,32,128]{4,3,2,1,0:T(8,128)(2,1)S(1)}, u32[]{:S(2)}, u32[]{:S(2)}) collective-permute-start(bf16[2,4,8,32,128]{4,3,2,1,0:T(8,128)(2,1)S(1)} %slice.75.refs_0_), channel_id=1, source_target_pairs={{0,8},{4,12},{8,0},{12,4},{1,9},{5,13},{9,1},{13,5},{2,10},{6,14},... | collective-permute-start | bytes 1572872 | tf_op jit(solution)/shard_map/ppermute | solution.py:302
  119.8 28.2 %collective-permute-start.15 = (bf16[2,4,8,32,128]{4,3,2,1,0:T(8,128)(2,1)S(1)}, bf16[2,4,8,32,128]{4,3,2,1,0:T(8,128)(2,1)S(1)}, u32[]{:S(2)}, u32[]{:S(2)}) collective-permute-start(bf16[2,4,8,32,128]{4,3,2,1,0:T(8,128)(2,1)S(1)} %slice.75.refs_0_), channel_id=1, source_target_pairs={{0,4},{4,0},{8,12},{12,8},{1,5},{5,1},{9,13},{13,9},{2,6},{6,2},{1... | collective-permute-start | bytes 1572872 | tf_op jit(solution)/shard_map/ppermute | solution.py:302
  121.3 26.8 %collective-permute-start.16 = (bf16[2,4,8,32,128]{4,3,2,1,0:T(8,128)(2,1)S(1)}, bf16[2,4,8,32,128]{4,3,2,1,0:T(8,128)(2,1)S(1)}, u32[]{:S(2)}, u32[]{:S(2)}) collective-permute-start(bf16[2,4,8,32,128]{4,3,2,1,0:T(8,128)(2,1)S(1)} %collective-permute-done.14.refs_2_), channel_id=1, source_target_pairs={{0,4},{4,0},{8,12},{12,8},{1,5},{5,1},{9,13},{13,9},{2,6},{6,2},{1... | collective-permute-start | bytes 1572872 | tf_op jit(solution)/shard_map/ppermute | solution.py:302
  180.6 3.1 %collective-permute-start.17 = (bf16[2,2,2,2,5,2,32,128]{7,6,5,4,3,2,1,0:T(8,128)(2,1)S(1)}, bf16[2,2,2,2,5,2,32,128]{7,6,5,4,3,2,1,0:T(8,128)(2,1)S(1)}, u32[]{:S(2)}, u32[]{:S(2)}) collective-permute-start(bf16[2,2,2,2,5,2,32,128]{7,6,5,4,3,2,1,0:T(8,128)(2,1)S(1)} %get-tuple-element.116), channel_id=1, source_target_pairs={{0,1},{1,0},{2,3},{3,2},{4,5},{5,4},{6,7},{7,6},{8,9},{9,8},{10,11... | collective-permute-start | bytes 3932168 | tf_op jit(solution)/shard_map/ppermute | solution.py:302
  184.3 9.8 %collective-permute-start.18 = (bf16[2,2,5,2,32,128]{5,4,3,2,1,0:T(8,128)(2,1)S(1)}, bf16[2,2,5,2,32,128]{5,4,3,2,1,0:T(8,128)(2,1)S(1)}, u32[]{:S(2)}, u32[]{:S(2)}) collective-permute-start(bf16[2,2,5,2,32,128]{5,4,3,2,1,0:T(8,128)(2,1)S(1)} %get-tuple-element.121), channel_id=1, source_target_pairs={{0,2},{1,3},{2,0},{3,1},{4,6},{5,7},{6,4},{7,5},{8,10},{9,11},{10,... | collective-permute-start | bytes 983048 | tf_op jit(solution)/shard_map/ppermute | solution.py:302
  184.9 25.3 %copy-start.14 = (f32[2,5,2,32,128]{4,3,2,1,0:T(8,128)S(1)}, f32[2,5,2,32,128]{4,3,2,1,0:T(8,128)}, u32[]{:S(2)}) copy-start(f32[2,5,2,32,128]{4,3,2,1,0:T(8,128)} %param.15) | copy-start | bytes 983044
  184.9 9.5 %collective-permute-start.20 = (bf16[2,2,5,2,32,128]{5,4,3,2,1,0:T(8,128)(2,1)S(1)}, bf16[2,2,5,2,32,128]{5,4,3,2,1,0:T(8,128)(2,1)S(1)}, u32[]{:S(2)}, u32[]{:S(2)}) collective-permute-start(bf16[2,2,5,2,32,128]{5,4,3,2,1,0:T(8,128)(2,1)S(1)} %get-tuple-element.122), channel_id=1, source_target_pairs={{0,4},{4,0},{8,12},{12,8},{1,5},{5,1},{9,13},{13,9},{2,6},{6,2},{1... | collective-permute-start | bytes 983048 | tf_op jit(solution)/shard_map/ppermute | solution.py:302
  194.4 16.6 %copy-start.1 = (bf16[2,5,8,32,128]{4,3,2,1,0:T(8,128)(2,1)S(1)}, bf16[2,5,8,32,128]{4,3,2,1,0:T(8,128)(2,1)}, u32[]{:S(2)}) copy-start(bf16[2,5,8,32,128]{4,3,2,1,0:T(8,128)(2,1)} %param.10) | copy-start | bytes 1966084
  194.6 5.4 %collective-permute-start.21 = (bf16[2,5,2,32,128]{4,3,2,1,0:T(8,128)(2,1)S(1)}, bf16[2,5,2,32,128]{4,3,2,1,0:T(8,128)(2,1)S(1)}, u32[]{:S(2)}, u32[]{:S(2)}) collective-permute-start(bf16[2,5,2,32,128]{4,3,2,1,0:T(8,128)(2,1)S(1)} %slice_bitcast_fusion.4), channel_id=1, source_target_pairs={{0,2},{1,3},{2,0},{3,1},{4,6},{5,7},{6,4},{7,5},{8,10},{9,11},{10,... | collective-permute-start | bytes 491528 | tf_op jit(solution)/shard_map/ppermute | solution.py:302
  196.2 5.4 %collective-permute-start.19 = (bf16[2,5,2,32,128]{4,3,2,1,0:T(8,128)(2,1)S(1)}, bf16[2,5,2,32,128]{4,3,2,1,0:T(8,128)(2,1)S(1)}, u32[]{:S(2)}, u32[]{:S(2)}) collective-permute-start(bf16[2,5,2,32,128]{4,3,2,1,0:T(8,128)(2,1)S(1)} %slice_bitcast_fusion.6), channel_id=1, source_target_pairs={{0,4},{4,0},{8,12},{12,8},{1,5},{5,1},{9,13},{13,9},{2,6},{6,2},{1... | collective-permute-start | bytes 491528 | tf_op jit(solution)/shard_map/ppermute | solution.py:302
  201.7 8.4 %collective-permute-start.22 = (bf16[2,5,2,32,128]{4,3,2,1,0:T(8,128)(2,1)S(1)}, bf16[2,5,2,32,128]{4,3,2,1,0:T(8,128)(2,1)S(1)}, u32[]{:S(2)}, u32[]{:S(2)}) collective-permute-start(bf16[2,5,2,32,128]{4,3,2,1,0:T(8,128)(2,1)S(1)} %pad_maximum_fusion.2), channel_id=1, source_target_pairs={{0,8},{4,12},{8,0},{12,4},{1,9},{5,13},{9,1},{13,5},{2,10},{6,14},... | collective-permute-start | bytes 491528 | tf_op jit(solution)/shard_map/ppermute | solution.py:302
  (6 other events, 5.9 us)

commit v4 on v3

--- a/solution.py
+++ b/solution.py
@@ -325,16 +325,19 @@
         orders = orders[:1]
     tx = np.stack([tx[:, list(o)] for o in orders])
     tix = np.stack([tix[:, :, list(o)] for o in orders])
-    if not butterfly:
-        ty = lax.dynamic_slice_in_dim(jnp.asarray(ty), here, 1, 0)
-        tiy = lax.dynamic_slice_in_dim(jnp.asarray(tiy), here, 1, 0)
     tables = [
-        jnp.asarray(ty).reshape(-1, 2 * ny, 2 * width),
-        jnp.asarray(tx).reshape(-1, 2 * nx, 4 * nx),
-        jnp.asarray(tix).reshape(-1, 4 * nx, 2 * nx),
-        jnp.asarray(tiy).reshape(-1, 2 * width, 2 * ny),
+        ty.reshape(-1, 2 * ny, 2 * width),
+        tx.reshape(-1, 2 * nx, 4 * nx),
+        tix.reshape(-1, 4 * nx, 2 * nx),
+        tiy.reshape(-1, 2 * width, 2 * ny),
     ]
-    where = jnp.stack([here if butterfly else 0 * here, me]).astype(jnp.int32)
+    tables = [
+        jnp.asarray(t)
+        if t.shape[0] == 1
+        else lax.dynamic_index_in_dim(jnp.asarray(t), here, 0, keepdims=True)
+        for t in tables
+    ]
+    where = jnp.stack([0 * here, me]).astype(jnp.int32)
     weights = kernel_weights(sampled, basis_products, point_spread, width - own)
     count = coil_maps.shape[1]
 
@@ -348,7 +351,7 @@
 
         mine = lax.dynamic_slice_in_dim(basis_image, me * (NZ // coil), NZ // coil, 2)
         mine = [mine] + [swap(mine, "dom", r) for r in (1, 2, 3)]
-        mine, weights[0], parts = fence((mine, weights[0], parts))
+        mine, weights[0], parts, tables = fence((mine, weights[0], parts, tables))
         mine = jnp.stack(mine)
         there = swap(mine, "coil", 2)
         one, two = swap(parts[0], "dom", 1), swap(parts[0], "dom", 2)

time: 212 us -> 205 us (0.967)
  Pallas kernels: 101 us -> 89.7 us
  waiting for transfers between devices: 51.2 us -> 61.5 us
  local copies, waits for them, and re-layouts: 20.7 us -> 16 us
    pallas_call x4, Pallas kernels: 101 us -> 89.7 us  [coils(): pl.pallas_call(functools.partial(coils_kernel, width, len(maps), len(imag...]
    ppermute x23, waiting for transfers between devices: 51.2 us -> 61.5 us  [swap(): return lax.ppermute(value, axis, [(i, i ^ bit) for i in range(size)])]
    dynamic_slice x0 -> x4, local copies, waits for them, and re-layouts: none -> 3.99 us  [body(): lax.dynamic_index_in_dim(jnp.asarray(t), here, 0, keepdims=True)]
    unnamed x30 -> x22, local copies, waits for them, and re-layouts: 9.83 us -> 5.88 us
    dot_general x2, local copies, waits for them, and re-layouts: 8.59 us -> 5.88 us  [kernel_weights(): jnp.einsum('gikjq,givu->qkjvu', jnp.stack(pair, 1).astype(BF), spread, pr...]
  transfers between devices with their start and end apart: 23 -> 23, of which waited for: 10 -> 12; matrix products, arithmetic and copies ran while one was open for 9% -> 9% of each run, Pallas kernels for 33% -> 30%
where the time goes in v4:
time: 205 us
  Pallas kernels  89.7 us (44%)
  waiting for transfers between devices  61.5 us (30%)
  starting transfers between devices  26.7 us (13%)
  local copies, waits for them, and re-layouts  16 us (8%)
  other arithmetic  6.81 us (3%)
  matrix products  3.92 us (2%)
    pallas_call x4, Pallas kernels, coils(): pl.pallas_call(functools.partial(coils_kernel, width, len(maps), len(imag...  89.7 us
    ppermute x23, waiting for transfers between devices, swap(): return lax.ppermute(value, axis, [(i, i ^ bit) for i in range(size)])  61.5 us
    ppermute x23, starting transfers between devices, swap(): return lax.ppermute(value, axis, [(i, i ^ bit) for i in range(size)])  26.7 us
    dot_general x2, local copies, waits for them, and re-layouts, kernel_weights(): jnp.einsum('gikjq,givu->qkjvu', jnp.stack(pair, 1).astype(BF), spread, pr...  5.88 us
    unnamed x22, local copies, waits for them, and re-layouts  5.88 us
  transfers between devices with their start and end apart: 23, of which 12 were waited for; matrix products, arithmetic and copies ran while one was open for 9% of the time, Pallas kernels for 30%

profile of v4, /device:TPU:0, one launch (start us, length us, event | category | flops | bytes accessed | tf_op | source)
XLA Modules:
  0.0 204.9 jit_solution(15802882563164740687)
XLA Ops:
  1.1 5.1 %collective-permute-start.2 = (bf16[2,5,2,32,128]{4,3,2,1,0:T(8,128)(2,1)S(1)}, bf16[2,5,2,32,128]{4,3,2,1,0:T(8,128)(2,1)S(1)}, u32[]{:S(2)}, u32[]{:S(2)}) collective-permute-start(bf16[2,5,2,32,128]{4,3,2,1,0:T(8,128)(2,1)S(1)} %constant_dynamic-slice_fusion.4), channel_id=1, source_target_pairs={{0,12},{4,8},{8,4},{12,0},{1,13},{5,9},{9,5},{13,1},{2,14},{6,10},... | collective-permute-start | bytes 491528 | tf_op jit(solution)/shard_map/ppermute | solution.py:302
  10.3 2.5 %convert_bitcast_fusion = bf16[32,2,64,256,1,1]{3,2,1,0,5,4:T(8,128)(2,1)S(1)} fusion(f32[32,2,64,256]{3,2,1,0:T(8,128)} %param.12), kind=kLoop, calls=%fused_computation.7 | loop fusion | flops 1048576 | bytes 6291456 | tf_op jit(solution)/shard_map/convert_element_type | solution.py:286
  12.8 2.0 convolution_bitcast_fusion.1
  15.7 1.6 copy.35
  18.6 1.5 collective-permute-done.1
  21.1 1.5 collective-permute-start.3
  23.4 2.1 %collective-permute-start.5 = (bf16[2,2,8,32,128]{4,3,2,1,0:T(8,128)(2,1)S(1)}, bf16[2,2,8,32,128]{4,3,2,1,0:T(8,128)(2,1)S(1)}, u32[]{:S(2)}, u32[]{:S(2)}) collective-permute-start(bf16[2,2,8,32,128]{4,3,2,1,0:T(8,128)(2,1)S(1)} %slice.72.refs_0_), channel_id=1, source_target_pairs={{0,8},{4,12},{8,0},{12,4},{1,9},{5,13},{9,1},{13,5},{2,10},{6,14},... | collective-permute-start | bytes 786440 | tf_op jit(solution)/shard_map/ppermute | solution.py:302
  25.7 2.0 convolution_bitcast_fusion
  27.6 4.3 %copy.36 = bf16[5,5,8,64,256]{4,3,1,0,2:T(8,128)(2,1)} copy(bf16[5,5,8,64,256]{4,2,3,1,0:T(8,128)(2,1)S(1)} %convolution_bitcast_fusion) | data formatting | bytes 13107200 | tf_op jit(solution)/shard_map/gikjq,givu->qkjvu/dot_general | solution.py:290
  31.9 20.8 %collective-permute-done.5.refs_2_ = bf16[2,2,8,32,128]{4,3,2,1,0:T(8,128)(2,1)S(1)} collective-permute-done((bf16[2,2,8,32,128]{4,3,2,1,0:T(8,128)(2,1)S(1)}, bf16[2,2,8,32,128]{4,3,2,1,0:T(8,128)(2,1)S(1)}, u32[]{:S(2)}, u32[]{:S(2)}) %collective-permute-start.5) | collective-permute-done | bytes 262176 | tf_op jit(solution)/shard_map/ppermute | solution.py:302
  53.1 8.6 %collective-permute-done.8.refs_3_ = bf16[2,2,8,32,128]{4,3,2,1,0:T(8,128)(2,1)S(1)} collective-permute-done((bf16[2,2,8,32,128]{4,3,2,1,0:T(8,128)(2,1)S(1)}, bf16[2,2,8,32,128]{4,3,2,1,0:T(8,128)(2,1)S(1)}, u32[]{:S(2)}, u32[]{:S(2)}) %collective-permute-start.8) | collective-permute-done | bytes 262176 | tf_op jit(solution)/shard_map/ppermute | solution.py:302
  61.9 1.8 collective-permute-start.10
  64.6 16.0 %shard_map.100.refs_12_ = f32[8,2,5,128,128]{4,3,2,1,0:T(8,128)S(1)} custom-call(s32[2]{0:T(128)S(1)} %pad_add_fusion.where, bf16[2,2,8,32,128]{4,3,2,1,0:T(8,128)(2,1)S(1)} %slice.72.refs_0_, bf16[2,2,8,32,128]{4,3,2,1,0:T(8,128)(2,1)S(1)} %collective-permute-done.4.refs_1_, bf16[2,2,8,32,128]{4,3,2,1,0:T(8,128)(2,1)S(1)} %collective-permute-done.5.refs_2_, ...), custom_call_target="tpu_custom_call" | custom-call | flops 8192000000 | bytes 30000000 | tf_op jit(solution)/shard_map/pallas_call | solution.py:263
  80.7 1.4 collective-permute-done.9.refs_1_
  82.1 7.1 %collective-permute-done.10.refs_3_ = bf16[2,3,8,32,128]{4,3,2,1,0:T(8,128)(2,1)S(1)} collective-permute-done((bf16[2,3,8,32,128]{4,3,2,1,0:T(8,128)(2,1)S(1)}, bf16[2,3,8,32,128]{4,3,2,1,0:T(8,128)(2,1)S(1)}, u32[]{:S(2)}, u32[]{:S(2)}) %collective-permute-start.10) | collective-permute-done | bytes 393248 | tf_op jit(solution)/shard_map/ppermute | solution.py:302
  91.2 1.4 collective-permute-start.14
  92.5 22.3 %shard_map.101.refs_12_ = f32[8,2,5,128,128]{4,3,2,1,0:T(8,128)S(1)} custom-call(s32[2]{0:T(128)S(1)} %pad_add_fusion.where, bf16[2,3,8,32,128]{4,3,2,1,0:T(8,128)(2,1)S(1)} %get-tuple-element.102.refs_0_, bf16[2,3,8,32,128]{4,3,2,1,0:T(8,128)(2,1)S(1)} %collective-permute-done.9.refs_1_, bf16[2,3,8,32,128]{4,3,2,1,0:T(8,128)(2,1)S(1)} %collective-permute-done.6.refs_2_, ...), custom_call_target="tpu_custom_call" | custom-call | flops 12288000000 | bytes 30000000 | tf_op jit(solution)/shard_map/pallas_call | solution.py:263
  114.8 2.3 %copy-done.3 = f32[8,2,5,128,128]{4,3,2,1,0:T(8,128)} copy-done((f32[8,2,5,128,128]{4,3,2,1,0:T(8,128)}, f32[8,2,5,128,128]{4,3,2,1,0:T(8,128)S(1)}, u32[]{:S(2)}) %copy-start.3) | copy-done | bytes 5242904
  117.1 1.5 collective-permute-done.13.refs_3_
  118.6 1.6 collective-permute-start.15
  120.6 2.5 %copy-done.4 = f32[8,2,5,128,128]{4,3,2,1,0:T(8,128)S(1)} copy-done((f32[8,2,5,128,128]{4,3,2,1,0:T(8,128)S(1)}, f32[8,2,5,128,128]{4,3,2,1,0:T(8,128)}, u32[]{:S(2)}) %copy-start.4) | copy-done | bytes 5242904
  123.1 22.5 %shard_map.102.refs_12_ = f32[8,2,5,128,128]{4,3,2,1,0:T(8,128)S(1)} custom-call(s32[2]{0:T(128)S(1)} %pad_add_fusion.where, bf16[2,3,8,32,128]{4,3,2,1,0:T(8,128)(2,1)S(1)} %get-tuple-element.111.refs_0_, bf16[2,3,8,32,128]{4,3,2,1,0:T(8,128)(2,1)S(1)} %collective-permute-done.12.refs_1_, bf16[2,3,8,32,128]{4,3,2,1,0:T(8,128)(2,1)S(1)} %collective-permute-done.11.refs_2_, ...), custom_call_target="tpu_custom_call" | custom-call | flops 12288000000 | bytes 30000000 | tf_op jit(solution)/shard_map/pallas_call | solution.py:263
  145.7 28.9 %shard_map.103 = (bf16[2,2,2,2,5,2,32,128]{7,6,5,4,3,2,1,0:T(8,128)(2,1)S(1)}, bf16[2,2,2,2,5,2,32,128]{7,6,5,4,3,2,1,0:T(8,128)(2,1)S(1)}) custom-call(s32[2]{0:T(128)S(1)} %pad_add_fusion.where, bf16[2,4,8,32,128]{4,3,2,1,0:T(8,128)(2,1)S(1)} %slice.75.refs_0_, bf16[2,4,8,32,128]{4,3,2,1,0:T(8,128)(2,1)S(1)} %collective-permute-done.15.refs_1_, ...), custom_call_target="tpu_custom_call" | custom-call | flops 16384000000 | bytes 30000000 | tf_op jit(solution)/shard_map/pallas_call | solution.py:263
  174.7 3.0 %collective-permute-done.17 = bf16[2,2,2,2,5,2,32,128]{7,6,5,4,3,2,1,0:T(8,128)(2,1)S(1)} collective-permute-done((bf16[2,2,2,2,5,2,32,128]{7,6,5,4,3,2,1,0:T(8,128)(2,1)S(1)}, bf16[2,2,2,2,5,2,32,128]{7,6,5,4,3,2,1,0:T(8,128)(2,1)S(1)}, u32[]{:S(2)}, u32[]{:S(2)}) %collective-permute-start.17) | collective-permute-done | bytes 1310752 | tf_op jit(solution)/shard_map/ppermute | solution.py:302
  178.9 1.6 collective-permute-start.20
  180.4 7.6 %collective-permute-done.18 = bf16[2,2,5,2,32,128]{5,4,3,2,1,0:T(8,128)(2,1)S(1)} collective-permute-done((bf16[2,2,5,2,32,128]{5,4,3,2,1,0:T(8,128)(2,1)S(1)}, bf16[2,2,5,2,32,128]{5,4,3,2,1,0:T(8,128)(2,1)S(1)}, u32[]{:S(2)}, u32[]{:S(2)}) %collective-permute-start.18) | collective-permute-done | bytes 327712 | tf_op jit(solution)/shard_map/ppermute | solution.py:302
  188.6 1.6 collective-permute-start.21
  190.2 1.6 collective-permute-start.19
  191.8 2.2 %collective-permute-done.21 = bf16[2,5,2,32,128]{4,3,2,1,0:T(8,128)(2,1)S(1)} collective-permute-done((bf16[2,5,2,32,128]{4,3,2,1,0:T(8,128)(2,1)S(1)}, bf16[2,5,2,32,128]{4,3,2,1,0:T(8,128)(2,1)S(1)}, u32[]{:S(2)}, u32[]{:S(2)}) %collective-permute-start.21) | collective-permute-done | bytes 163872 | tf_op jit(solution)/shard_map/ppermute | solution.py:302
  194.1 1.5 collective-permute-done.19
  195.7 2.3 %collective-permute-start.22 = (bf16[2,5,2,32,128]{4,3,2,1,0:T(8,128)(2,1)S(1)}, bf16[2,5,2,32,128]{4,3,2,1,0:T(8,128)(2,1)S(1)}, u32[]{:S(2)}, u32[]{:S(2)}) collective-permute-start(bf16[2,5,2,32,128]{4,3,2,1,0:T(8,128)(2,1)S(1)} %pad_maximum_fusion.2), channel_id=1, source_target_pairs={{0,8},{4,12},{8,0},{12,4},{1,9},{5,13},{9,1},{13,5},{2,10},{6,14},... | collective-permute-start | bytes 491528 | tf_op jit(solution)/shard_map/ppermute | solution.py:302
  198.0 6.1 %collective-permute-done.22 = bf16[2,5,2,32,128]{4,3,2,1,0:T(8,128)(2,1)S(1)} collective-permute-done((bf16[2,5,2,32,128]{4,3,2,1,0:T(8,128)(2,1)S(1)}, bf16[2,5,2,32,128]{4,3,2,1,0:T(8,128)(2,1)S(1)}, u32[]{:S(2)}, u32[]{:S(2)}) %collective-permute-start.22) | collective-permute-done | bytes 163872 | tf_op jit(solution)/shard_map/ppermute | solution.py:302
  (73 shorter events, 16.1 us)
Async XLA Ops:
  0.0 10.2 %copy-start.7 = (bf16[2,12,8,32,128]{4,3,2,1,0:T(8,128)(2,1)S(1)}, bf16[2,12,8,32,128]{4,3,2,1,0:T(8,128)(2,1)}, u32[]{:S(2)}) copy-start(bf16[2,12,8,32,128]{4,3,2,1,0:T(8,128)(2,1)} %param.11) | copy-start | bytes 4718596
  1.1 17.5 %collective-permute-start.2 = (bf16[2,5,2,32,128]{4,3,2,1,0:T(8,128)(2,1)S(1)}, bf16[2,5,2,32,128]{4,3,2,1,0:T(8,128)(2,1)S(1)}, u32[]{:S(2)}, u32[]{:S(2)}) collective-permute-start(bf16[2,5,2,32,128]{4,3,2,1,0:T(8,128)(2,1)S(1)} %constant_dynamic-slice_fusion.4), channel_id=1, source_target_pairs={{0,12},{4,8},{8,4},{12,0},{1,13},{5,9},{9,5},{13,1},{2,14},{6,10},... | collective-permute-start | bytes 491528 | tf_op jit(solution)/shard_map/ppermute | solution.py:302
  6.2 13.9 %collective-permute-start.1 = (bf16[2,5,2,32,128]{4,3,2,1,0:T(8,128)(2,1)S(1)}, bf16[2,5,2,32,128]{4,3,2,1,0:T(8,128)(2,1)S(1)}, u32[]{:S(2)}, u32[]{:S(2)}) collective-permute-start(bf16[2,5,2,32,128]{4,3,2,1,0:T(8,128)(2,1)S(1)} %constant_dynamic-slice_fusion.4), channel_id=1, source_target_pairs={{0,8},{4,12},{8,0},{12,4},{1,9},{5,13},{9,1},{13,5},{2,10},{6,14},... | collective-permute-start | bytes 491528 | tf_op jit(solution)/shard_map/ppermute | solution.py:302
  6.2 13.9 %collective-permute-start = (bf16[2,5,2,32,128]{4,3,2,1,0:T(8,128)(2,1)S(1)}, bf16[2,5,2,32,128]{4,3,2,1,0:T(8,128)(2,1)S(1)}, u32[]{:S(2)}, u32[]{:S(2)}) collective-permute-start(bf16[2,5,2,32,128]{4,3,2,1,0:T(8,128)(2,1)S(1)} %constant_dynamic-slice_fusion.4), channel_id=1, source_target_pairs={{0,4},{4,0},{8,12},{12,8},{1,5},{5,1},{9,13},{13,9},{2,6},{6,2},{1... | collective-permute-start | bytes 491528 | tf_op jit(solution)/shard_map/ppermute | solution.py:302
  17.2 47.4 %copy-start.2 = (bf16[5,5,8,64,256]{4,3,1,0,2:T(8,128)(2,1)}, bf16[5,5,8,64,256]{4,3,1,0,2:T(8,128)(2,1)S(1)}, u32[]{:S(2)}) copy-start(bf16[5,5,8,64,256]{4,3,1,0,2:T(8,128)(2,1)S(1)} %copy.35) | copy-start | bytes 19660804
  17.3 8.4 %copy-start.6 = (bf16[32,2,64,256,1,1]{3,2,1,0,5,4:T(8,128)(2,1)S(1)}, bf16[32,2,64,256,1,1]{3,2,1,0,5,4:T(8,128)(2,1)}, u32[]{:S(2)}) copy-start(bf16[32,2,64,256,1,1]{3,2,1,0,5,4:T(8,128)(2,1)} %copy-done.5) | copy-start | bytes 6291460
  21.1 31.6 %collective-permute-start.3 = (bf16[4,2,5,2,32,128]{5,4,3,2,1,0:T(8,128)(2,1)}, bf16[4,2,5,2,32,128]{5,4,3,2,1,0:T(8,128)(2,1)S(1)}, u32[]{:S(2)}, u32[]{:S(2)}) collective-permute-start(bf16[4,2,5,2,32,128]{5,4,3,2,1,0:T(8,128)(2,1)} %get-tuple-element.132), channel_id=1, source_target_pairs={{0,2},{1,3},{2,0},{3,1},{4,6},{5,7},{6,4},{7,5},{8,10},{9,11},{10,... | collective-permute-start | bytes 1966088 | tf_op jit(solution)/shard_map/ppermute | solution.py:302
  22.6 30.1 %collective-permute-start.6 = (bf16[2,3,8,32,128]{4,3,2,1,0:T(8,128)(2,1)S(1)}, bf16[2,3,8,32,128]{4,3,2,1,0:T(8,128)(2,1)S(1)}, u32[]{:S(2)}, u32[]{:S(2)}) collective-permute-start(bf16[2,3,8,32,128]{4,3,2,1,0:T(8,128)(2,1)S(1)} %get-tuple-element.102.refs_0_), channel_id=1, source_target_pairs={{0,8},{4,12},{8,0},{12,4},{1,9},{5,13},{9,1},{13,5},{2,10},{6,14},... | collective-permute-start | bytes 1179656 | tf_op jit(solution)/shard_map/ppermute | solution.py:302
  23.4 29.3 %collective-permute-start.5 = (bf16[2,2,8,32,128]{4,3,2,1,0:T(8,128)(2,1)S(1)}, bf16[2,2,8,32,128]{4,3,2,1,0:T(8,128)(2,1)S(1)}, u32[]{:S(2)}, u32[]{:S(2)}) collective-permute-start(bf16[2,2,8,32,128]{4,3,2,1,0:T(8,128)(2,1)S(1)} %slice.72.refs_0_), channel_id=1, source_target_pairs={{0,8},{4,12},{8,0},{12,4},{1,9},{5,13},{9,1},{13,5},{2,10},{6,14},... | collective-permute-start | bytes 786440 | tf_op jit(solution)/shard_map/ppermute | solution.py:302
  25.5 27.2 %collective-permute-start.4 = (bf16[2,2,8,32,128]{4,3,2,1,0:T(8,128)(2,1)S(1)}, bf16[2,2,8,32,128]{4,3,2,1,0:T(8,128)(2,1)S(1)}, u32[]{:S(2)}, u32[]{:S(2)}) collective-permute-start(bf16[2,2,8,32,128]{4,3,2,1,0:T(8,128)(2,1)S(1)} %slice.72.refs_0_), channel_id=1, source_target_pairs={{0,4},{4,0},{8,12},{12,8},{1,5},{5,1},{9,13},{13,9},{2,6},{6,2},{1... | collective-permute-start | bytes 786440 | tf_op jit(solution)/shard_map/ppermute | solution.py:302
  52.8 8.8 %collective-permute-start.7 = (bf16[2,4,2,5,2,32,128]{6,5,4,3,2,1,0:T(8,128)(2,1)S(1)}, bf16[2,4,2,5,2,32,128]{6,5,4,3,2,1,0:T(8,128)(2,1)S(1)}, u32[]{:S(2)}, u32[]{:S(2)}) collective-permute-start(bf16[2,4,2,5,2,32,128]{6,5,4,3,2,1,0:T(8,128)(2,1)S(1)} %pad_maximum_fusion.refs_4_), channel_id=1, source_target_pairs={{0,1},{1,0},{2,3},{3,2},{4,5},{5,4},{6,7},{7,6},{8,9},{9,8},{10,11... | collective-permute-start | bytes 3932168 | tf_op jit(solution)/shard_map/ppermute | solution.py:302
  52.9 8.7 %collective-permute-start.8 = (bf16[2,2,8,32,128]{4,3,2,1,0:T(8,128)(2,1)S(1)}, bf16[2,2,8,32,128]{4,3,2,1,0:T(8,128)(2,1)S(1)}, u32[]{:S(2)}, u32[]{:S(2)}) collective-permute-start(bf16[2,2,8,32,128]{4,3,2,1,0:T(8,128)(2,1)S(1)} %collective-permute-done.5.refs_2_), channel_id=1, source_target_pairs={{0,4},{4,0},{8,12},{12,8},{1,5},{5,1},{9,13},{13,9},{2,6},{6,2},{1... | collective-permute-start | bytes 786440 | tf_op jit(solution)/shard_map/ppermute | solution.py:302
  61.6 20.5 %collective-permute-start.9 = (bf16[2,3,8,32,128]{4,3,2,1,0:T(8,128)(2,1)S(1)}, bf16[2,3,8,32,128]{4,3,2,1,0:T(8,128)(2,1)S(1)}, u32[]{:S(2)}, u32[]{:S(2)}) collective-permute-start(bf16[2,3,8,32,128]{4,3,2,1,0:T(8,128)(2,1)S(1)} %get-tuple-element.102.refs_0_), channel_id=1, source_target_pairs={{0,4},{4,0},{8,12},{12,8},{1,5},{5,1},{9,13},{13,9},{2,6},{6,2},{1... | collective-permute-start | bytes 1179656 | tf_op jit(solution)/shard_map/ppermute | solution.py:302
  61.9 27.3 %collective-permute-start.10 = (bf16[2,3,8,32,128]{4,3,2,1,0:T(8,128)(2,1)S(1)}, bf16[2,3,8,32,128]{4,3,2,1,0:T(8,128)(2,1)S(1)}, u32[]{:S(2)}, u32[]{:S(2)}) collective-permute-start(bf16[2,3,8,32,128]{4,3,2,1,0:T(8,128)(2,1)S(1)} %collective-permute-done.6.refs_2_), channel_id=1, source_target_pairs={{0,4},{4,0},{8,12},{12,8},{1,5},{5,1},{9,13},{13,9},{2,6},{6,2},{1... | collective-permute-start | bytes 1179656 | tf_op jit(solution)/shard_map/ppermute | solution.py:302
  63.6 25.5 %collective-permute-start.11 = (bf16[2,3,8,32,128]{4,3,2,1,0:T(8,128)(2,1)S(1)}, bf16[2,3,8,32,128]{4,3,2,1,0:T(8,128)(2,1)S(1)}, u32[]{:S(2)}, u32[]{:S(2)}) collective-permute-start(bf16[2,3,8,32,128]{4,3,2,1,0:T(8,128)(2,1)S(1)} %get-tuple-element.111.refs_0_), channel_id=1, source_target_pairs={{0,8},{4,12},{8,0},{12,4},{1,9},{5,13},{9,1},{13,5},{2,10},{6,14},... | collective-permute-start | bytes 1179656 | tf_op jit(solution)/shard_map/ppermute | solution.py:302
  89.2 28.0 %collective-permute-start.12 = (bf16[2,3,8,32,128]{4,3,2,1,0:T(8,128)(2,1)S(1)}, bf16[2,3,8,32,128]{4,3,2,1,0:T(8,128)(2,1)S(1)}, u32[]{:S(2)}, u32[]{:S(2)}) collective-permute-start(bf16[2,3,8,32,128]{4,3,2,1,0:T(8,128)(2,1)S(1)} %get-tuple-element.111.refs_0_), channel_id=1, source_target_pairs={{0,4},{4,0},{8,12},{12,8},{1,5},{5,1},{9,13},{13,9},{2,6},{6,2},{1... | collective-permute-start | bytes 1179656 | tf_op jit(solution)/shard_map/ppermute | solution.py:302
  90.3 28.3 %collective-permute-start.13 = (bf16[2,3,8,32,128]{4,3,2,1,0:T(8,128)(2,1)S(1)}, bf16[2,3,8,32,128]{4,3,2,1,0:T(8,128)(2,1)S(1)}, u32[]{:S(2)}, u32[]{:S(2)}) collective-permute-start(bf16[2,3,8,32,128]{4,3,2,1,0:T(8,128)(2,1)S(1)} %collective-permute-done.11.refs_2_), channel_id=1, source_target_pairs={{0,4},{4,0},{8,12},{12,8},{1,5},{5,1},{9,13},{13,9},{2,6},{6,2},{1... | collective-permute-start | bytes 1179656 | tf_op jit(solution)/shard_map/ppermute | solution.py:302
  91.2 27.4 %collective-permute-start.14 = (bf16[2,4,8,32,128]{4,3,2,1,0:T(8,128)(2,1)S(1)}, bf16[2,4,8,32,128]{4,3,2,1,0:T(8,128)(2,1)S(1)}, u32[]{:S(2)}, u32[]{:S(2)}) collective-permute-start(bf16[2,4,8,32,128]{4,3,2,1,0:T(8,128)(2,1)S(1)} %slice.75.refs_0_), channel_id=1, source_target_pairs={{0,8},{4,12},{8,0},{12,4},{1,9},{5,13},{9,1},{13,5},{2,10},{6,14},... | collective-permute-start | bytes 1572872 | tf_op jit(solution)/shard_map/ppermute | solution.py:302
  92.5 53.1 %slice-start = ((s8[6553600]{0:T(1024)(128)(4,1)}), s8[4194304]{0:T(1024)(128)(4,1)S(1)}, s32[]{:S(2)}) async-start(s8[6553600]{0:T(1024)(128)(4,1)} %bitcast.64), calls=%async_computation | async-start | bytes 8388608
  114.8 2.3 %copy-start.3 = (f32[8,2,5,128,128]{4,3,2,1,0:T(8,128)}, f32[8,2,5,128,128]{4,3,2,1,0:T(8,128)S(1)}, u32[]{:S(2)}) copy-start(f32[8,2,5,128,128]{4,3,2,1,0:T(8,128)S(1)} %shard_map.101.refs_12_) | copy-start | bytes 15728644
  117.1 28.6 %slice-start.1 = ((s8[6553600]{0:T(1024)(128)(4,1)}), s8[2359296]{0:T(1024)(128)(4,1)S(1)}, s32[]{:S(2)}) async-start(s8[6553600]{0:T(1024)(128)(4,1)} %bitcast.64), calls=%async_computation.1 | async-start | bytes 4718592
  118.6 27.0 %collective-permute-start.15 = (bf16[2,4,8,32,128]{4,3,2,1,0:T(8,128)(2,1)S(1)}, bf16[2,4,8,32,128]{4,3,2,1,0:T(8,128)(2,1)S(1)}, u32[]{:S(2)}, u32[]{:S(2)}) collective-permute-start(bf16[2,4,8,32,128]{4,3,2,1,0:T(8,128)(2,1)S(1)} %slice.75.refs_0_), channel_id=1, source_target_pairs={{0,4},{4,0},{8,12},{12,8},{1,5},{5,1},{9,13},{13,9},{2,6},{6,2},{1... | collective-permute-start | bytes 1572872 | tf_op jit(solution)/shard_map/ppermute | solution.py:302
  120.2 25.5 %collective-permute-start.16 = (bf16[2,4,8,32,128]{4,3,2,1,0:T(8,128)(2,1)S(1)}, bf16[2,4,8,32,128]{4,3,2,1,0:T(8,128)(2,1)S(1)}, u32[]{:S(2)}, u32[]{:S(2)}) collective-permute-start(bf16[2,4,8,32,128]{4,3,2,1,0:T(8,128)(2,1)S(1)} %collective-permute-done.14.refs_2_), channel_id=1, source_target_pairs={{0,4},{4,0},{8,12},{12,8},{1,5},{5,1},{9,13},{13,9},{2,6},{6,2},{1... | collective-permute-start | bytes 1572872 | tf_op jit(solution)/shard_map/ppermute | solution.py:302
  120.6 2.5 %copy-start.4 = (f32[8,2,5,128,128]{4,3,2,1,0:T(8,128)S(1)}, f32[8,2,5,128,128]{4,3,2,1,0:T(8,128)}, u32[]{:S(2)}) copy-start(f32[8,2,5,128,128]{4,3,2,1,0:T(8,128)} %copy-done.3) | copy-start | bytes 15728644
  174.6 3.1 %collective-permute-start.17 = (bf16[2,2,2,2,5,2,32,128]{7,6,5,4,3,2,1,0:T(8,128)(2,1)S(1)}, bf16[2,2,2,2,5,2,32,128]{7,6,5,4,3,2,1,0:T(8,128)(2,1)S(1)}, u32[]{:S(2)}, u32[]{:S(2)}) collective-permute-start(bf16[2,2,2,2,5,2,32,128]{7,6,5,4,3,2,1,0:T(8,128)(2,1)S(1)} %get-tuple-element.124), channel_id=1, source_target_pairs={{0,1},{1,0},{2,3},{3,2},{4,5},{5,4},{6,7},{7,6},{8,9},{9,8},{10,11... | collective-permute-start | bytes 3932168 | tf_op jit(solution)/shard_map/ppermute | solution.py:302
  178.3 9.8 %collective-permute-start.18 = (bf16[2,2,5,2,32,128]{5,4,3,2,1,0:T(8,128)(2,1)S(1)}, bf16[2,2,5,2,32,128]{5,4,3,2,1,0:T(8,128)(2,1)S(1)}, u32[]{:S(2)}, u32[]{:S(2)}) collective-permute-start(bf16[2,2,5,2,32,128]{5,4,3,2,1,0:T(8,128)(2,1)S(1)} %get-tuple-element.129), channel_id=1, source_target_pairs={{0,2},{1,3},{2,0},{3,1},{4,6},{5,7},{6,4},{7,5},{8,10},{9,11},{10,... | collective-permute-start | bytes 983048 | tf_op jit(solution)/shard_map/ppermute | solution.py:302
  178.9 25.3 %copy-start.8 = (f32[2,5,2,32,128]{4,3,2,1,0:T(8,128)S(1)}, f32[2,5,2,32,128]{4,3,2,1,0:T(8,128)}, u32[]{:S(2)}) copy-start(f32[2,5,2,32,128]{4,3,2,1,0:T(8,128)} %param.15) | copy-start | bytes 983044
  178.9 9.5 %collective-permute-start.20 = (bf16[2,2,5,2,32,128]{5,4,3,2,1,0:T(8,128)(2,1)S(1)}, bf16[2,2,5,2,32,128]{5,4,3,2,1,0:T(8,128)(2,1)S(1)}, u32[]{:S(2)}, u32[]{:S(2)}) collective-permute-start(bf16[2,2,5,2,32,128]{5,4,3,2,1,0:T(8,128)(2,1)S(1)} %get-tuple-element.130), channel_id=1, source_target_pairs={{0,4},{4,0},{8,12},{12,8},{1,5},{5,1},{9,13},{13,9},{2,6},{6,2},{1... | collective-permute-start | bytes 983048 | tf_op jit(solution)/shard_map/ppermute | solution.py:302
  188.3 16.6 %copy-start.1 = (bf16[2,5,8,32,128]{4,3,2,1,0:T(8,128)(2,1)S(1)}, bf16[2,5,8,32,128]{4,3,2,1,0:T(8,128)(2,1)}, u32[]{:S(2)}) copy-start(bf16[2,5,8,32,128]{4,3,2,1,0:T(8,128)(2,1)} %param.10) | copy-start | bytes 1966084
  188.6 5.4 %collective-permute-start.21 = (bf16[2,5,2,32,128]{4,3,2,1,0:T(8,128)(2,1)S(1)}, bf16[2,5,2,32,128]{4,3,2,1,0:T(8,128)(2,1)S(1)}, u32[]{:S(2)}, u32[]{:S(2)}) collective-permute-start(bf16[2,5,2,32,128]{4,3,2,1,0:T(8,128)(2,1)S(1)} %slice_bitcast_fusion.4), channel_id=1, source_target_pairs={{0,2},{1,3},{2,0},{3,1},{4,6},{5,7},{6,4},{7,5},{8,10},{9,11},{10,... | collective-permute-start | bytes 491528 | tf_op jit(solution)/shard_map/ppermute | solution.py:302
  190.2 5.4 %collective-permute-start.19 = (bf16[2,5,2,32,128]{4,3,2,1,0:T(8,128)(2,1)S(1)}, bf16[2,5,2,32,128]{4,3,2,1,0:T(8,128)(2,1)S(1)}, u32[]{:S(2)}, u32[]{:S(2)}) collective-permute-start(bf16[2,5,2,32,128]{4,3,2,1,0:T(8,128)(2,1)S(1)} %slice_bitcast_fusion.6), channel_id=1, source_target_pairs={{0,4},{4,0},{8,12},{12,8},{1,5},{5,1},{9,13},{13,9},{2,6},{6,2},{1... | collective-permute-start | bytes 491528 | tf_op jit(solution)/shard_map/ppermute | solution.py:302
  195.7 8.4 %collective-permute-start.22 = (bf16[2,5,2,32,128]{4,3,2,1,0:T(8,128)(2,1)S(1)}, bf16[2,5,2,32,128]{4,3,2,1,0:T(8,128)(2,1)S(1)}, u32[]{:S(2)}, u32[]{:S(2)}) collective-permute-start(bf16[2,5,2,32,128]{4,3,2,1,0:T(8,128)(2,1)S(1)} %pad_maximum_fusion.2), channel_id=1, source_target_pairs={{0,8},{4,12},{8,0},{12,4},{1,9},{5,13},{9,1},{13,5},{2,10},{6,14},... | collective-permute-start | bytes 491528 | tf_op jit(solution)/shard_map/ppermute | solution.py:302
  (2 other events, 3.1 us)
